TPU v7x, 32 devices: a whole 2x2x4 slice. The times are simulated.
32 devices in a mesh: virt: 8 (over y, x, core), pair: 4 (over z).
Axes of the slice: x: 2, y: 2, z: 4, core: 2. Of those that a mesh axis runs over, the one named last changes fastest.
Arguments:
- lambda_amps: bfloat16 [160, 896, 896], P('pair', 'virt'), may hold values from -0.0234375 to 0.0234375
- t2_amps: bfloat16 [160, 896, 896], P('pair', 'virt'), may hold values from -6 to 6
- chol_ov: bfloat16 [4096, 4, 896], P('pair', None, 'virt'), may hold values from -0.1875 to 0.1875
Outputs:
- density: bfloat16 [4096, 4, 896], P('pair', None, 'virt')
All inputs are finite; a program needn't handle non-finite values.
Results may differ from a plain program's by a relative error of at most 0.0049.
Values may be sent and summed in bfloat16 or wider, within the bound.
No kernel may reach another device: no remote copies, remote signals or barrier semaphores. Data moves between devices by JAX's collectives and lax.ppermute only.
A program may use at most 64 MiB of HBM per device.

v0:
```python
import jax
import jax.numpy as jnp
from jax import lax
from jax.sharding import PartitionSpec as P


def pair_product(left, right):
    return lax.dot_general(
        left, right, (((0, 1), (0, 1)), ((), ())), preferred_element_type=jnp.float32
    )


def shards(lambda_amps, t2_amps, chol_ov):
    own_rows = chol_ov.shape[2]
    partial_value = pair_product(lambda_amps, t2_amps)
    summed = lax.psum(partial_value, "pair")
    vv_rows = lax.psum_scatter(summed, "virt", scatter_dimension=0, tiled=True)
    vv_low = vv_rows.astype(jnp.bfloat16)
    vec_count = chol_ov.shape[0]
    occ_count = chol_ov.shape[1]
    piece = lax.all_gather(chol_ov, "virt", axis=2, tiled=True)
    width = piece.shape[2]
    flat = piece.reshape(vec_count * occ_count, width)
    result = lax.dot_general(
        flat, vv_low, (((1,), (1,)), ((), ())), preferred_element_type=jnp.float32
    )
    return result.reshape(vec_count, occ_count, own_rows).astype(jnp.bfloat16)


def solution(mesh):
    placed = (P("pair", "virt", None), P("pair", "virt", None), P("pair", None, "virt"))
    return jax.shard_map(
        shards, mesh=mesh, in_specs=placed, out_specs=P("pair", None, "virt"), check_vma=False
    )
```

profile of v0, /device:TPU:0, one launch (start us, length us, event | category | flops | bytes accessed | tf_op | source)
XLA Modules:
  0.0 161.1 jit_solution(549603812823770135)
XLA Ops:
  6.5 0.0 reduce-scatter.2.cloned.1.call-start
  6.5 14.1 %convolution_bitcast_fusion = f32[896,896]{1,0:T(8,128)} fusion(bf16[40,112,896]{2,1,0:T(8,128)(2,1)} %param.3, bf16[40,112,896]{2,1,0:T(8,128)(2,1)} %param.4), kind=kOutput, calls=%fused_computation.2 | convolution fusion | flops 7193231360 | bytes 19267584 | tf_op jit(solution)/shard_map/dot_general | solution.py:8
  20.6 0.0 reduce-scatter.2.cloned.1.call-update
  20.6 0.0 all-gather.2.cloned.1.call-start
  20.7 0.7 all-gather.2.cloned.1.call-update
  21.4 48.7 %reduce-scatter.2.cloned.1.call-done = f32[112,896]{1,0:T(8,128)} async-done(((f32[896,896]{1,0:T(8,128)}), f32[112,896]{1,0:T(8,128)}) %reduce-scatter.2.cloned.1.call-update) | async-done | bytes 401424 | tf_op jit(solution)/shard_map/reduce_scatter | solution.py:17
  70.1 27.6 %all-reduce.1 = bf16[112,896]{1,0:T(8,128)(2,1)S(1)} all-reduce(f32[112,896]{1,0:T(8,128)} %reduce-scatter.2.cloned.1.call-done), channel_id=1, replica_groups=mesh['virt'=8,'pair'=4] {'pair'}, use_global_device_ids=true, to_apply=%region_0.0 | all-reduce | flops 100352 | bytes 602112 | tf_op jit(solution)/shard_map/psum | solution.py:16
  97.6 24.5 %all-gather.2.cloned.1.call-done = bf16[1024,4,896]{0,2,1:T(8,128)(2,1)} async-done(((bf16[1024,4,112]{0,2,1:T(8,128)(2,1)}), bf16[1024,4,896]{0,2,1:T(8,128)(2,1)}) %all-gather.2.cloned.1.call-update) | async-done | bytes 7340048 | tf_op jit(solution)/shard_map/all_gather | solution.py:21
  122.1 12.3 %copy.5 = bf16[1024,4,896]{2,1,0:T(4,128)(2,1)} copy(bf16[1024,4,896]{0,2,1:T(8,128)(2,1)} %all-gather.2.cloned.1.call-done) | data formatting | bytes 14680064 | tf_op jit(solution)/shard_map/all_gather | solution.py:21
  134.5 12.3 %reshape.5 = bf16[4096,896]{1,0:T(8,128)(2,1)} reshape(bf16[1024,4,896]{2,1,0:T(4,128)(2,1)} %copy.5) | data formatting | bytes 14680064 | tf_op jit(solution)/shard_map/reshape | solution.py:23
  146.8 5.4 %fusion = bf16[4096,112]{0,1:T(8,128)(2,1)S(1)} fusion(bf16[4096,896]{1,0:T(8,128)(2,1)} %reshape.5, bf16[112,896]{1,0:T(8,128)(2,1)S(1)} %all-reduce.1), kind=kOutput, calls=%fused_computation.1 | convolution fusion | flops 822542336 | bytes 8458240 | tf_op jit(solution)/shard_map/dot_general | solution.py:24
  152.2 0.7 copy.6
  152.9 1.4 copy.7
Async XLA Ops:
  6.5 63.5 %reduce-scatter.2.cloned.1.call-start = ((), (), s32[]{:S(2)}) async-start(), calls=%async_computation.2 | async-start | bytes 3612672 | tf_op jit(solution)/shard_map/reduce_scatter | solution.py:17
  20.6 101.5 %all-gather.2.cloned.1.call-start = ((), (), s32[]{:S(2)}) async-start(), calls=%async_computation.1 | async-start | bytes 8257536 | tf_op jit(solution)/shard_map/all_gather | solution.py:21
Sparse Core Ops, SparseCore 0:
  20.8 49.2 reduce-scatter.1
  72.1 49.9 all-gather.1
where the time goes:
time: 162 us; the launch traced here: 161 us
  waiting for transfers between devices  73.9 us (46%)
  blocking collectives  27.6 us (17%)
  local copies, waits for them, and re-layouts  26.7 us (16%)
  matrix products  19.5 us (12%)
  between operations  13.4 us (8%)
    reduce_scatter x1, waiting for transfers between devices, shards(): vv_rows = lax.psum_scatter(summed, 'virt', scatter_dimension=0, tiled=True)  48.7 us
    psum x1, blocking collectives, shards(): summed = lax.psum(partial_value, 'pair')  27.6 us
    all_gather x1, waiting for transfers between devices, shards(): piece = lax.all_gather(chol_ov, 'virt', axis=2, tiled=True)  24.5 us
    dot_general x1, matrix products, pair_product(): lax.dot_general(left, right, (((0, 1), (0, 1)), ((), ())), preferred_elem...  14.1 us
    all_gather x1, local copies, waits for them, and re-layouts, shards(): piece = lax.all_gather(chol_ov, 'virt', axis=2, tiled=True)  12.3 us
    reshape x1, local copies, waits for them, and re-layouts, shards(): flat = piece.reshape(vec_count * occ_count, width)  12.3 us
    dot_general x1, matrix products, shards(): lax.dot_general(flat, vv_low, (((1,), (1,)), ((), ())), preferred_element...  5.41 us
  transfers between devices with their start and end apart: 2, of which 2 were waited for; matrix products, arithmetic and copies ran while one was open for 0% of the time, Pallas kernels for 0%

commit v1 on v0

v1 whole, which is shorter than its diff:
```python
import functools

import jax
import jax.numpy as jnp
from jax import lax
from jax.experimental import pallas as pl
from jax.experimental.pallas import tpu as pltpu
from jax.sharding import PartitionSpec as P

VMEM_LIMIT = 56 * 2**20


def swap(array, axis, size, offset):
    return lax.ppermute(array, axis, [(i, i ^ offset) for i in range(size)])


def depth_chunks(depth):
    step = 1280
    first = 512
    if depth <= first + step:
        return [(0, depth)]
    cuts = [0] + list(range(first, depth, step)) + [depth]
    return [(a, b - a) for a, b in zip(cuts, cuts[1:])]


def pair_kernel(chunks, rows, left_hbm, right_hbm, keep_ref, send_ref, left, right, total, sems):
    core = lax.axis_index("virt") % 2
    copies = []
    for n, (start, size) in enumerate(chunks):
        span = pl.ds(start, size)
        pair = (
            pltpu.make_async_copy(left_hbm.at[span], left.at[span], sems.at[0, n]),
            pltpu.make_async_copy(right_hbm.at[span], right.at[span], sems.at[1, n]),
        )
        for copy in pair:
            copy.start()
        copies.append(pair)
    for n, (start, size) in enumerate(chunks):
        for copy in copies[n]:
            copy.wait()
        span = pl.ds(start, size)
        term = lax.dot_general(
            left[span], right[span], (((0,), (0,)), ((), ())), preferred_element_type=jnp.float32
        )
        if n == 0:
            total[...] = term
        else:
            total[...] += term
    for mine in range(2):

        @pl.when(core == mine)
        def _():
            for chip in range(keep_ref.shape[0]):
                keep_ref[chip] = total[pl.ds((2 * chip + mine) * rows, rows)]
                send_ref[chip] = total[pl.ds((2 * chip + 1 - mine) * rows, rows)].astype(
                    send_ref.dtype
                )


def pair_product(left, right, rows):
    depth, full = left.shape
    width = right.shape[1]
    chips = full // rows // 2
    chunks = depth_chunks(depth)
    return pl.pallas_call(
        functools.partial(pair_kernel, chunks, rows),
        out_shape=(
            jax.ShapeDtypeStruct((chips, rows, width), jnp.float32),
            jax.ShapeDtypeStruct((chips, rows, width), jnp.bfloat16),
        ),
        in_specs=[pl.BlockSpec(memory_space=pl.ANY)] * 2,
        out_specs=(pl.BlockSpec(memory_space=pltpu.VMEM),) * 2,
        scratch_shapes=[
            pltpu.VMEM((depth, full), left.dtype),
            pltpu.VMEM((depth, width), right.dtype),
            pltpu.VMEM((full, width), jnp.float32),
            pltpu.SemaphoreType.DMA((2, len(chunks))),
        ],
        compiler_params=pltpu.CompilerParams(vmem_limit_bytes=VMEM_LIMIT),
        cost_estimate=pl.CostEstimate(
            flops=2 * depth * full * width,
            bytes_accessed=2 * depth * (full + width) + 6 * full * width // 2,
            transcendentals=0,
        ),
    )(left, right)


def density_kernel(count, rows, vv_ref, *refs):
    blocks, out_ref, low = refs[:count], refs[count], refs[count + 1]
    me = lax.axis_index("virt")

    @pl.when(pl.program_id(0) == 0)
    def _():
        turned = vv_ref[...].T
        for k in range(count):
            for v in range(count):

                @pl.when((me ^ k) == v)
                def _():
                    low[pl.ds(k * rows, rows)] = turned[v * rows : (v + 1) * rows].astype(low.dtype)

    flat = jnp.concatenate([block[0] for block in blocks], axis=0)
    out_ref[0] = lax.dot_general(
        low[...], flat, (((0,), (0,)), ((), ())), preferred_element_type=jnp.float32
    ).astype(out_ref.dtype)


def density_product(vv, blocks):
    rows, full = vv.shape
    occ, _, vectors = blocks[0].shape
    count = len(blocks)
    block = pl.BlockSpec((1, rows, vectors), lambda i: (i, 0, 0))
    return pl.pallas_call(
        functools.partial(density_kernel, count, rows),
        grid=(occ,),
        out_shape=jax.ShapeDtypeStruct((occ, rows, vectors), jnp.bfloat16),
        in_specs=[pl.BlockSpec((rows, full), lambda i: (0, 0))] + [block] * count,
        out_specs=block,
        scratch_shapes=[pltpu.VMEM((full, rows), jnp.bfloat16)],
        compiler_params=pltpu.CompilerParams(vmem_limit_bytes=VMEM_LIMIT),
        cost_estimate=pl.CostEstimate(
            flops=2 * occ * rows * full * vectors,
            bytes_accessed=2 * occ * vectors * (full + rows),
            transcendentals=0,
        ),
    )(vv, *blocks)


def gather_blocks(own, count):
    bits = [1 << b for b in range(1, count.bit_length() - 1)]
    pieces = jnp.split(own, len(bits), axis=0) if len(bits) > 1 else [own]
    held = [{0: piece} for piece in pieces]
    for step in range(len(bits)):
        for n, piece in enumerate(held):
            bit = bits[(n + step) % len(bits)]
            for k in list(piece):
                piece[k ^ bit] = swap(piece[k], "virt", count, bit)
    for piece in held:
        for k in list(piece):
            piece[k ^ 1] = swap(piece[k], "virt", count, 1)
    return [jnp.concatenate([piece[k] for piece in held], axis=0) for k in range(count)]


def shards(count, groups, lambda_amps, t2_amps, chol_ov):
    vectors, occ, rows = chol_ov.shape
    full = lambda_amps.shape[2]
    own = jnp.transpose(chol_ov, (1, 2, 0))
    blocks = gather_blocks(own, count)
    left = lambda_amps.reshape(-1, full)
    right = t2_amps.reshape(-1, full)
    keep, send = pair_product(left, right, rows)
    summed = keep + swap(send, "virt", count, 1)
    chip = lax.axis_index("virt") // 2
    vv = lax.dynamic_index_in_dim(summed, chip, keepdims=False)
    for k in range(1, count // 2):
        part = lax.dynamic_index_in_dim(summed, chip ^ k, keepdims=False)
        vv = vv + swap(part.astype(jnp.bfloat16), "virt", count, 2 * k)
    step = 1
    while step < groups:
        vv = vv + swap(vv.astype(jnp.bfloat16), "pair", groups, step)
        step *= 2
    if rows % 16 == 0:
        density = density_product(vv, blocks)
    else:
        me = lax.axis_index("virt")
        low = vv.astype(jnp.bfloat16).reshape(rows, count, rows)
        density = sum(
            jnp.einsum(
                "ab,ibq->iaq",
                lax.dynamic_index_in_dim(low, me ^ k, axis=1, keepdims=False),
                blocks[k],
                preferred_element_type=jnp.float32,
            )
            for k in range(count)
        ).astype(jnp.bfloat16)
    return jnp.transpose(density, (2, 0, 1))


def solution(mesh):
    placed = (P("pair", "virt", None), P("pair", "virt", None), P("pair", None, "virt"))
    step = functools.partial(shards, mesh.shape["virt"], mesh.shape["pair"])
    return jax.shard_map(
        step, mesh=mesh, in_specs=placed, out_specs=P("pair", None, "virt"), check_vma=False
    )
```

time: 162 us -> 86.2 us (0.53)
  waiting for transfers between devices: 73.9 us -> 38.3 us
  blocking collectives: 27.6 us -> 0 us
  local copies, waits for them, and re-layouts: 26.7 us -> 1.11 us
  matrix products: 19.5 us -> 0 us
  Pallas kernels: 0 us -> 19.4 us
  starting transfers between devices: 0.04 us -> 17.8 us
  between operations: 13.4 us -> 0.07 us
  other arithmetic: 0 us -> 9.44 us
    reduce_scatter x1 -> x0, waiting for transfers between devices: 48.7 us -> none  [shards(): vv_rows = lax.psum_scatter(summed, 'virt', scatter_dimension=0, tiled=True)]
    ppermute x0 -> x20, waiting for transfers between devices: none -> 38.3 us  [swap(): return lax.ppermute(array, axis, [(i, i ^ offset) for i in range(size)])]
    psum x1 -> x0, blocking collectives: 27.6 us -> none  [shards(): summed = lax.psum(partial_value, 'pair')]
    all_gather x1 -> x0, waiting for transfers between devices: 24.5 us -> none  [shards(): piece = lax.all_gather(chol_ov, 'virt', axis=2, tiled=True)]
    dot_general x2 -> x0, matrix products: 19.5 us -> none  [the longest x1 14.1 us: pair_product(): lax.dot_general(left, right, (((0, 1), (0, 1)), ((), ())), preferred_elem...]
    pallas_call x0 -> x2, Pallas kernels: none -> 19.4 us  [the longest x1 13 us: pair_product(): pl.pallas_call(functools.partial(pair_kernel, chunks, rows), out_shape=(j...]
    ppermute x0 -> x20, starting transfers between devices: none -> 17.8 us  [swap(): return lax.ppermute(array, axis, [(i, i ^ offset) for i in range(size)])]
    all_gather x1 -> x0, local copies, waits for them, and re-layouts: 12.3 us -> none  [shards(): piece = lax.all_gather(chol_ov, 'virt', axis=2, tiled=True)]
  transfers between devices with their start and end apart: 2 -> 20, of which waited for: 2 -> 6; matrix products, arithmetic and copies ran while one was open for 0% -> 11% of each run, Pallas kernels for 0% -> 0%
where the time goes in v1:
time: 86.2 us; the launch traced here: 86.1 us
  waiting for transfers between devices  38.3 us (44%)
  Pallas kernels  19.4 us (23%)
  starting transfers between devices  17.8 us (21%)
  other arithmetic  9.44 us (11%)
  local copies, waits for them, and re-layouts  1.11 us (1%)
    ppermute x20, waiting for transfers between devices, swap(): return lax.ppermute(array, axis, [(i, i ^ offset) for i in range(size)])  38.3 us
    ppermute x20, starting transfers between devices, swap(): return lax.ppermute(array, axis, [(i, i ^ offset) for i in range(size)])  17.8 us
    pallas_call x1, Pallas kernels, pair_product(): pl.pallas_call(functools.partial(pair_kernel, chunks, rows), out_shape=(j...  13 us
    concatenate x7, other arithmetic, gather_blocks(): jnp.concatenate([piece[k] for piece in held], axis=0)  8.33 us
    pallas_call x1, Pallas kernels, density_product(): pl.pallas_call(functools.partial(density_kernel, count, rows), grid=(occ,...  6.43 us
  transfers between devices with their start and end apart: 20, of which 6 were waited for; matrix products, arithmetic and copies ran while one was open for 11% of the time, Pallas kernels for 0%

profile of v1, /device:TPU:0, one launch (start us, length us, event | category | flops | bytes accessed | tf_op | source)
XLA Modules:
  0.0 86.1 jit_solution(15522783875517077286)
XLA Ops:
  0.0 0.0 copy-start
  0.0 13.0 %shard_map.37 = (f32[4,112,896]{2,1,0:T(8,128)}, bf16[4,112,896]{2,1,0:T(8,128)(2,1)}) custom-call(bf16[4480,896]{1,0:T(8,128)(2,1)} %bitcast.19, bf16[4480,896]{1,0:T(8,128)(2,1)} %bitcast.20), custom_call_target="tpu_custom_call" | custom-call | flops 7193231360 | bytes 18464768 | tf_op jit(solution)/shard_map/pallas_call | solution.py:65
  13.0 0.0 copy-start.1
  13.0 0.5 collective-permute-start
  13.5 0.0 copy-done
  13.5 1.0 %fusion.8 = (bf16[2,112,1024]{2,1,0:T(8,128)(2,1)}, bf16[2,112,1024]{2,1,0:T(8,128)(2,1)}) fusion(bf16[4,112,1024]{2,1,0:T(8,128)(2,1)S(1)} %bitcast.18), kind=kLoop, calls=%fused_computation.21 | loop fusion | bytes 1835008 | tf_op jit(solution)/shard_map/split | solution.py:131
  14.6 2.5 %collective-permute-start.8 = (bf16[2,112,1024]{2,1,0:T(8,128)(2,1)}, bf16[2,112,1024]{2,1,0:T(8,128)(2,1)}, u32[]{:S(2)}, u32[]{:S(2)}) collective-permute-start(bf16[2,112,1024]{2,1,0:T(8,128)(2,1)} %get-tuple-element.14), channel_id=1, source_target_pairs={{0,8},{4,12},{8,0},{12,4},{16,24},{20,28},{24,16},{28,20},{1,9},{5... | collective-permute-start | bytes 1376264 | tf_op jit(solution)/shard_map/ppermute | solution.py:14
  17.0 1.5 %collective-permute-start.13 = (bf16[2,112,1024]{2,1,0:T(8,128)(2,1)}, bf16[2,112,1024]{2,1,0:T(8,128)(2,1)S(1)}, u32[]{:S(2)}, u32[]{:S(2)}) collective-permute-start(bf16[2,112,1024]{2,1,0:T(8,128)(2,1)} %get-tuple-element.15), channel_id=1, source_target_pairs={{0,16},{4,20},{8,24},{12,28},{16,0},{20,4},{24,8},{28,12},{1,17},{... | collective-permute-start | bytes 1376264 | tf_op jit(solution)/shard_map/ppermute | solution.py:14
  18.6 0.5 collective-permute-start.9
  19.1 0.0 collective-permute-start.12
  19.1 9.6 %collective-permute-done.8 = bf16[2,112,1024]{2,1,0:T(8,128)(2,1)} collective-permute-done((bf16[2,112,1024]{2,1,0:T(8,128)(2,1)}, bf16[2,112,1024]{2,1,0:T(8,128)(2,1)}, u32[]{:S(2)}, u32[]{:S(2)}) %collective-permute-start.8) | collective-permute-done | bytes 458784 | tf_op jit(solution)/shard_map/ppermute | solution.py:14
  28.7 0.0 collective-permute-start.6
  28.7 0.0 collective-permute-done
  28.7 0.5 collective-permute-start.7
  29.2 0.0 copy-done.1
  29.2 0.1 convert_add_fusion
  29.4 0.1 fusion.3
  29.5 1.1 %collective-permute-done.13 = bf16[2,112,1024]{2,1,0:T(8,128)(2,1)S(1)} collective-permute-done((bf16[2,112,1024]{2,1,0:T(8,128)(2,1)}, bf16[2,112,1024]{2,1,0:T(8,128)(2,1)S(1)}, u32[]{:S(2)}, u32[]{:S(2)}) %collective-permute-start.13) | collective-permute-done | bytes 458784 | tf_op jit(solution)/shard_map/ppermute | solution.py:14
  30.6 0.9 %collective-permute-start.1 = (bf16[112,896]{1,0:T(8,128)(2,1)S(1)}, bf16[112,896]{1,0:T(8,128)(2,1)S(1)}, u32[]{:S(2)}, u32[]{:S(2)}) collective-permute-start(bf16[112,896]{1,0:T(8,128)(2,1)S(1)} %get-tuple-element.11), channel_id=1, source_target_pairs={{0,8},{4,12},{8,0},{12,4},{16,24},{20,28},{24,16},{28,20},{1,9},{5... | collective-permute-start | bytes 602120 | tf_op jit(solution)/shard_map/ppermute | solution.py:14
  31.5 7.1 %collective-permute-done.9 = bf16[2,112,1024]{2,1,0:T(8,128)(2,1)} collective-permute-done((bf16[2,112,1024]{2,1,0:T(8,128)(2,1)}, bf16[2,112,1024]{2,1,0:T(8,128)(2,1)}, u32[]{:S(2)}, u32[]{:S(2)}) %collective-permute-start.9) | collective-permute-done | bytes 458784 | tf_op jit(solution)/shard_map/ppermute | solution.py:14
  38.6 2.0 %collective-permute-start.2 = (bf16[112,896]{1,0:T(8,128)(2,1)S(1)}, bf16[112,896]{1,0:T(8,128)(2,1)S(1)}, u32[]{:S(2)}, u32[]{:S(2)}) collective-permute-start(bf16[112,896]{1,0:T(8,128)(2,1)S(1)} %get-tuple-element.13), channel_id=1, source_target_pairs={{0,16},{4,20},{8,24},{12,28},{16,0},{20,4},{24,8},{28,12},{1,17},{... | collective-permute-start | bytes 602120 | tf_op jit(solution)/shard_map/ppermute | solution.py:14
  40.5 2.2 %pad_maximum_fusion.1.refs_2_ = bf16[4,112,1024]{2,1,0:T(8,128)(2,1)} fusion(bf16[2,112,1024]{2,1,0:T(8,128)(2,1)} %collective-permute-done.9, bf16[2,112,1024]{2,1,0:T(8,128)(2,1)} %collective-permute-done.8), kind=kLoop, calls=%fused_computation.2 | loop fusion | flops 458752 | bytes 1835008 | tf_op jit(solution)/shard_map/concatenate | solution.py:141
  42.7 0.0 collective-permute-done.12
  42.7 0.0 collective-permute-start.16
  42.8 0.0 collective-permute-done.6
  42.8 1.9 %collective-permute-start.17 = (bf16[2,112,1024]{2,1,0:T(8,128)(2,1)S(1)}, bf16[2,112,1024]{2,1,0:T(8,128)(2,1)S(1)}, u32[]{:S(2)}, u32[]{:S(2)}) collective-permute-start(bf16[2,112,1024]{2,1,0:T(8,128)(2,1)S(1)} %collective-permute-done.13), channel_id=1, source_target_pairs={{0,8},{4,12},{8,0},{12,4},{16,24},{20,28},{24,16},{28,20},{1,9},{5... | collective-permute-start | bytes 1376264 | tf_op jit(solution)/shard_map/ppermute | solution.py:14
  44.7 0.0 collective-permute-done.7
  44.7 1.5 %collective-permute-start.3 = (bf16[112,896]{1,0:T(8,128)(2,1)S(1)}, bf16[112,896]{1,0:T(8,128)(2,1)S(1)}, u32[]{:S(2)}, u32[]{:S(2)}) collective-permute-start(bf16[112,896]{1,0:T(8,128)(2,1)S(1)} %get-tuple-element.12), channel_id=1, source_target_pairs={{0,24},{4,28},{8,16},{12,20},{16,8},{20,12},{24,0},{28,4},{1,25},{... | collective-permute-start | bytes 602120 | tf_op jit(solution)/shard_map/ppermute | solution.py:14
  46.2 1.0 %pad_maximum_fusion.3.refs_4_ = bf16[4,112,1024]{2,1,0:T(8,128)(2,1)} fusion(bf16[2,112,1024]{2,1,0:T(8,128)(2,1)S(1)} %collective-permute-done.13, bf16[2,112,1024]{2,1,0:T(8,128)(2,1)S(1)} %collective-permute-done.12), kind=kLoop, calls=%fused_computation.4 | loop fusion | flops 458752 | bytes 1835008 | tf_op jit(solution)/shard_map/concatenate | solution.py:141
  47.2 0.0 collective-permute-done.1
  47.2 0.0 collective-permute-start.10
  47.2 0.0 collective-permute-done.2
  47.3 0.5 collective-permute-start.11
  47.8 1.0 %pad_maximum_fusion.refs_1_ = bf16[4,112,1024]{2,1,0:T(8,128)(2,1)} fusion(bf16[2,112,1024]{2,1,0:T(8,128)(2,1)S(1)} %collective-permute-done.7, bf16[2,112,1024]{2,1,0:T(8,128)(2,1)S(1)} %collective-permute-done.6), kind=kLoop, calls=%fused_computation.1 | loop fusion | flops 458752 | bytes 1835008 | tf_op jit(solution)/shard_map/concatenate | solution.py:141
  48.8 10.9 %collective-permute-done.3 = bf16[112,896]{1,0:T(8,128)(2,1)S(1)} collective-permute-done((bf16[112,896]{1,0:T(8,128)(2,1)S(1)}, bf16[112,896]{1,0:T(8,128)(2,1)S(1)}, u32[]{:S(2)}, u32[]{:S(2)}) %collective-permute-start.3) | collective-permute-done | bytes 200736 | tf_op jit(solution)/shard_map/ppermute | solution.py:14
  59.7 0.0 collective-permute-start.15
  59.7 0.1 fusion.6
  59.8 0.0 collective-permute-done.16
  59.8 0.6 collective-permute-start.14
  60.4 0.0 collective-permute-done.17
  60.4 1.6 %collective-permute-start.4 = (bf16[112,896]{1,0:T(8,128)(2,1)S(1)}, bf16[112,896]{1,0:T(8,128)(2,1)S(1)}, u32[]{:S(2)}, u32[]{:S(2)}) collective-permute-start(bf16[112,896]{1,0:T(8,128)(2,1)S(1)} %get-tuple-element.9), channel_id=1, source_target_pairs={{0,1},{1,0},{2,3},{3,2},{4,5},{5,4},{6,7},{7,6},{8,9},{9,8},{10,11... | collective-permute-start | bytes 602120 | tf_op jit(solution)/shard_map/ppermute | solution.py:14
  61.9 1.0 %pad_maximum_fusion.5.refs_6_ = bf16[4,112,1024]{2,1,0:T(8,128)(2,1)} fusion(bf16[2,112,1024]{2,1,0:T(8,128)(2,1)S(1)} %collective-permute-done.17, bf16[2,112,1024]{2,1,0:T(8,128)(2,1)S(1)} %collective-permute-done.16), kind=kLoop, calls=%fused_computation.6 | loop fusion | flops 458752 | bytes 1835008 | tf_op jit(solution)/shard_map/concatenate | solution.py:141
  62.9 0.0 collective-permute-done.10
  62.9 0.0 collective-permute-start.18
  62.9 0.0 collective-permute-done.11
  62.9 0.5 collective-permute-start.19
  63.5 1.0 %pad_maximum_fusion.2.refs_3_ = bf16[4,112,1024]{2,1,0:T(8,128)(2,1)} fusion(bf16[2,112,1024]{2,1,0:T(8,128)(2,1)S(1)} %collective-permute-done.11, bf16[2,112,1024]{2,1,0:T(8,128)(2,1)S(1)} %collective-permute-done.10), kind=kLoop, calls=%fused_computation.3 | loop fusion | flops 458752 | bytes 1835008 | tf_op jit(solution)/shard_map/concatenate | solution.py:141
  64.5 2.9 %collective-permute-done.4 = bf16[112,896]{1,0:T(8,128)(2,1)S(1)} collective-permute-done((bf16[112,896]{1,0:T(8,128)(2,1)S(1)}, bf16[112,896]{1,0:T(8,128)(2,1)S(1)}, u32[]{:S(2)}, u32[]{:S(2)}) %collective-permute-start.4) | collective-permute-done | bytes 200736 | tf_op jit(solution)/shard_map/ppermute | solution.py:14
  67.4 2.6 %collective-permute-start.5 = (bf16[112,896]{1,0:T(8,128)(2,1)S(1)}, bf16[112,896]{1,0:T(8,128)(2,1)S(1)}, u32[]{:S(2)}, u32[]{:S(2)}) collective-permute-start(bf16[112,896]{1,0:T(8,128)(2,1)S(1)} %fusion.2), channel_id=1, source_target_pairs={{0,2},{1,3},{2,0},{3,1},{4,6},{5,7},{6,4},{7,5},{8,10},{9,11},{10,... | collective-permute-start | bytes 602120 | tf_op jit(solution)/shard_map/ppermute | solution.py:14
  70.0 0.0 collective-permute-done.15
  70.0 0.0 collective-permute-done.14
  70.0 1.0 %pad_maximum_fusion.4.refs_5_ = bf16[4,112,1024]{2,1,0:T(8,128)(2,1)} fusion(bf16[2,112,1024]{2,1,0:T(8,128)(2,1)S(1)} %collective-permute-done.15, bf16[2,112,1024]{2,1,0:T(8,128)(2,1)S(1)} %collective-permute-done.14), kind=kLoop, calls=%fused_computation.5 | loop fusion | flops 458752 | bytes 1835008 | tf_op jit(solution)/shard_map/concatenate | solution.py:141
  71.1 0.0 collective-permute-done.18
  71.1 0.0 collective-permute-done.19
  71.1 1.0 %pad_maximum_fusion.6.refs_7_ = bf16[4,112,1024]{2,1,0:T(8,128)(2,1)} fusion(bf16[2,112,1024]{2,1,0:T(8,128)(2,1)S(1)} %collective-permute-done.19, bf16[2,112,1024]{2,1,0:T(8,128)(2,1)S(1)} %collective-permute-done.18), kind=kLoop, calls=%fused_computation.7 | loop fusion | flops 458752 | bytes 1835008 | tf_op jit(solution)/shard_map/concatenate | solution.py:141
  72.1 6.7 %collective-permute-done.5 = bf16[112,896]{1,0:T(8,128)(2,1)S(1)} collective-permute-done((bf16[112,896]{1,0:T(8,128)(2,1)S(1)}, bf16[112,896]{1,0:T(8,128)(2,1)S(1)}, u32[]{:S(2)}, u32[]{:S(2)}) %collective-permute-start.5) | collective-permute-done | bytes 200736 | tf_op jit(solution)/shard_map/ppermute | solution.py:14
  78.8 0.8 convert_add_fusion.1.vv_ref
  79.6 6.4 %shard_map.38 = bf16[4,112,1024]{2,1,0:T(8,128)(2,1)} custom-call(f32[112,896]{1,0:T(8,128)} %convert_add_fusion.1.vv_ref, bf16[4,112,1024]{2,1,0:T(8,128)(2,1)} %bitcast.17, bf16[4,112,1024]{2,1,0:T(8,128)(2,1)} %pad_maximum_fusion.refs_1_, bf16[4,112,1024]{2,1,0:T(8,128)(2,1)} %pad_maximum_fusion.1.refs_2_, ...), custom_call_target="tpu_custom_call" | custom-call | flops 822083584 | bytes 8257536 | tf_op jit(solution)/shard_map/pallas_call | solution.py:113
  (1 shorter events, 0.0 us)
Async XLA Ops:
  0.0 13.5 %copy-start = (bf16[1024,4,112]{0,2,1:T(8,128)(2,1)S(1)}, bf16[1024,4,112]{0,2,1:T(8,128)(2,1)}, u32[]{:S(2)}) copy-start(bf16[1024,4,112]{0,2,1:T(8,128)(2,1)} %param.5) | copy-start | bytes 2752516
  13.0 16.2 %copy-start.1 = (f32[4,112,896]{2,1,0:T(8,128)S(1)}, f32[4,112,896]{2,1,0:T(8,128)}, u32[]{:S(2)}) copy-start(f32[4,112,896]{2,1,0:T(8,128)} %get-tuple-element.7) | copy-start | bytes 4816900
  13.0 15.7 %collective-permute-start = (bf16[4,112,896]{2,1,0:T(8,128)(2,1)}, bf16[4,112,896]{2,1,0:T(8,128)(2,1)S(1)}, u32[]{:S(2)}, u32[]{:S(2)}) collective-permute-start(bf16[4,112,896]{2,1,0:T(8,128)(2,1)} %get-tuple-element.8), channel_id=1, source_target_pairs={{0,4},{4,0},{8,12},{12,8},{16,20},{20,16},{24,28},{28,24},{1,5},{5... | collective-permute-start | bytes 2408456 | tf_op jit(solution)/shard_map/ppermute | solution.py:14
  14.6 14.2 %collective-permute-start.8 = (bf16[2,112,1024]{2,1,0:T(8,128)(2,1)}, bf16[2,112,1024]{2,1,0:T(8,128)(2,1)}, u32[]{:S(2)}, u32[]{:S(2)}) collective-permute-start(bf16[2,112,1024]{2,1,0:T(8,128)(2,1)} %get-tuple-element.14), channel_id=1, source_target_pairs={{0,8},{4,12},{8,0},{12,4},{16,24},{20,28},{24,16},{28,20},{1,9},{5... | collective-permute-start | bytes 1376264 | tf_op jit(solution)/shard_map/ppermute | solution.py:14
  17.0 13.6 %collective-permute-start.13 = (bf16[2,112,1024]{2,1,0:T(8,128)(2,1)}, bf16[2,112,1024]{2,1,0:T(8,128)(2,1)S(1)}, u32[]{:S(2)}, u32[]{:S(2)}) collective-permute-start(bf16[2,112,1024]{2,1,0:T(8,128)(2,1)} %get-tuple-element.15), channel_id=1, source_target_pairs={{0,16},{4,20},{8,24},{12,28},{16,0},{20,4},{24,8},{28,12},{1,17},{... | collective-permute-start | bytes 1376264 | tf_op jit(solution)/shard_map/ppermute | solution.py:14
  18.6 20.0 %collective-permute-start.9 = (bf16[2,112,1024]{2,1,0:T(8,128)(2,1)}, bf16[2,112,1024]{2,1,0:T(8,128)(2,1)}, u32[]{:S(2)}, u32[]{:S(2)}) collective-permute-start(bf16[2,112,1024]{2,1,0:T(8,128)(2,1)} %get-tuple-element.15), channel_id=1, source_target_pairs={{0,8},{4,12},{8,0},{12,4},{16,24},{20,28},{24,16},{28,20},{1,9},{5... | collective-permute-start | bytes 1376264 | tf_op jit(solution)/shard_map/ppermute | solution.py:14
  19.1 23.6 %collective-permute-start.12 = (bf16[2,112,1024]{2,1,0:T(8,128)(2,1)}, bf16[2,112,1024]{2,1,0:T(8,128)(2,1)S(1)}, u32[]{:S(2)}, u32[]{:S(2)}) collective-permute-start(bf16[2,112,1024]{2,1,0:T(8,128)(2,1)} %get-tuple-element.14), channel_id=1, source_target_pairs={{0,16},{4,20},{8,24},{12,28},{16,0},{20,4},{24,8},{28,12},{1,17},{... | collective-permute-start | bytes 1376264 | tf_op jit(solution)/shard_map/ppermute | solution.py:14
  28.7 14.0 %collective-permute-start.6 = (bf16[2,112,1024]{2,1,0:T(8,128)(2,1)}, bf16[2,112,1024]{2,1,0:T(8,128)(2,1)S(1)}, u32[]{:S(2)}, u32[]{:S(2)}) collective-permute-start(bf16[2,112,1024]{2,1,0:T(8,128)(2,1)} %get-tuple-element.14), channel_id=1, source_target_pairs={{0,4},{4,0},{8,12},{12,8},{16,20},{20,16},{24,28},{28,24},{1,5},{5... | collective-permute-start | bytes 1376264 | tf_op jit(solution)/shard_map/ppermute | solution.py:14
  28.7 16.0 %collective-permute-start.7 = (bf16[2,112,1024]{2,1,0:T(8,128)(2,1)}, bf16[2,112,1024]{2,1,0:T(8,128)(2,1)S(1)}, u32[]{:S(2)}, u32[]{:S(2)}) collective-permute-start(bf16[2,112,1024]{2,1,0:T(8,128)(2,1)} %get-tuple-element.15), channel_id=1, source_target_pairs={{0,4},{4,0},{8,12},{12,8},{16,20},{20,16},{24,28},{28,24},{1,5},{5... | collective-permute-start | bytes 1376264 | tf_op jit(solution)/shard_map/ppermute | solution.py:14
  30.6 16.6 %collective-permute-start.1 = (bf16[112,896]{1,0:T(8,128)(2,1)S(1)}, bf16[112,896]{1,0:T(8,128)(2,1)S(1)}, u32[]{:S(2)}, u32[]{:S(2)}) collective-permute-start(bf16[112,896]{1,0:T(8,128)(2,1)S(1)} %get-tuple-element.11), channel_id=1, source_target_pairs={{0,8},{4,12},{8,0},{12,4},{16,24},{20,28},{24,16},{28,20},{1,9},{5... | collective-permute-start | bytes 602120 | tf_op jit(solution)/shard_map/ppermute | solution.py:14
  38.6 8.7 %collective-permute-start.2 = (bf16[112,896]{1,0:T(8,128)(2,1)S(1)}, bf16[112,896]{1,0:T(8,128)(2,1)S(1)}, u32[]{:S(2)}, u32[]{:S(2)}) collective-permute-start(bf16[112,896]{1,0:T(8,128)(2,1)S(1)} %get-tuple-element.13), channel_id=1, source_target_pairs={{0,16},{4,20},{8,24},{12,28},{16,0},{20,4},{24,8},{28,12},{1,17},{... | collective-permute-start | bytes 602120 | tf_op jit(solution)/shard_map/ppermute | solution.py:14
  42.7 17.1 %collective-permute-start.16 = (bf16[2,112,1024]{2,1,0:T(8,128)(2,1)}, bf16[2,112,1024]{2,1,0:T(8,128)(2,1)S(1)}, u32[]{:S(2)}, u32[]{:S(2)}) collective-permute-start(bf16[2,112,1024]{2,1,0:T(8,128)(2,1)} %collective-permute-done.8), channel_id=1, source_target_pairs={{0,16},{4,20},{8,24},{12,28},{16,0},{20,4},{24,8},{28,12},{1,17},{... | collective-permute-start | bytes 1376264 | tf_op jit(solution)/shard_map/ppermute | solution.py:14
  42.8 17.6 %collective-permute-start.17 = (bf16[2,112,1024]{2,1,0:T(8,128)(2,1)S(1)}, bf16[2,112,1024]{2,1,0:T(8,128)(2,1)S(1)}, u32[]{:S(2)}, u32[]{:S(2)}) collective-permute-start(bf16[2,112,1024]{2,1,0:T(8,128)(2,1)S(1)} %collective-permute-done.13), channel_id=1, source_target_pairs={{0,8},{4,12},{8,0},{12,4},{16,24},{20,28},{24,16},{28,20},{1,9},{5... | collective-permute-start | bytes 1376264 | tf_op jit(solution)/shard_map/ppermute | solution.py:14
  44.7 14.9 %collective-permute-start.3 = (bf16[112,896]{1,0:T(8,128)(2,1)S(1)}, bf16[112,896]{1,0:T(8,128)(2,1)S(1)}, u32[]{:S(2)}, u32[]{:S(2)}) collective-permute-start(bf16[112,896]{1,0:T(8,128)(2,1)S(1)} %get-tuple-element.12), channel_id=1, source_target_pairs={{0,24},{4,28},{8,16},{12,20},{16,8},{20,12},{24,0},{28,4},{1,25},{... | collective-permute-start | bytes 602120 | tf_op jit(solution)/shard_map/ppermute | solution.py:14
  47.2 15.7 %collective-permute-start.10 = (bf16[2,112,1024]{2,1,0:T(8,128)(2,1)}, bf16[2,112,1024]{2,1,0:T(8,128)(2,1)S(1)}, u32[]{:S(2)}, u32[]{:S(2)}) collective-permute-start(bf16[2,112,1024]{2,1,0:T(8,128)(2,1)} %collective-permute-done.8), channel_id=1, source_target_pairs={{0,4},{4,0},{8,12},{12,8},{16,20},{20,16},{24,28},{28,24},{1,5},{5... | collective-permute-start | bytes 1376264 | tf_op jit(solution)/shard_map/ppermute | solution.py:14
  47.3 15.7 %collective-permute-start.11 = (bf16[2,112,1024]{2,1,0:T(8,128)(2,1)}, bf16[2,112,1024]{2,1,0:T(8,128)(2,1)S(1)}, u32[]{:S(2)}, u32[]{:S(2)}) collective-permute-start(bf16[2,112,1024]{2,1,0:T(8,128)(2,1)} %collective-permute-done.9), channel_id=1, source_target_pairs={{0,4},{4,0},{8,12},{12,8},{16,20},{20,16},{24,28},{28,24},{1,5},{5... | collective-permute-start | bytes 1376264 | tf_op jit(solution)/shard_map/ppermute | solution.py:14
  59.7 10.4 %collective-permute-start.15 = (bf16[2,112,1024]{2,1,0:T(8,128)(2,1)S(1)}, bf16[2,112,1024]{2,1,0:T(8,128)(2,1)S(1)}, u32[]{:S(2)}, u32[]{:S(2)}) collective-permute-start(bf16[2,112,1024]{2,1,0:T(8,128)(2,1)S(1)} %collective-permute-done.13), channel_id=1, source_target_pairs={{0,4},{4,0},{8,12},{12,8},{16,20},{20,16},{24,28},{28,24},{1,5},{5... | collective-permute-start | bytes 1376264 | tf_op jit(solution)/shard_map/ppermute | solution.py:14
  59.8 10.3 %collective-permute-start.14 = (bf16[2,112,1024]{2,1,0:T(8,128)(2,1)S(1)}, bf16[2,112,1024]{2,1,0:T(8,128)(2,1)S(1)}, u32[]{:S(2)}, u32[]{:S(2)}) collective-permute-start(bf16[2,112,1024]{2,1,0:T(8,128)(2,1)S(1)} %collective-permute-done.12), channel_id=1, source_target_pairs={{0,4},{4,0},{8,12},{12,8},{16,20},{20,16},{24,28},{28,24},{1,5},{5... | collective-permute-start | bytes 1376264 | tf_op jit(solution)/shard_map/ppermute | solution.py:14
  60.4 7.0 %collective-permute-start.4 = (bf16[112,896]{1,0:T(8,128)(2,1)S(1)}, bf16[112,896]{1,0:T(8,128)(2,1)S(1)}, u32[]{:S(2)}, u32[]{:S(2)}) collective-permute-start(bf16[112,896]{1,0:T(8,128)(2,1)S(1)} %get-tuple-element.9), channel_id=1, source_target_pairs={{0,1},{1,0},{2,3},{3,2},{4,5},{5,4},{6,7},{7,6},{8,9},{9,8},{10,11... | collective-permute-start | bytes 602120 | tf_op jit(solution)/shard_map/ppermute | solution.py:14
  62.9 8.1 %collective-permute-start.18 = (bf16[2,112,1024]{2,1,0:T(8,128)(2,1)S(1)}, bf16[2,112,1024]{2,1,0:T(8,128)(2,1)S(1)}, u32[]{:S(2)}, u32[]{:S(2)}) collective-permute-start(bf16[2,112,1024]{2,1,0:T(8,128)(2,1)S(1)} %collective-permute-done.16), channel_id=1, source_target_pairs={{0,4},{4,0},{8,12},{12,8},{16,20},{20,16},{24,28},{28,24},{1,5},{5... | collective-permute-start | bytes 1376264 | tf_op jit(solution)/shard_map/ppermute | solution.py:14
  62.9 8.1 %collective-permute-start.19 = (bf16[2,112,1024]{2,1,0:T(8,128)(2,1)S(1)}, bf16[2,112,1024]{2,1,0:T(8,128)(2,1)S(1)}, u32[]{:S(2)}, u32[]{:S(2)}) collective-permute-start(bf16[2,112,1024]{2,1,0:T(8,128)(2,1)S(1)} %collective-permute-done.17), channel_id=1, source_target_pairs={{0,4},{4,0},{8,12},{12,8},{16,20},{20,16},{24,28},{28,24},{1,5},{5... | collective-permute-start | bytes 1376264 | tf_op jit(solution)/shard_map/ppermute | solution.py:14
  67.4 11.4 %collective-permute-start.5 = (bf16[112,896]{1,0:T(8,128)(2,1)S(1)}, bf16[112,896]{1,0:T(8,128)(2,1)S(1)}, u32[]{:S(2)}, u32[]{:S(2)}) collective-permute-start(bf16[112,896]{1,0:T(8,128)(2,1)S(1)} %fusion.2), channel_id=1, source_target_pairs={{0,2},{1,3},{2,0},{3,1},{4,6},{5,7},{6,4},{7,5},{8,10},{9,11},{10,... | collective-permute-start | bytes 602120 | tf_op jit(solution)/shard_map/ppermute | solution.py:14

commit v2 on v1

v2 whole, which is shorter than its diff:
```python
import functools

import jax
import jax.numpy as jnp
from jax import lax
from jax.experimental import pallas as pl
from jax.experimental.pallas import tpu as pltpu
from jax.sharding import PartitionSpec as P

EARLY = 3
PAIR_VMEM = 40 * 2**20


def swap(array, axis, size, offset):
    return lax.ppermute(array, axis, [(i, i ^ offset) for i in range(size)])


def depth_chunks(depth):
    step = 1408
    first = 256
    if depth <= first + step:
        return [(0, depth)]
    cuts = [0] + list(range(first, depth, step)) + [depth]
    return [(a, b - a) for a, b in zip(cuts, cuts[1:])]


def pair_kernel(chunks, rows, left_hbm, right_hbm, *refs):
    *outs, left, right, total, sems = refs
    me = lax.axis_index("virt")
    count = len(outs)
    copies = []
    for n, (start, size) in enumerate(chunks):
        span = pl.ds(start, size)
        pair = (
            pltpu.make_async_copy(left_hbm.at[span], left.at[span], sems.at[0, n]),
            pltpu.make_async_copy(right_hbm.at[span], right.at[span], sems.at[1, n]),
        )
        for copy in pair:
            copy.start()
        copies.append(pair)
    for n, (start, size) in enumerate(chunks):
        for copy in copies[n]:
            copy.wait()
        span = pl.ds(start, size)
        term = lax.dot_general(
            left[span], right[span], (((0,), (0,)), ((), ())), preferred_element_type=jnp.float32
        )
        if n == 0:
            total[...] = term
        else:
            total[...] += term
    for mine in range(count):

        @pl.when(me == mine)
        def _():
            for k, out in enumerate(outs):
                block = total[pl.ds((mine ^ k) * rows, rows)]
                out[...] = block.astype(out.dtype)


def pair_product(left, right, rows):
    depth, full = left.shape
    width = right.shape[1]
    count = full // rows
    chunks = depth_chunks(depth)
    kinds = [jnp.bfloat16 if k % 2 else jnp.float32 for k in range(count)]
    return pl.pallas_call(
        functools.partial(pair_kernel, chunks, rows),
        out_shape=[pltpu.VMEM((rows, width), kind) for kind in kinds],
        in_specs=[pl.BlockSpec(memory_space=pltpu.HBM)] * 2,
        out_specs=[pl.BlockSpec(memory_space=pltpu.VMEM)] * count,
        scratch_shapes=[
            pltpu.VMEM((depth, full), left.dtype),
            pltpu.VMEM((depth, width), right.dtype),
            pltpu.VMEM((full, width), jnp.float32),
            pltpu.SemaphoreType.DMA((2, len(chunks))),
        ],
        compiler_params=pltpu.CompilerParams(vmem_limit_bytes=PAIR_VMEM),
        cost_estimate=pl.CostEstimate(
            flops=2 * depth * full * width,
            bytes_accessed=2 * depth * (full + width) + 3 * full * width,
            transcendentals=0,
        ),
    )(*[pltpu.with_memory_space_constraint(side, pltpu.HBM) for side in (left, right)])


def fold_kernel(count, *refs):
    half = count // 2
    terms, arrived, outs = refs[:half], refs[half:count], refs[len(refs) - half :]
    for term, other, out in zip(terms, arrived, outs):
        out[...] = (term[...] + other[...].astype(jnp.float32)).astype(out.dtype)


def fold(terms, arrived, after):
    count = 2 * len(terms)
    shape = terms[0].shape
    kinds = [jnp.float32] + [jnp.bfloat16] * (len(terms) - 1)
    return pl.pallas_call(
        functools.partial(fold_kernel, count),
        out_shape=[pltpu.VMEM(shape, kind) for kind in kinds],
        in_specs=[pl.BlockSpec(memory_space=pltpu.VMEM)] * count
        + [pl.BlockSpec(memory_space=pl.ANY)] * len(after),
        out_specs=[pl.BlockSpec(memory_space=pltpu.VMEM)] * len(terms),
        compiler_params=pltpu.CompilerParams(vmem_limit_bytes=8 * 2**20),
        cost_estimate=pl.CostEstimate(flops=0, bytes_accessed=0, transcendentals=0),
    )(*terms, *arrived, *after)


def pass_kernel(*refs):
    pass


def hold(arrays, after):
    return pl.pallas_call(
        pass_kernel,
        out_shape=[jax.ShapeDtypeStruct(array.shape, array.dtype) for array in arrays],
        in_specs=[pl.BlockSpec(memory_space=pl.ANY)] * (len(arrays) + len(after)),
        out_specs=[pl.BlockSpec(memory_space=pl.ANY)] * len(arrays),
        input_output_aliases={n: n for n in range(len(arrays))},
        compiler_params=pltpu.CompilerParams(vmem_limit_bytes=2**20),
        cost_estimate=pl.CostEstimate(flops=0, bytes_accessed=0, transcendentals=0),
    )(*arrays, *after)


def density_kernel(count, rows, splits, vv_ref, *refs):
    total = sum(len(s) for s in splits)
    parts, out_ref, low = refs[:total], refs[total], refs[total + 1]
    me = lax.axis_index("virt")
    step = pl.program_id(0)

    @pl.when(step == 0)
    def _():
        turned = vv_ref[...].T
        for k in range(count):
            for v in range(count):

                @pl.when((me ^ k) == v)
                def _():
                    low[pl.ds(k * rows, rows)] = turned[v * rows : (v + 1) * rows].astype(low.dtype)

    flat, at = [], 0
    for split in splits:
        block = parts[at][0]
        for n in range(1, len(split)):
            block = jnp.where(step < split[n], block, parts[at + n][0])
        flat.append(block)
        at += len(split)
    out_ref[0] = lax.dot_general(
        low[...],
        jnp.concatenate(flat, axis=0),
        (((0,), (0,)), ((), ())),
        preferred_element_type=jnp.float32,
    ).astype(out_ref.dtype)


def density_product(vv, blocks):
    rows, full = vv.shape
    count = len(blocks)
    vectors = blocks[0][0].shape[2]
    occ = sum(part.shape[0] for part in blocks[0])
    splits, specs = [], []
    for block in blocks:
        start, split = 0, []
        for part in block:
            size = part.shape[0]
            split.append(start)
            specs.append(
                pl.BlockSpec(
                    (1, rows, vectors),
                    lambda i, start=start, size=size: (jnp.clip(i - start, 0, size - 1), 0, 0),
                )
            )
            start += size
        splits.append(split)
    return pl.pallas_call(
        functools.partial(density_kernel, count, rows, splits),
        grid=(occ,),
        out_shape=jax.ShapeDtypeStruct((occ, rows, vectors), jnp.bfloat16),
        in_specs=[pl.BlockSpec((rows, full), lambda i: (0, 0))] + specs,
        out_specs=pl.BlockSpec((1, rows, vectors), lambda i: (i, 0, 0)),
        scratch_shapes=[pltpu.VMEM((full, rows), jnp.bfloat16)],
        compiler_params=pltpu.CompilerParams(vmem_limit_bytes=24 * 2**20),
        cost_estimate=pl.CostEstimate(flops=0, bytes_accessed=0, transcendentals=0),
    )(vv, *[part for block in blocks for part in block])


def send_early(own, count, early):
    occ = own.shape[0]
    early = min(early, occ)
    bits = [k for k in range(2, count) if k & (k - 1) == 0]
    start = {k: occ - early if k == 2 else 0 for k in bits}
    came = {k: swap(own[start[k] : start[k] + early], "virt", count, k) for k in bits}
    rest = {k: own[: occ - early] if k == 2 else own[early:] for k in bits}
    return came, {k: part for k, part in rest.items() if part.shape[0]}


def gather_rest(own, came, rest, count):
    occ = own.shape[0]
    half = (occ + 1) // 2
    held = {0: [own]}
    for k in sorted(range(2, count, 2), key=lambda k: (bin(k).count("1"), k)):
        low_bit, high_bit = k & -k, 1 << (k.bit_length() - 1)
        if k in came:
            parts = [came[k]] + ([swap(rest[k], "virt", count, k)] if k in rest else [])
            held[k] = parts[::-1] if k == 2 else parts
        else:
            held[k] = [swap(take(held[k ^ high_bit], half, occ), "virt", count, high_bit)]
            if half < occ:
                held[k].insert(0, swap(take(held[k ^ low_bit], 0, half), "virt", count, low_bit))
    return held


def take(parts, start, stop):
    kept, at = [], 0
    for part in parts:
        size = part.shape[0]
        low, high = max(start - at, 0), min(stop - at, size)
        if low < high:
            kept.append(part[low:high])
        at += size
    return kept[0] if len(kept) == 1 else jnp.concatenate(kept, axis=0)


def shards(count, groups, lambda_amps, t2_amps, chol_ov):
    rows = chol_ov.shape[2]
    full = lambda_amps.shape[2]
    own = jnp.transpose(chol_ov, (1, 2, 0))
    came, rest = send_early(own, count, EARLY)
    left = lambda_amps.reshape(-1, full)
    right = t2_amps.reshape(-1, full)
    terms = pair_product(left, right, rows)
    even = range(0, count, 2)
    arrived = [swap(terms[k ^ 1], "virt", count, 1) for k in even]
    sums = fold([terms[k] for k in even], arrived, list(came.values()))
    arrived = [swap(sums[k // 2], "virt", count, k) for k in range(2, count, 2)]
    kept = hold([*came.values(), *rest.values()], arrived)
    came = dict(zip(came, kept))
    rest = dict(zip(rest, kept[len(came) :]))
    held = gather_rest(own, came, rest, count)
    vv = sums[0]
    for part in arrived:
        vv = vv + part
    step = 1
    while step < groups:
        part = swap(vv.astype(jnp.bfloat16), "pair", groups, step)
        vv = vv + part
        step *= 2
    names = [(k, n) for k in held for n in range(len(held[k]))]
    late = [(k, n) for k, n in names if k and not (k in came and held[k][n] is came[k])]
    kept = hold([held[k][n] for k, n in late], [part])
    for (k, n), array in zip(late, kept):
        held[k][n] = array
    for k in list(held):
        held[k ^ 1] = [swap(array, "virt", count, 1) for array in held[k]]
    blocks = [held[k] for k in range(count)]
    if rows % 16 == 0:
        density = density_product(vv, blocks)
    else:
        me = lax.axis_index("virt")
        low = vv.astype(jnp.bfloat16).reshape(rows, count, rows)
        density = sum(
            jnp.einsum(
                "ab,ibq->iaq",
                lax.dynamic_index_in_dim(low, me ^ k, axis=1, keepdims=False),
                jnp.concatenate(blocks[k], axis=0),
                preferred_element_type=jnp.float32,
            )
            for k in range(count)
        ).astype(jnp.bfloat16)
    return jnp.transpose(density, (2, 0, 1))


def solution(mesh):
    placed = (P("pair", "virt", None), P("pair", "virt", None), P("pair", None, "virt"))
    step = functools.partial(shards, mesh.shape["virt"], mesh.shape["pair"])
    return jax.shard_map(
        step, mesh=mesh, in_specs=placed, out_specs=P("pair", None, "virt"), check_vma=False
    )
```

time: 86.2 us -> 58.2 us (0.68)
  waiting for transfers between devices: 38.3 us -> 21.5 us
  other arithmetic: 9.44 us -> 0.2 us
  Pallas kernels: 19.4 us -> 15.7 us
  starting transfers between devices: 17.8 us -> 19.1 us
    ppermute x20 -> x22, waiting for transfers between devices: 38.3 us -> 21.5 us  [swap(): return lax.ppermute(array, axis, [(i, i ^ offset) for i in range(size)])]
    concatenate x7 -> x0, other arithmetic: 8.33 us -> none  [gather_blocks(): jnp.concatenate([piece[k] for piece in held], axis=0)]
    pallas_call x2 -> x5, Pallas kernels: 19.4 us -> 15.7 us  [the longest x1 12.2 us: pair_product(): pl.pallas_call(functools.partial(pair_kernel, chunks, rows), out_shape=[p...]
    slice x0 -> x4, local copies, waits for them, and re-layouts: none -> 1.54 us  [the longest x1 1.44 us: send_early(): own[start[k]:start[k] + early]]
    ppermute x20 -> x22, starting transfers between devices: 17.8 us -> 19.1 us  [swap(): return lax.ppermute(array, axis, [(i, i ^ offset) for i in range(size)])]
    split x1 -> x0, local copies, waits for them, and re-layouts: 1.01 us -> none  [gather_blocks(): pieces = jnp.split(own, len(bits), axis=0) if len(bits) > 1 else [own]]
    add x2 -> x1, other arithmetic: 0.96 us -> 0.07 us  [shards(): vv = vv + part]
  transfers between devices with their start and end apart: 20 -> 22, of which waited for: 6 -> 13; matrix products, arithmetic and copies ran while one was open for 11% -> 1% of each run, Pallas kernels for 0% -> 21%
where the time goes in v2:
time: 58.2 us; the launch traced here: 58.1 us
  waiting for transfers between devices  21.5 us (37%)
  starting transfers between devices  19.1 us (33%)
  Pallas kernels  15.7 us (27%)
  local copies, waits for them, and re-layouts  1.54 us (3%)
    ppermute x22, waiting for transfers between devices, swap(): return lax.ppermute(array, axis, [(i, i ^ offset) for i in range(size)])  21.5 us
    ppermute x22, starting transfers between devices, swap(): return lax.ppermute(array, axis, [(i, i ^ offset) for i in range(size)])  19.1 us
    pallas_call x1, Pallas kernels, pair_product(): pl.pallas_call(functools.partial(pair_kernel, chunks, rows), out_shape=[p...  12.2 us
    pallas_call x1, Pallas kernels, density_product(): pl.pallas_call(functools.partial(density_kernel, count, rows, splits), gr...  3.29 us
    slice x1, local copies, waits for them, and re-layouts, send_early(): own[start[k]:start[k] + early]  1.44 us
  transfers between devices with their start and end apart: 22, of which 13 were waited for; matrix products, arithmetic and copies ran while one was open for 1% of the time, Pallas kernels for 21%

profile of v2, /device:TPU:0, one launch (start us, length us, event | category | flops | bytes accessed | tf_op | source)
XLA Modules:
  0.0 58.1 jit_solution(13023041722792637391)
XLA Ops:
  0.0 1.4 %fusion.3 = (bf16[3,112,1024]{2,1,0:T(8,128)(2,1)S(1)}, bf16[3,112,1024]{2,1,0:T(8,128)(2,1)S(1)}) fusion(bf16[4,112,1024]{2,1,0:T(8,128)(2,1)} %bitcast.4), kind=kLoop, calls=%fused_computation.6 | loop fusion | bytes 2752512 | tf_op jit(solution)/shard_map/slice | solution.py:192
  1.5 3.0 %collective-permute-start.5 = (bf16[3,112,1024]{2,1,0:T(8,128)(2,1)S(1)}, bf16[3,112,1024]{2,1,0:T(8,128)(2,1)S(1)}, u32[]{:S(2)}, u32[]{:S(2)}) collective-permute-start(bf16[3,112,1024]{2,1,0:T(8,128)(2,1)S(1)} %get-tuple-element.49), channel_id=1, source_target_pairs={{0,16},{4,20},{8,24},{12,28},{16,0},{20,4},{24,8},{28,12},{1,17},{... | collective-permute-start | bytes 2064392 | tf_op jit(solution)/shard_map/ppermute | solution.py:15
  4.5 1.5 %collective-permute-start.4 = (bf16[3,112,1024]{2,1,0:T(8,128)(2,1)S(1)}, bf16[3,112,1024]{2,1,0:T(8,128)(2,1)S(1)}, u32[]{:S(2)}, u32[]{:S(2)}) collective-permute-start(bf16[3,112,1024]{2,1,0:T(8,128)(2,1)S(1)} %get-tuple-element.50), channel_id=1, source_target_pairs={{0,8},{4,12},{8,0},{12,4},{16,24},{20,28},{24,16},{28,20},{1,9},{5... | collective-permute-start | bytes 2064392 | tf_op jit(solution)/shard_map/ppermute | solution.py:15
  6.0 0.0 copy-start
  6.0 12.2 %shard_map.37 = (f32[112,896]{1,0:T(8,128)S(1)}, bf16[112,896]{1,0:T(8,128)(2,1)S(1)}, f32[112,896]{1,0:T(8,128)S(1)}, bf16[112,896]{1,0:T(8,128)(2,1)S(1)}, f32...) custom-call(bf16[4480,896]{1,0:T(8,128)(2,1)} %bitcast.8, ...), custom_call_target="tpu_custom_call" | custom-call | flops 7193231360 | bytes 18464768 | tf_op jit(solution)/shard_map/pallas_call | solution.py:67
  18.2 0.1 collective-permute-start
  18.3 0.5 collective-permute-start.1
  18.8 0.1 collective-permute-start.2
  18.8 0.9 %collective-permute-done.refs_4_ = bf16[112,896]{1,0:T(8,128)(2,1)S(1)} collective-permute-done((bf16[112,896]{1,0:T(8,128)(2,1)S(1)}, bf16[112,896]{1,0:T(8,128)(2,1)S(1)}, u32[]{:S(2)}, u32[]{:S(2)}) %collective-permute-start) | collective-permute-done | bytes 200736 | tf_op jit(solution)/shard_map/ppermute | solution.py:15
  19.7 0.1 collective-permute-start.3
  19.8 0.1 collective-permute-done.1.refs_5_
  20.0 0.3 collective-permute-done.2.refs_6_
  20.3 0.9 %collective-permute-done.3.refs_7_ = bf16[112,896]{1,0:T(8,128)(2,1)S(1)} collective-permute-done((bf16[112,896]{1,0:T(8,128)(2,1)S(1)}, bf16[112,896]{1,0:T(8,128)(2,1)S(1)}, u32[]{:S(2)}, u32[]{:S(2)}) %collective-permute-start.3) | collective-permute-done | bytes 200736 | tf_op jit(solution)/shard_map/ppermute | solution.py:15
  21.2 0.0 collective-permute-done.5.refs_9_.refs_1_
  21.2 0.2 collective-permute-done.4.refs_8_.refs_0_
  21.4 0.2 shard_map.38
  21.6 1.6 %collective-permute-start.6 = (bf16[112,896]{1,0:T(8,128)(2,1)S(1)}, bf16[112,896]{1,0:T(8,128)(2,1)S(1)}, u32[]{:S(2)}, u32[]{:S(2)}) collective-permute-start(bf16[112,896]{1,0:T(8,128)(2,1)S(1)} %get-tuple-element.34), channel_id=1, source_target_pairs={{0,8},{4,12},{8,0},{12,4},{16,24},{20,28},{24,16},{28,20},{1,9},{5... | collective-permute-start | bytes 602120 | tf_op jit(solution)/shard_map/ppermute | solution.py:15
  23.1 0.5 collective-permute-start.7
  23.6 1.5 %collective-permute-start.8 = (bf16[112,896]{1,0:T(8,128)(2,1)S(1)}, bf16[112,896]{1,0:T(8,128)(2,1)S(1)}, u32[]{:S(2)}, u32[]{:S(2)}) collective-permute-start(bf16[112,896]{1,0:T(8,128)(2,1)S(1)} %get-tuple-element.36), channel_id=1, source_target_pairs={{0,24},{4,28},{8,16},{12,20},{16,8},{20,12},{24,0},{28,4},{1,25},{... | collective-permute-start | bytes 602120 | tf_op jit(solution)/shard_map/ppermute | solution.py:15
  25.1 0.0 copy-done
  25.1 0.0 collective-permute-start.11
  25.1 4.4 %collective-permute-done.6.refs_4_ = bf16[112,896]{1,0:T(8,128)(2,1)S(1)} collective-permute-done((bf16[112,896]{1,0:T(8,128)(2,1)S(1)}, bf16[112,896]{1,0:T(8,128)(2,1)S(1)}, u32[]{:S(2)}, u32[]{:S(2)}) %collective-permute-start.6) | collective-permute-done | bytes 200736 | tf_op jit(solution)/shard_map/ppermute | solution.py:15
  29.5 3.6 %collective-permute-done.7.refs_5_ = bf16[112,896]{1,0:T(8,128)(2,1)S(1)} collective-permute-done((bf16[112,896]{1,0:T(8,128)(2,1)S(1)}, bf16[112,896]{1,0:T(8,128)(2,1)S(1)}, u32[]{:S(2)}, u32[]{:S(2)}) %collective-permute-start.7) | collective-permute-done | bytes 200736 | tf_op jit(solution)/shard_map/ppermute | solution.py:15
  33.1 0.0 collective-permute-done.8.refs_6_
  33.1 0.1 fusion.1
  33.2 1.6 %collective-permute-start.9 = (bf16[112,896]{1,0:T(8,128)(2,1)S(1)}, bf16[112,896]{1,0:T(8,128)(2,1)S(1)}, u32[]{:S(2)}, u32[]{:S(2)}) collective-permute-start(bf16[112,896]{1,0:T(8,128)(2,1)S(1)} %get-tuple-element.45), channel_id=1, source_target_pairs={{0,1},{1,0},{2,3},{3,2},{4,5},{5,4},{6,7},{7,6},{8,9},{9,8},{10,11... | collective-permute-start | bytes 602120 | tf_op jit(solution)/shard_map/ppermute | solution.py:15
  34.9 1.4 %collective-permute-start.12 = (bf16[1,112,1024]{2,1,0:T(8,128)(2,1)S(1)}, bf16[1,112,1024]{2,1,0:T(8,128)(2,1)S(1)}, u32[]{:S(2)}, u32[]{:S(2)}) collective-permute-start(bf16[1,112,1024]{2,1,0:T(8,128)(2,1)S(1)} %get-tuple-element.37), channel_id=1, source_target_pairs={{0,8},{4,12},{8,0},{12,4},{16,24},{20,28},{24,16},{28,20},{1,9},{5... | collective-permute-start | bytes 688136 | tf_op jit(solution)/shard_map/ppermute | solution.py:15
  36.4 0.5 collective-permute-start.13
  37.0 1.6 %collective-permute-start.15 = (bf16[2,112,1024]{2,1,0:T(8,128)(2,1)S(1)}, bf16[2,112,1024]{2,1,0:T(8,128)(2,1)S(1)}, u32[]{:S(2)}, u32[]{:S(2)}) collective-permute-start(bf16[2,112,1024]{2,1,0:T(8,128)(2,1)S(1)} %slice.23), channel_id=1, source_target_pairs={{0,16},{4,20},{8,24},{12,28},{16,0},{20,4},{24,8},{28,12},{1,17},{... | collective-permute-start | bytes 1376264 | tf_op jit(solution)/shard_map/ppermute | solution.py:15
  38.5 0.5 collective-permute-done.9
  39.1 1.3 %collective-permute-start.14 = (bf16[2,112,1024]{2,1,0:T(8,128)(2,1)S(1)}, bf16[2,112,1024]{2,1,0:T(8,128)(2,1)S(1)}, u32[]{:S(2)}, u32[]{:S(2)}) collective-permute-start(bf16[2,112,1024]{2,1,0:T(8,128)(2,1)S(1)} %slice.22), channel_id=1, source_target_pairs={{0,8},{4,12},{8,0},{12,4},{16,24},{20,28},{24,16},{28,20},{1,9},{5... | collective-permute-start | bytes 1376264 | tf_op jit(solution)/shard_map/ppermute | solution.py:15
  40.4 2.3 %collective-permute-done.12.refs_0_ = bf16[1,112,1024]{2,1,0:T(8,128)(2,1)S(1)} collective-permute-done((bf16[1,112,1024]{2,1,0:T(8,128)(2,1)S(1)}, bf16[1,112,1024]{2,1,0:T(8,128)(2,1)S(1)}, u32[]{:S(2)}, u32[]{:S(2)}) %collective-permute-start.12) | collective-permute-done | bytes 229408 | tf_op jit(solution)/shard_map/ppermute | solution.py:15
  42.8 2.8 %collective-permute-start.10 = (bf16[112,896]{1,0:T(8,128)(2,1)S(1)}, bf16[112,896]{1,0:T(8,128)(2,1)S(1)}, u32[]{:S(2)}, u32[]{:S(2)}) collective-permute-start(bf16[112,896]{1,0:T(8,128)(2,1)S(1)} %fusion), channel_id=1, source_target_pairs={{0,2},{1,3},{2,0},{3,1},{4,6},{5,7},{6,4},{7,5},{8,10},{9,11},{10,... | collective-permute-start | bytes 602120 | tf_op jit(solution)/shard_map/ppermute | solution.py:15
  45.5 0.0 collective-permute-done.13.refs_1_
  45.5 0.0 collective-permute-start.18
  45.5 5.1 %collective-permute-done.10.refs_4_ = bf16[112,896]{1,0:T(8,128)(2,1)S(1)} collective-permute-done((bf16[112,896]{1,0:T(8,128)(2,1)S(1)}, bf16[112,896]{1,0:T(8,128)(2,1)S(1)}, u32[]{:S(2)}, u32[]{:S(2)}) %collective-permute-start.10) | collective-permute-done | bytes 200736 | tf_op jit(solution)/shard_map/ppermute | solution.py:15
  50.7 0.0 collective-permute-start.17
  50.7 0.2 collective-permute-done.15.refs_3_
  50.8 0.0 collective-permute-done.14.refs_2_
  50.9 0.3 collective-permute-start.16
  51.2 0.2 collective-permute-start.20
  51.4 0.0 collective-permute-done.11.refs_1_
  51.4 0.3 collective-permute-start.21
  51.7 1.4 %collective-permute-done.16.refs_4_ = bf16[1,112,1024]{2,1,0:T(8,128)(2,1)S(1)} collective-permute-done((bf16[1,112,1024]{2,1,0:T(8,128)(2,1)S(1)}, bf16[1,112,1024]{2,1,0:T(8,128)(2,1)S(1)}, u32[]{:S(2)}, u32[]{:S(2)}) %collective-permute-start.16) | collective-permute-done | bytes 229408 | tf_op jit(solution)/shard_map/ppermute | solution.py:15
  53.1 0.1 collective-permute-start.19
  53.3 0.1 convert_add_fusion.vv_ref
  53.3 1.4 %collective-permute-done.19.refs_9_ = bf16[1,112,1024]{2,1,0:T(8,128)(2,1)S(1)} collective-permute-done((bf16[1,112,1024]{2,1,0:T(8,128)(2,1)S(1)}, bf16[1,112,1024]{2,1,0:T(8,128)(2,1)S(1)}, u32[]{:S(2)}, u32[]{:S(2)}) %collective-permute-start.19) | collective-permute-done | bytes 229408 | tf_op jit(solution)/shard_map/ppermute | solution.py:15
  54.8 0.0 collective-permute-done.18.refs_8_
  54.8 0.0 collective-permute-done.17.refs_5_
  54.8 0.0 collective-permute-done.20.refs_12_
  54.8 0.0 collective-permute-done.21.refs_13_
  54.8 3.3 %shard_map.41 = bf16[4,112,1024]{2,1,0:T(8,128)(2,1)} custom-call(f32[112,896]{1,0:T(8,128)S(1)} %convert_add_fusion.vv_ref, bf16[4,112,1024]{2,1,0:T(8,128)(2,1)S(1)} %bitcast.7, bf16[4,112,1024]{2,1,0:T(8,128)(2,1)S(1)} %collective-permute-done.11.refs_1_, bf16[1,112,1024]{2,1,0:T(8,128)(2,1)S(1)} %get-tuple-element.41.refs_2_, ...), custom_call_target="tpu_custom_call" | custom-call | tf_op jit(solution)/shard_map/pallas_call | solution.py:175
  (6 shorter events, 0.1 us)
Async XLA Ops:
  1.5 19.7 %collective-permute-start.5 = (bf16[3,112,1024]{2,1,0:T(8,128)(2,1)S(1)}, bf16[3,112,1024]{2,1,0:T(8,128)(2,1)S(1)}, u32[]{:S(2)}, u32[]{:S(2)}) collective-permute-start(bf16[3,112,1024]{2,1,0:T(8,128)(2,1)S(1)} %get-tuple-element.49), channel_id=1, source_target_pairs={{0,16},{4,20},{8,24},{12,28},{16,0},{20,4},{24,8},{28,12},{1,17},{... | collective-permute-start | bytes 2064392 | tf_op jit(solution)/shard_map/ppermute | solution.py:15
  4.5 16.9 %collective-permute-start.4 = (bf16[3,112,1024]{2,1,0:T(8,128)(2,1)S(1)}, bf16[3,112,1024]{2,1,0:T(8,128)(2,1)S(1)}, u32[]{:S(2)}, u32[]{:S(2)}) collective-permute-start(bf16[3,112,1024]{2,1,0:T(8,128)(2,1)S(1)} %get-tuple-element.50), channel_id=1, source_target_pairs={{0,8},{4,12},{8,0},{12,4},{16,24},{20,28},{24,16},{28,20},{1,9},{5... | collective-permute-start | bytes 2064392 | tf_op jit(solution)/shard_map/ppermute | solution.py:15
  6.0 19.1 %copy-start = (bf16[1024,4,112]{0,2,1:T(8,128)(2,1)S(1)}, bf16[1024,4,112]{0,2,1:T(8,128)(2,1)}, u32[]{:S(2)}) copy-start(bf16[1024,4,112]{0,2,1:T(8,128)(2,1)} %param.5) | copy-start | bytes 2752516
  18.2 1.5 %collective-permute-start = (bf16[112,896]{1,0:T(8,128)(2,1)S(1)}, bf16[112,896]{1,0:T(8,128)(2,1)S(1)}, u32[]{:S(2)}, u32[]{:S(2)}) collective-permute-start(bf16[112,896]{1,0:T(8,128)(2,1)S(1)} %get-tuple-element.29), channel_id=1, source_target_pairs={{0,4},{4,0},{8,12},{12,8},{16,20},{20,16},{24,28},{28,24},{1,5},{5... | collective-permute-start | bytes 602120 | tf_op jit(solution)/shard_map/ppermute | solution.py:15
  18.3 1.7 %collective-permute-start.1 = (bf16[112,896]{1,0:T(8,128)(2,1)S(1)}, bf16[112,896]{1,0:T(8,128)(2,1)S(1)}, u32[]{:S(2)}, u32[]{:S(2)}) collective-permute-start(bf16[112,896]{1,0:T(8,128)(2,1)S(1)} %get-tuple-element.30), channel_id=1, source_target_pairs={{0,4},{4,0},{8,12},{12,8},{16,20},{20,16},{24,28},{28,24},{1,5},{5... | collective-permute-start | bytes 602120 | tf_op jit(solution)/shard_map/ppermute | solution.py:15
  18.8 1.5 %collective-permute-start.2 = (bf16[112,896]{1,0:T(8,128)(2,1)S(1)}, bf16[112,896]{1,0:T(8,128)(2,1)S(1)}, u32[]{:S(2)}, u32[]{:S(2)}) collective-permute-start(bf16[112,896]{1,0:T(8,128)(2,1)S(1)} %get-tuple-element.31), channel_id=1, source_target_pairs={{0,4},{4,0},{8,12},{12,8},{16,20},{20,16},{24,28},{28,24},{1,5},{5... | collective-permute-start | bytes 602120 | tf_op jit(solution)/shard_map/ppermute | solution.py:15
  19.7 1.4 %collective-permute-start.3 = (bf16[112,896]{1,0:T(8,128)(2,1)S(1)}, bf16[112,896]{1,0:T(8,128)(2,1)S(1)}, u32[]{:S(2)}, u32[]{:S(2)}) collective-permute-start(bf16[112,896]{1,0:T(8,128)(2,1)S(1)} %get-tuple-element.32), channel_id=1, source_target_pairs={{0,4},{4,0},{8,12},{12,8},{16,20},{20,16},{24,28},{28,24},{1,5},{5... | collective-permute-start | bytes 602120 | tf_op jit(solution)/shard_map/ppermute | solution.py:15
  21.6 7.9 %collective-permute-start.6 = (bf16[112,896]{1,0:T(8,128)(2,1)S(1)}, bf16[112,896]{1,0:T(8,128)(2,1)S(1)}, u32[]{:S(2)}, u32[]{:S(2)}) collective-permute-start(bf16[112,896]{1,0:T(8,128)(2,1)S(1)} %get-tuple-element.34), channel_id=1, source_target_pairs={{0,8},{4,12},{8,0},{12,4},{16,24},{20,28},{24,16},{28,20},{1,9},{5... | collective-permute-start | bytes 602120 | tf_op jit(solution)/shard_map/ppermute | solution.py:15
  23.1 10.0 %collective-permute-start.7 = (bf16[112,896]{1,0:T(8,128)(2,1)S(1)}, bf16[112,896]{1,0:T(8,128)(2,1)S(1)}, u32[]{:S(2)}, u32[]{:S(2)}) collective-permute-start(bf16[112,896]{1,0:T(8,128)(2,1)S(1)} %get-tuple-element.35), channel_id=1, source_target_pairs={{0,16},{4,20},{8,24},{12,28},{16,0},{20,4},{24,8},{28,12},{1,17},{... | collective-permute-start | bytes 602120 | tf_op jit(solution)/shard_map/ppermute | solution.py:15
  23.6 9.5 %collective-permute-start.8 = (bf16[112,896]{1,0:T(8,128)(2,1)S(1)}, bf16[112,896]{1,0:T(8,128)(2,1)S(1)}, u32[]{:S(2)}, u32[]{:S(2)}) collective-permute-start(bf16[112,896]{1,0:T(8,128)(2,1)S(1)} %get-tuple-element.36), channel_id=1, source_target_pairs={{0,24},{4,28},{8,16},{12,20},{16,8},{20,12},{24,0},{28,4},{1,25},{... | collective-permute-start | bytes 602120 | tf_op jit(solution)/shard_map/ppermute | solution.py:15
  25.1 26.2 %collective-permute-start.11 = (bf16[4,112,1024]{2,1,0:T(8,128)(2,1)S(1)}, bf16[4,112,1024]{2,1,0:T(8,128)(2,1)S(1)}, u32[]{:S(2)}, u32[]{:S(2)}) collective-permute-start(bf16[4,112,1024]{2,1,0:T(8,128)(2,1)S(1)} %bitcast.5), channel_id=1, source_target_pairs={{0,4},{4,0},{8,12},{12,8},{16,20},{20,16},{24,28},{28,24},{1,5},{5... | collective-permute-start | bytes 2752520 | tf_op jit(solution)/shard_map/ppermute | solution.py:15
  33.2 5.8 %collective-permute-start.9 = (bf16[112,896]{1,0:T(8,128)(2,1)S(1)}, bf16[112,896]{1,0:T(8,128)(2,1)S(1)}, u32[]{:S(2)}, u32[]{:S(2)}) collective-permute-start(bf16[112,896]{1,0:T(8,128)(2,1)S(1)} %get-tuple-element.45), channel_id=1, source_target_pairs={{0,1},{1,0},{2,3},{3,2},{4,5},{5,4},{6,7},{7,6},{8,9},{9,8},{10,11... | collective-permute-start | bytes 602120 | tf_op jit(solution)/shard_map/ppermute | solution.py:15
  34.9 7.8 %collective-permute-start.12 = (bf16[1,112,1024]{2,1,0:T(8,128)(2,1)S(1)}, bf16[1,112,1024]{2,1,0:T(8,128)(2,1)S(1)}, u32[]{:S(2)}, u32[]{:S(2)}) collective-permute-start(bf16[1,112,1024]{2,1,0:T(8,128)(2,1)S(1)} %get-tuple-element.37), channel_id=1, source_target_pairs={{0,8},{4,12},{8,0},{12,4},{16,24},{20,28},{24,16},{28,20},{1,9},{5... | collective-permute-start | bytes 688136 | tf_op jit(solution)/shard_map/ppermute | solution.py:15
  36.4 9.2 %collective-permute-start.13 = (bf16[1,112,1024]{2,1,0:T(8,128)(2,1)S(1)}, bf16[1,112,1024]{2,1,0:T(8,128)(2,1)S(1)}, u32[]{:S(2)}, u32[]{:S(2)}) collective-permute-start(bf16[1,112,1024]{2,1,0:T(8,128)(2,1)S(1)} %get-tuple-element.38), channel_id=1, source_target_pairs={{0,16},{4,20},{8,24},{12,28},{16,0},{20,4},{24,8},{28,12},{1,17},{... | collective-permute-start | bytes 688136 | tf_op jit(solution)/shard_map/ppermute | solution.py:15
  37.0 13.9 %collective-permute-start.15 = (bf16[2,112,1024]{2,1,0:T(8,128)(2,1)S(1)}, bf16[2,112,1024]{2,1,0:T(8,128)(2,1)S(1)}, u32[]{:S(2)}, u32[]{:S(2)}) collective-permute-start(bf16[2,112,1024]{2,1,0:T(8,128)(2,1)S(1)} %slice.23), channel_id=1, source_target_pairs={{0,16},{4,20},{8,24},{12,28},{16,0},{20,4},{24,8},{28,12},{1,17},{... | collective-permute-start | bytes 1376264 | tf_op jit(solution)/shard_map/ppermute | solution.py:15
  39.1 11.8 %collective-permute-start.14 = (bf16[2,112,1024]{2,1,0:T(8,128)(2,1)S(1)}, bf16[2,112,1024]{2,1,0:T(8,128)(2,1)S(1)}, u32[]{:S(2)}, u32[]{:S(2)}) collective-permute-start(bf16[2,112,1024]{2,1,0:T(8,128)(2,1)S(1)} %slice.22), channel_id=1, source_target_pairs={{0,8},{4,12},{8,0},{12,4},{16,24},{20,28},{24,16},{28,20},{1,9},{5... | collective-permute-start | bytes 1376264 | tf_op jit(solution)/shard_map/ppermute | solution.py:15
  42.8 7.9 %collective-permute-start.10 = (bf16[112,896]{1,0:T(8,128)(2,1)S(1)}, bf16[112,896]{1,0:T(8,128)(2,1)S(1)}, u32[]{:S(2)}, u32[]{:S(2)}) collective-permute-start(bf16[112,896]{1,0:T(8,128)(2,1)S(1)} %fusion), channel_id=1, source_target_pairs={{0,2},{1,3},{2,0},{3,1},{4,6},{5,7},{6,4},{7,5},{8,10},{9,11},{10,... | collective-permute-start | bytes 602120 | tf_op jit(solution)/shard_map/ppermute | solution.py:15
  45.5 9.3 %collective-permute-start.18 = (bf16[3,112,1024]{2,1,0:T(8,128)(2,1)S(1)}, bf16[3,112,1024]{2,1,0:T(8,128)(2,1)S(1)}, u32[]{:S(2)}, u32[]{:S(2)}) collective-permute-start(bf16[3,112,1024]{2,1,0:T(8,128)(2,1)S(1)} %get-tuple-element.39.refs_6_), channel_id=1, source_target_pairs={{0,4},{4,0},{8,12},{12,8},{16,20},{20,16},{24,28},{28,24},{1,5},{5... | collective-permute-start | bytes 2064392 | tf_op jit(solution)/shard_map/ppermute | solution.py:15
  50.7 4.1 %collective-permute-start.17 = (bf16[3,112,1024]{2,1,0:T(8,128)(2,1)S(1)}, bf16[3,112,1024]{2,1,0:T(8,128)(2,1)S(1)}, u32[]{:S(2)}, u32[]{:S(2)}) collective-permute-start(bf16[3,112,1024]{2,1,0:T(8,128)(2,1)S(1)} %get-tuple-element.40.refs_3_), channel_id=1, source_target_pairs={{0,4},{4,0},{8,12},{12,8},{16,20},{20,16},{24,28},{28,24},{1,5},{5... | collective-permute-start | bytes 2064392 | tf_op jit(solution)/shard_map/ppermute | solution.py:15
  50.9 2.3 %collective-permute-start.16 = (bf16[1,112,1024]{2,1,0:T(8,128)(2,1)S(1)}, bf16[1,112,1024]{2,1,0:T(8,128)(2,1)S(1)}, u32[]{:S(2)}, u32[]{:S(2)}) collective-permute-start(bf16[1,112,1024]{2,1,0:T(8,128)(2,1)S(1)} %get-tuple-element.41.refs_2_), channel_id=1, source_target_pairs={{0,4},{4,0},{8,12},{12,8},{16,20},{20,16},{24,28},{28,24},{1,5},{5... | collective-permute-start | bytes 688136 | tf_op jit(solution)/shard_map/ppermute | solution.py:15
  51.2 3.6 %collective-permute-start.20 = (bf16[2,112,1024]{2,1,0:T(8,128)(2,1)S(1)}, bf16[2,112,1024]{2,1,0:T(8,128)(2,1)S(1)}, u32[]{:S(2)}, u32[]{:S(2)}) collective-permute-start(bf16[2,112,1024]{2,1,0:T(8,128)(2,1)S(1)} %get-tuple-element.43.refs_10_), channel_id=1, source_target_pairs={{0,4},{4,0},{8,12},{12,8},{16,20},{20,16},{24,28},{28,24},{1,5},{5... | collective-permute-start | bytes 1376264 | tf_op jit(solution)/shard_map/ppermute | solution.py:15
  51.4 3.4 %collective-permute-start.21 = (bf16[2,112,1024]{2,1,0:T(8,128)(2,1)S(1)}, bf16[2,112,1024]{2,1,0:T(8,128)(2,1)S(1)}, u32[]{:S(2)}, u32[]{:S(2)}) collective-permute-start(bf16[2,112,1024]{2,1,0:T(8,128)(2,1)S(1)} %get-tuple-element.44.refs_11_), channel_id=1, source_target_pairs={{0,4},{4,0},{8,12},{12,8},{16,20},{20,16},{24,28},{28,24},{1,5},{5... | collective-permute-start | bytes 1376264 | tf_op jit(solution)/shard_map/ppermute | solution.py:15
  53.1 1.6 %collective-permute-start.19 = (bf16[1,112,1024]{2,1,0:T(8,128)(2,1)S(1)}, bf16[1,112,1024]{2,1,0:T(8,128)(2,1)S(1)}, u32[]{:S(2)}, u32[]{:S(2)}) collective-permute-start(bf16[1,112,1024]{2,1,0:T(8,128)(2,1)S(1)} %get-tuple-element.42.refs_7_), channel_id=1, source_target_pairs={{0,4},{4,0},{8,12},{12,8},{16,20},{20,16},{24,28},{28,24},{1,5},{5... | collective-permute-start | bytes 688136 | tf_op jit(solution)/shard_map/ppermute | solution.py:15

commit v3 on v0

v3 whole, which is shorter than its diff:
```python
import functools

import jax
import jax.numpy as jnp
from jax import lax
from jax.experimental import pallas as pl
from jax.experimental.pallas import tpu as pltpu
from jax.sharding import PartitionSpec as P

AHEAD = 3
PAIR_VMEM = 40 * 2**20
SMALL_VMEM = 12 * 2**20
HBM = pl.BlockSpec(memory_space=pltpu.HBM)
VMEM = pl.BlockSpec(memory_space=pltpu.VMEM)
ANY = pl.BlockSpec(memory_space=pl.ANY)
FREE = pl.CostEstimate(flops=0, bytes_accessed=0, transcendentals=0)
LONG = pl.CostEstimate(flops=10**10, bytes_accessed=0, transcendentals=0)


def swap(array, axis, size, offset):
    return lax.ppermute(array, axis, [(i, i ^ offset) for i in range(size)])


def in_vmem(arrays):
    return [pltpu.with_memory_space_constraint(array, pltpu.VMEM) for array in arrays]


def depth_chunks(depth):
    cuts = [0]
    for size in (256, 512, 1024, 1280):
        if cuts[-1] + size < depth:
            cuts.append(cuts[-1] + size)
    while depth - cuts[-1] > 2048:
        cuts.append(cuts[-1] + 1024)
    return [(a, b - a) for a, b in zip(cuts, cuts[1:] + [depth])]


def pair_kernel(chunks, left_hbm, right_hbm, own_hbm, total, own_ref, left, right, sems, own_sem):
    copies = []
    for n, (start, size) in enumerate(chunks):
        span = pl.ds(start, size)
        pair = (
            pltpu.make_async_copy(left_hbm.at[span], left.at[span], sems.at[0, n]),
            pltpu.make_async_copy(right_hbm.at[span], right.at[span], sems.at[1, n]),
        )
        copies.append(pair)
    own_copy = pltpu.make_async_copy(own_hbm, own_ref, own_sem)
    copies.append((own_copy,))
    for copy in [copy for pair in copies[:AHEAD] for copy in pair]:
        copy.start()
    for n, (start, size) in enumerate(chunks):
        for copy in copies[n]:
            copy.wait()
        for copy in [copy for pair in copies[n + AHEAD : n + AHEAD + 1] for copy in pair]:
            copy.start()
        span = pl.ds(start, size)
        term = lax.dot_general(
            left[span], right[span], (((0,), (0,)), ((), ())), preferred_element_type=jnp.float32
        )
        if n == 0:
            total[...] = term
        else:
            total[...] += term
    own_copy.wait()


def pair_product(left, right, own):
    depth, full = left.shape
    chunks = depth_chunks(depth)
    return pl.pallas_call(
        functools.partial(pair_kernel, chunks),
        out_shape=[pltpu.VMEM((full, full), jnp.float32), pltpu.VMEM(own.shape, own.dtype)],
        in_specs=[HBM] * 3,
        out_specs=[VMEM] * 2,
        scratch_shapes=[
            pltpu.VMEM((depth, full), left.dtype),
            pltpu.VMEM((depth, full), right.dtype),
            pltpu.SemaphoreType.DMA((2, len(chunks))),
            pltpu.SemaphoreType.DMA,
        ],
        compiler_params=pltpu.CompilerParams(vmem_limit_bytes=PAIR_VMEM),
        cost_estimate=pl.CostEstimate(
            flops=2 * depth * full * full, bytes_accessed=4 * depth * full, transcendentals=0
        ),
    )(*[pltpu.with_memory_space_constraint(side, pltpu.HBM) for side in (left, right, own)])


def cut_kernel(rows, parity, total, *outs):
    me = lax.axis_index("virt")
    chips = len(outs)
    for mine in range(2 * chips):

        @pl.when(me == mine)
        def _():
            for k, out in enumerate(outs):
                chip, core = (mine >> 1) ^ k, (mine & 1) ^ parity
                pieces = []
                for side in range(2):
                    a = 2 * chip + (side ^ core)
                    for offset in range(chips):
                        b = 2 * (chip ^ offset) + core
                        pieces.append(total[a * rows : (a + 1) * rows, b * rows : (b + 1) * rows])
                out[...] = jnp.concatenate(pieces, axis=1).astype(out.dtype)


def cut(total, rows, parity, kind):
    full = total.shape[0]
    chips = full // rows // 2
    return pl.pallas_call(
        functools.partial(cut_kernel, rows, parity),
        out_shape=[pltpu.VMEM((rows, full), kind)] * chips,
        in_specs=[VMEM],
        out_specs=[VMEM] * chips,
        compiler_params=pltpu.CompilerParams(vmem_limit_bytes=SMALL_VMEM),
        cost_estimate=FREE,
    )(*in_vmem([total]))


def fold_kernel(half, *refs):
    terms, arrived, outs = refs[:half], refs[half : 2 * half], refs[len(refs) - half :]
    for term, other, out in zip(terms, arrived, outs):
        out[...] = (term[...] + other[...].astype(jnp.float32)).astype(out.dtype)


def fold(terms, arrived, after):
    shape = terms[0].shape
    kinds = [jnp.float32] + [jnp.bfloat16] * (len(terms) - 1)
    return pl.pallas_call(
        functools.partial(fold_kernel, len(terms)),
        out_shape=[pltpu.VMEM(shape, kind) for kind in kinds],
        in_specs=[VMEM] * (2 * len(terms)) + [ANY] * len(after),
        out_specs=[VMEM] * len(terms),
        compiler_params=pltpu.CompilerParams(vmem_limit_bytes=SMALL_VMEM),
        cost_estimate=FREE,
    )(*in_vmem([*terms, *arrived]), *after)


def total_kernel(parts, *refs):
    wide, narrow = refs[-2:]
    total = refs[0][...]
    for ref in refs[1:parts]:
        total += ref[...].astype(jnp.float32)
    wide[...] = total
    narrow[...] = total.astype(narrow.dtype)


def total(parts, after, flops=0):
    shape = parts[0].shape
    return pl.pallas_call(
        functools.partial(total_kernel, len(parts)),
        out_shape=[pltpu.VMEM(shape, jnp.float32), pltpu.VMEM(shape, jnp.bfloat16)],
        in_specs=[VMEM] * len(parts) + [ANY] * len(after),
        out_specs=[VMEM] * 2,
        compiler_params=pltpu.CompilerParams(vmem_limit_bytes=SMALL_VMEM),
        cost_estimate=pl.CostEstimate(flops=flops, bytes_accessed=0, transcendentals=0),
    )(*in_vmem(parts), *after)


def low_kernel(vv_ref, part_ref, low_ref):
    rows, full = vv_ref.shape
    whole = vv_ref[...] + part_ref[...].astype(jnp.float32)
    for side in range(2):
        half = whole[:, side * (full // 2) : (side + 1) * (full // 2)]
        low_ref[side * rows : (side + 1) * rows] = half.astype(low_ref.dtype)


def low_rows(vv, part):
    rows, full = vv.shape
    return pl.pallas_call(
        low_kernel,
        out_shape=pltpu.VMEM((2 * rows, full // 2), jnp.bfloat16),
        in_specs=[VMEM] * 2,
        out_specs=VMEM,
        compiler_params=pltpu.CompilerParams(vmem_limit_bytes=SMALL_VMEM),
        cost_estimate=FREE,
    )(*in_vmem([vv, part]))


def pass_kernel(*refs):
    pass


def hold(arrays, after, cost):
    return pl.pallas_call(
        pass_kernel,
        out_shape=[jax.ShapeDtypeStruct(array.shape, array.dtype) for array in arrays],
        in_specs=[ANY] * (len(arrays) + len(after)),
        out_specs=[ANY] * len(arrays),
        input_output_aliases={n: n for n in range(len(arrays))},
        compiler_params=pltpu.CompilerParams(vmem_limit_bytes=2**20),
        cost_estimate=cost,
    )(*arrays, *after)


def density_kernel(spans, low_ref, *refs):
    *blocks, mine_ref, theirs_ref = refs
    rows = mine_ref.shape[1]
    for i in range(mine_ref.shape[0]):
        flat = jnp.concatenate([block[start + i] for block, start in zip(blocks, spans)], axis=0)
        both = jnp.dot(low_ref[...], flat, preferred_element_type=jnp.float32)
        mine_ref[i] = both[:rows]
        theirs_ref[i] = both[rows:].astype(theirs_ref.dtype)


def density_product(low, blocks, count):
    rows = low.shape[0] // 2
    vectors = blocks[0][0].shape[2]
    shape = (count, rows, vectors)
    return pl.pallas_call(
        functools.partial(density_kernel, [start for _, start in blocks]),
        out_shape=[pltpu.VMEM(shape, jnp.float32), pltpu.VMEM(shape, jnp.bfloat16)],
        in_specs=[VMEM] * (1 + len(blocks)),
        out_specs=[VMEM] * 2,
        compiler_params=pltpu.CompilerParams(vmem_limit_bytes=SMALL_VMEM),
        cost_estimate=FREE,
    )(*in_vmem([low, *[array for array, _ in blocks]]))


def join_kernel(mine_ref, arrived_ref, *refs):
    i = pl.program_id(0)
    refs[-1][0] = (mine_ref[i] + arrived_ref[i].astype(jnp.float32)).astype(refs[-1].dtype)


def join(mine, arrived, occ, start, base):
    count, rows, vectors = mine.shape
    given = [] if base is None else [base]
    return pl.pallas_call(
        join_kernel,
        grid=(count,),
        out_shape=jax.ShapeDtypeStruct((occ, rows, vectors), jnp.bfloat16),
        in_specs=[VMEM] * 2 + [ANY] * len(given),
        out_specs=pl.BlockSpec((1, rows, vectors), lambda i: (i + start, 0, 0)),
        input_output_aliases={2: 0} if given else {},
        compiler_params=pltpu.CompilerParams(vmem_limit_bytes=SMALL_VMEM),
        cost_estimate=FREE,
    )(*in_vmem([mine, arrived]), *given)


def permuted(count, groups, lambda_amps, t2_amps, chol_ov):
    rows, full = chol_ov.shape[2], lambda_amps.shape[2]
    own = jnp.transpose(chol_ov, (1, 2, 0))
    occ = own.shape[0]
    half = occ // 2
    bits = [k for k in range(2, count) if k & (k - 1) == 0]
    came = {k: swap(own, "virt", count, k) for k in bits}

    product, own = pair_product(lambda_amps.reshape(-1, full), t2_amps.reshape(-1, full), own)
    even = range(0, count, 2)
    arrived = [swap(part, "virt", count, 1) for part in cut(product, rows, 1, jnp.bfloat16)]
    sums = fold(cut(product, rows, 0, jnp.float32), arrived, [])
    arrived = [swap(sums[k // 2], "virt", count, k) for k in range(2, count, 2)]
    vv, narrow = total([sums[0], *arrived], list(came.values()))
    came = dict(zip(bits, hold(list(came.values()), arrived[:1], FREE)))

    held = {0: [(own, 0), (own, half)]} | {k: [(came[k], 0), (came[k], half)] for k in bits}
    for k in sorted(set(even) - set(held), key=lambda k: (bin(k).count("1"), k)):
        low_bit, high_bit = k & -k, 1 << (k.bit_length() - 1)
        lower, start = held[k ^ low_bit][0]
        upper, middle = held[k ^ high_bit][1]
        lower = lower[start : start + half]
        upper = upper[middle : middle + occ - half]
        held[k] = [
            (swap(lower, "virt", count, low_bit), 0),
            (swap(upper, "virt", count, high_bit), 0),
        ]
    step = 1
    while step < groups:
        part = swap(narrow, "pair", groups, step)
        if 2 * step < groups:
            vv, narrow = total([vv, part], [], 2 * 10**9)
        step *= 2
    low = low_rows(vv, part)
    parts = []
    for n, size in enumerate((half, occ - half)):
        mine, theirs = density_product(low, [held[k][n] for k in even], size)
        parts.append((mine, swap(theirs, "virt", count, 1), occ, n * half))
    density = None
    for part in parts:
        density = join(*part, density)
    return jnp.transpose(density, (2, 0, 1))


def gathered(lambda_amps, t2_amps, chol_ov):
    vv = lax.dot_general(
        lambda_amps, t2_amps, (((0, 1), (0, 1)), ((), ())), preferred_element_type=jnp.float32
    )
    vv = lax.psum_scatter(vv, "virt", scatter_dimension=0, tiled=True)
    low = lax.psum(vv, "pair").astype(jnp.bfloat16)
    blocks = lax.all_gather(jnp.transpose(chol_ov, (1, 2, 0)), "virt", axis=1, tiled=True)
    density = jnp.einsum("ab,ibq->iaq", low, blocks, preferred_element_type=jnp.float32)
    return jnp.transpose(density, (2, 0, 1)).astype(jnp.bfloat16)


def solution(mesh):
    count, groups = mesh.shape["virt"], mesh.shape["pair"]
    paired = count & (count - 1) == 0 and groups & (groups - 1) == 0 and count > 3 and groups > 1

    def shards(lambda_amps, t2_amps, chol_ov):
        if paired and chol_ov.shape[2] % 16 == 0 and chol_ov.shape[1] > 1:
            return permuted(count, groups, lambda_amps, t2_amps, chol_ov)
        return gathered(lambda_amps, t2_amps, chol_ov)

    placed = (P("pair", "virt", None), P("pair", "virt", None), P("pair", None, "virt"))
    return jax.shard_map(
        shards, mesh=mesh, in_specs=placed, out_specs=P("pair", None, "virt"), check_vma=False
    )
```

time: 162 us -> 53.8 us (0.33)
  waiting for transfers between devices: 73.9 us -> 21.8 us
  blocking collectives: 27.6 us -> 0 us
  local copies, waits for them, and re-layouts: 26.7 us -> 0.06 us
  matrix products: 19.5 us -> 0 us
  starting transfers between devices: 0.04 us -> 15.9 us
  Pallas kernels: 0 us -> 15.7 us
  between operations: 13.4 us -> 0.13 us
    reduce_scatter x1 -> x0, waiting for transfers between devices: 48.7 us -> none  [shards(): vv_rows = lax.psum_scatter(summed, 'virt', scatter_dimension=0, tiled=True)]
    psum x1 -> x0, blocking collectives: 27.6 us -> none  [shards(): summed = lax.psum(partial_value, 'pair')]
    all_gather x1 -> x0, waiting for transfers between devices: 24.5 us -> none  [shards(): piece = lax.all_gather(chol_ov, 'virt', axis=2, tiled=True)]
    ppermute x0 -> x15, waiting for transfers between devices: none -> 21.8 us  [swap(): return lax.ppermute(array, axis, [(i, i ^ offset) for i in range(size)])]
    dot_general x2 -> x0, matrix products: 19.5 us -> none  [the longest x1 14.1 us: pair_product(): lax.dot_general(left, right, (((0, 1), (0, 1)), ((), ())), preferred_elem...]
    ppermute x0 -> x15, starting transfers between devices: none -> 15.9 us  [swap(): return lax.ppermute(array, axis, [(i, i ^ offset) for i in range(size)])]
    pallas_call x0 -> x12, Pallas kernels: none -> 15.7 us  [the longest x1 10.8 us: pair_product(): pl.pallas_call(functools.partial(pair_kernel, chunks), out_shape=[pltpu.V...]
    all_gather x1 -> x0, local copies, waits for them, and re-layouts: 12.3 us -> none  [shards(): piece = lax.all_gather(chol_ov, 'virt', axis=2, tiled=True)]
  transfers between devices with their start and end apart: 2 -> 15, of which waited for: 2 -> 8; matrix products, arithmetic and copies ran while one was open for 0% -> 0% of each run, Pallas kernels for 0% -> 28%
where the time goes in v3:
time: 53.8 us; the launch traced here: 53.6 us
  waiting for transfers between devices  21.8 us (41%)
  starting transfers between devices  15.9 us (30%)
  Pallas kernels  15.7 us (29%)
    ppermute x15, waiting for transfers between devices, swap(): return lax.ppermute(array, axis, [(i, i ^ offset) for i in range(size)])  21.8 us
    ppermute x15, starting transfers between devices, swap(): return lax.ppermute(array, axis, [(i, i ^ offset) for i in range(size)])  15.9 us
    pallas_call x1, Pallas kernels, pair_product(): pl.pallas_call(functools.partial(pair_kernel, chunks), out_shape=[pltpu.V...  10.8 us
    pallas_call x2, Pallas kernels, join(): pl.pallas_call(join_kernel, grid=(count,), out_shape=jax.ShapeDtypeStruct...  1.61 us
    pallas_call x2, Pallas kernels, cut(): pl.pallas_call(functools.partial(cut_kernel, rows, parity), out_shape=[pl...  1.49 us
    pallas_call x2, Pallas kernels, density_product(): pl.pallas_call(functools.partial(density_kernel, [start for _, start in b...  1.3 us
  transfers between devices with their start and end apart: 15, of which 8 were waited for; matrix products, arithmetic and copies ran while one was open for 0% of the time, Pallas kernels for 28%

profile of v3, /device:TPU:0, one launch (start us, length us, event | category | flops | bytes accessed | tf_op | source)
XLA Modules:
  0.0 53.6 jit_solution(5595197205016544849)
XLA Ops:
  0.0 2.9 %collective-permute-start.7 = (bf16[4,112,1024]{2,1,0:T(8,128)(2,1)}, bf16[4,112,1024]{2,1,0:T(8,128)(2,1)S(1)}, u32[]{:S(2)}, u32[]{:S(2)}) collective-permute-start(bf16[4,112,1024]{2,1,0:T(8,128)(2,1)} %bitcast.6), channel_id=1, source_target_pairs={{0,8},{4,12},{8,0},{12,4},{16,24},{20,28},{24,16},{28,20},{1,9},{5... | collective-permute-start | bytes 2752520 | tf_op jit(solution)/shard_map/ppermute | solution.py:21
  2.9 1.5 %collective-permute-start.8 = (bf16[4,112,1024]{2,1,0:T(8,128)(2,1)}, bf16[4,112,1024]{2,1,0:T(8,128)(2,1)S(1)}, u32[]{:S(2)}, u32[]{:S(2)}) collective-permute-start(bf16[4,112,1024]{2,1,0:T(8,128)(2,1)} %bitcast.7), channel_id=1, source_target_pairs={{0,16},{4,20},{8,24},{12,28},{16,0},{20,4},{24,8},{28,12},{1,17},{... | collective-permute-start | bytes 2752520 | tf_op jit(solution)/shard_map/ppermute | solution.py:21
  4.5 10.8 %shard_map.37 = (f32[896,896]{1,0:T(8,128)S(1)}, bf16[4,112,1024]{2,1,0:T(8,128)(2,1)S(1)}) custom-call(bf16[4480,896]{1,0:T(8,128)(2,1)} %bitcast.4, bf16[4480,896]{1,0:T(8,128)(2,1)} %bitcast.5, bf16[4,112,1024]{2,1,0:T(8,128)(2,1)} %bitcast.8), custom_call_target="tpu_custom_call" | custom-call | flops 7193231360 | bytes 16056320 | tf_op jit(solution)/shard_map/pallas_call | solution.py:70
  15.3 0.5 shard_map.39
  15.8 0.1 collective-permute-start
  15.9 0.5 collective-permute-start.1
  16.4 0.1 collective-permute-start.2
  16.5 0.9 %collective-permute-done.refs_4_ = bf16[112,896]{1,0:T(8,128)(2,1)S(1)} collective-permute-done((bf16[112,896]{1,0:T(8,128)(2,1)S(1)}, bf16[112,896]{1,0:T(8,128)(2,1)S(1)}, u32[]{:S(2)}, u32[]{:S(2)}) %collective-permute-start) | collective-permute-done | bytes 200736 | tf_op jit(solution)/shard_map/ppermute | solution.py:21
  17.3 0.1 collective-permute-start.3
  17.5 1.0 %shard_map.38 = (f32[112,896]{1,0:T(8,128)S(1)}, f32[112,896]{1,0:T(8,128)S(1)}, f32[112,896]{1,0:T(8,128)S(1)}, f32[112,896]{1,0:T(8,128)S(1)}) custom-call(f32[896,896]{1,0:T(8,128)S(1)} %get-tuple-element.29.total), custom_call_target="tpu_custom_call" | custom-call | tf_op jit(solution)/shard_map/pallas_call | solution.py:109
  18.5 0.0 collective-permute-done.1.refs_5_
  18.5 0.0 collective-permute-done.2.refs_6_
  18.5 0.3 collective-permute-done.3.refs_7_
  18.8 0.2 shard_map.40
  18.9 0.6 %collective-permute-start.4 = (bf16[112,896]{1,0:T(8,128)(2,1)S(1)}, bf16[112,896]{1,0:T(8,128)(2,1)S(1)}, u32[]{:S(2)}, u32[]{:S(2)}) collective-permute-start(bf16[112,896]{1,0:T(8,128)(2,1)S(1)} %get-tuple-element.39), channel_id=1, source_target_pairs={{0,8},{4,12},{8,0},{12,4},{16,24},{20,28},{24,16},{28,20},{1,9},{5... | collective-permute-start | bytes 602120 | tf_op jit(solution)/shard_map/ppermute | solution.py:21
  19.5 0.1 collective-permute-start.5
  19.6 2.9 %collective-permute-start.6 = (bf16[112,896]{1,0:T(8,128)(2,1)S(1)}, bf16[112,896]{1,0:T(8,128)(2,1)S(1)}, u32[]{:S(2)}, u32[]{:S(2)}) collective-permute-start(bf16[112,896]{1,0:T(8,128)(2,1)S(1)} %get-tuple-element.41), channel_id=1, source_target_pairs={{0,24},{4,28},{8,16},{12,20},{16,8},{20,12},{24,0},{28,4},{1,25},{... | collective-permute-start | bytes 602120 | tf_op jit(solution)/shard_map/ppermute | solution.py:21
  22.5 6.1 %collective-permute-done.4.refs_1_.refs_2_ = bf16[112,896]{1,0:T(8,128)(2,1)S(1)} collective-permute-done((bf16[112,896]{1,0:T(8,128)(2,1)S(1)}, bf16[112,896]{1,0:T(8,128)(2,1)S(1)}, u32[]{:S(2)}, u32[]{:S(2)}) %collective-permute-start.4) | collective-permute-done | bytes 200736 | tf_op jit(solution)/shard_map/ppermute | solution.py:21
  28.6 4.9 %collective-permute-done.5.refs_2_ = bf16[112,896]{1,0:T(8,128)(2,1)S(1)} collective-permute-done((bf16[112,896]{1,0:T(8,128)(2,1)S(1)}, bf16[112,896]{1,0:T(8,128)(2,1)S(1)}, u32[]{:S(2)}, u32[]{:S(2)}) %collective-permute-start.5) | collective-permute-done | bytes 200736 | tf_op jit(solution)/shard_map/ppermute | solution.py:21
  33.6 0.0 collective-permute-done.6.refs_3_
  33.6 0.0 collective-permute-done.7.refs_4_.refs_0_
  33.6 0.0 collective-permute-done.8.refs_5_.refs_1_
  33.6 0.1 shard_map.41
  33.7 1.6 %collective-permute-start.9 = (bf16[112,896]{1,0:T(8,128)(2,1)S(1)}, bf16[112,896]{1,0:T(8,128)(2,1)S(1)}, u32[]{:S(2)}, u32[]{:S(2)}) collective-permute-start(bf16[112,896]{1,0:T(8,128)(2,1)S(1)} %get-tuple-element.43), channel_id=1, source_target_pairs={{0,1},{1,0},{2,3},{3,2},{4,5},{5,4},{6,7},{7,6},{8,9},{9,8},{10,11... | collective-permute-start | bytes 602120 | tf_op jit(solution)/shard_map/ppermute | solution.py:21
  35.4 1.3 %collective-permute-start.13 = (bf16[2,112,1024]{2,1,0:T(8,128)(2,1)S(1)}, bf16[2,112,1024]{2,1,0:T(8,128)(2,1)S(1)}, u32[]{:S(2)}, u32[]{:S(2)}) collective-permute-start(bf16[2,112,1024]{2,1,0:T(8,128)(2,1)S(1)} %slice.7), channel_id=1, source_target_pairs={{0,8},{4,12},{8,0},{12,4},{16,24},{20,28},{24,16},{28,20},{1,9},{5... | collective-permute-start | bytes 1376264 | tf_op jit(solution)/shard_map/ppermute | solution.py:21
  36.7 0.9 %collective-permute-start.11 = (bf16[2,112,1024]{2,1,0:T(8,128)(2,1)S(1)}, bf16[2,112,1024]{2,1,0:T(8,128)(2,1)S(1)}, u32[]{:S(2)}, u32[]{:S(2)}) collective-permute-start(bf16[2,112,1024]{2,1,0:T(8,128)(2,1)S(1)} %slice.6), channel_id=1, source_target_pairs={{0,16},{4,20},{8,24},{12,28},{16,0},{20,4},{24,8},{28,12},{1,17},{... | collective-permute-start | bytes 1376264 | tf_op jit(solution)/shard_map/ppermute | solution.py:21
  37.6 1.9 %collective-permute-done.9.refs_1_ = bf16[112,896]{1,0:T(8,128)(2,1)S(1)} collective-permute-done((bf16[112,896]{1,0:T(8,128)(2,1)S(1)}, bf16[112,896]{1,0:T(8,128)(2,1)S(1)}, u32[]{:S(2)}, u32[]{:S(2)}) %collective-permute-start.9) | collective-permute-done | bytes 200736 | tf_op jit(solution)/shard_map/ppermute | solution.py:21
  39.5 0.1 shard_map.42
  39.5 2.7 %collective-permute-start.10 = (bf16[112,896]{1,0:T(8,128)(2,1)S(1)}, bf16[112,896]{1,0:T(8,128)(2,1)S(1)}, u32[]{:S(2)}, u32[]{:S(2)}) collective-permute-start(bf16[112,896]{1,0:T(8,128)(2,1)S(1)} %get-tuple-element.45), channel_id=1, source_target_pairs={{0,2},{1,3},{2,0},{3,1},{4,6},{5,7},{6,4},{7,5},{8,10},{9,11},{10,... | collective-permute-start | bytes 602120 | tf_op jit(solution)/shard_map/ppermute | solution.py:21
  42.2 7.1 %collective-permute-done.10.part_ref = bf16[112,896]{1,0:T(8,128)(2,1)S(1)} collective-permute-done((bf16[112,896]{1,0:T(8,128)(2,1)S(1)}, bf16[112,896]{1,0:T(8,128)(2,1)S(1)}, u32[]{:S(2)}, u32[]{:S(2)}) %collective-permute-start.10) | collective-permute-done | bytes 200736 | tf_op jit(solution)/shard_map/ppermute | solution.py:21
  49.3 0.1 shard_map.43.low_ref
  49.4 0.0 collective-permute-done.13.refs_3_
  49.4 0.6 %shard_map.46 = (f32[2,112,1024]{2,1,0:T(8,128)S(1)}, bf16[2,112,1024]{2,1,0:T(8,128)(2,1)S(1)}) custom-call(bf16[224,448]{1,0:T(8,128)(2,1)S(1)} %shard_map.43.low_ref, bf16[4,112,1024]{2,1,0:T(8,128)(2,1)S(1)} %get-tuple-element.46.refs_0_, bf16[4,112,1024]{2,1,0:T(8,128)(2,1)S(1)} %get-tuple-element.47.refs_1_, ...), custom_call_target="tpu_custom_call" | custom-call | tf_op jit(solution)/shard_map/pallas_call | solution.py:209
  50.1 0.1 collective-permute-start.14
  50.2 0.0 collective-permute-done.11.refs_3_
  50.2 0.6 %shard_map.45 = (f32[2,112,1024]{2,1,0:T(8,128)S(1)}, bf16[2,112,1024]{2,1,0:T(8,128)(2,1)S(1)}) custom-call(bf16[224,448]{1,0:T(8,128)(2,1)S(1)} %shard_map.43.low_ref, bf16[4,112,1024]{2,1,0:T(8,128)(2,1)S(1)} %get-tuple-element.46.refs_0_, bf16[4,112,1024]{2,1,0:T(8,128)(2,1)S(1)} %get-tuple-element.47.refs_1_, ...), custom_call_target="tpu_custom_call" | custom-call | tf_op jit(solution)/shard_map/pallas_call | solution.py:209
  50.8 0.6 %collective-permute-start.12 = (bf16[2,112,1024]{2,1,0:T(8,128)(2,1)S(1)}, bf16[2,112,1024]{2,1,0:T(8,128)(2,1)S(1)}, u32[]{:S(2)}, u32[]{:S(2)}) collective-permute-start(bf16[2,112,1024]{2,1,0:T(8,128)(2,1)S(1)} %get-tuple-element.50), channel_id=1, source_target_pairs={{0,4},{4,0},{8,12},{12,8},{16,20},{20,16},{24,28},{28,24},{1,5},{5... | collective-permute-start | bytes 1376264 | tf_op jit(solution)/shard_map/ppermute | solution.py:21
  51.4 0.6 %collective-permute-done.14.arrived_ref = bf16[2,112,1024]{2,1,0:T(8,128)(2,1)S(1)} collective-permute-done((bf16[2,112,1024]{2,1,0:T(8,128)(2,1)S(1)}, bf16[2,112,1024]{2,1,0:T(8,128)(2,1)S(1)}, u32[]{:S(2)}, u32[]{:S(2)}) %collective-permute-start.14) | collective-permute-done | bytes 458784 | tf_op jit(solution)/shard_map/ppermute | solution.py:21
  52.0 0.8 %shard_map.47.refs_0_ = bf16[4,112,1024]{2,1,0:T(8,128)(2,1)} custom-call(f32[2,112,1024]{2,1,0:T(8,128)S(1)} %get-tuple-element.51.mine_ref, bf16[2,112,1024]{2,1,0:T(8,128)(2,1)S(1)} %collective-permute-done.14.arrived_ref), custom_call_target="tpu_custom_call" | custom-call | tf_op jit(solution)/shard_map/pallas_call | solution.py:227
  52.8 0.1 collective-permute-done.12.arrived_ref
  52.8 0.8 %shard_map.48 = bf16[4,112,1024]{2,1,0:T(8,128)(2,1)} custom-call(f32[2,112,1024]{2,1,0:T(8,128)S(1)} %get-tuple-element.49.mine_ref, bf16[2,112,1024]{2,1,0:T(8,128)(2,1)S(1)} %collective-permute-done.12.arrived_ref, bf16[4,112,1024]{2,1,0:T(8,128)(2,1)} %shard_map.47.refs_0_), custom_call_target="tpu_custom_call", output_to_operand_aliasing={{}: (2, {})} | custom-call | tf_op jit(solution)/shard_map/pallas_call | solution.py:227
  (3 shorter events, 0.1 us)
Async XLA Ops:
  0.0 33.6 %collective-permute-start.7 = (bf16[4,112,1024]{2,1,0:T(8,128)(2,1)}, bf16[4,112,1024]{2,1,0:T(8,128)(2,1)S(1)}, u32[]{:S(2)}, u32[]{:S(2)}) collective-permute-start(bf16[4,112,1024]{2,1,0:T(8,128)(2,1)} %bitcast.6), channel_id=1, source_target_pairs={{0,8},{4,12},{8,0},{12,4},{16,24},{20,28},{24,16},{28,20},{1,9},{5... | collective-permute-start | bytes 2752520 | tf_op jit(solution)/shard_map/ppermute | solution.py:21
  2.9 30.6 %collective-permute-start.8 = (bf16[4,112,1024]{2,1,0:T(8,128)(2,1)}, bf16[4,112,1024]{2,1,0:T(8,128)(2,1)S(1)}, u32[]{:S(2)}, u32[]{:S(2)}) collective-permute-start(bf16[4,112,1024]{2,1,0:T(8,128)(2,1)} %bitcast.7), channel_id=1, source_target_pairs={{0,16},{4,20},{8,24},{12,28},{16,0},{20,4},{24,8},{28,12},{1,17},{... | collective-permute-start | bytes 2752520 | tf_op jit(solution)/shard_map/ppermute | solution.py:21
  15.8 1.5 %collective-permute-start = (bf16[112,896]{1,0:T(8,128)(2,1)S(1)}, bf16[112,896]{1,0:T(8,128)(2,1)S(1)}, u32[]{:S(2)}, u32[]{:S(2)}) collective-permute-start(bf16[112,896]{1,0:T(8,128)(2,1)S(1)} %get-tuple-element.34), channel_id=1, source_target_pairs={{0,4},{4,0},{8,12},{12,8},{16,20},{20,16},{24,28},{28,24},{1,5},{5... | collective-permute-start | bytes 602120 | tf_op jit(solution)/shard_map/ppermute | solution.py:21
  15.9 2.6 %collective-permute-start.1 = (bf16[112,896]{1,0:T(8,128)(2,1)S(1)}, bf16[112,896]{1,0:T(8,128)(2,1)S(1)}, u32[]{:S(2)}, u32[]{:S(2)}) collective-permute-start(bf16[112,896]{1,0:T(8,128)(2,1)S(1)} %get-tuple-element.35), channel_id=1, source_target_pairs={{0,4},{4,0},{8,12},{12,8},{16,20},{20,16},{24,28},{28,24},{1,5},{5... | collective-permute-start | bytes 602120 | tf_op jit(solution)/shard_map/ppermute | solution.py:21
  16.4 2.1 %collective-permute-start.2 = (bf16[112,896]{1,0:T(8,128)(2,1)S(1)}, bf16[112,896]{1,0:T(8,128)(2,1)S(1)}, u32[]{:S(2)}, u32[]{:S(2)}) collective-permute-start(bf16[112,896]{1,0:T(8,128)(2,1)S(1)} %get-tuple-element.36), channel_id=1, source_target_pairs={{0,4},{4,0},{8,12},{12,8},{16,20},{20,16},{24,28},{28,24},{1,5},{5... | collective-permute-start | bytes 602120 | tf_op jit(solution)/shard_map/ppermute | solution.py:21
  17.3 1.4 %collective-permute-start.3 = (bf16[112,896]{1,0:T(8,128)(2,1)S(1)}, bf16[112,896]{1,0:T(8,128)(2,1)S(1)}, u32[]{:S(2)}, u32[]{:S(2)}) collective-permute-start(bf16[112,896]{1,0:T(8,128)(2,1)S(1)} %get-tuple-element.37), channel_id=1, source_target_pairs={{0,4},{4,0},{8,12},{12,8},{16,20},{20,16},{24,28},{28,24},{1,5},{5... | collective-permute-start | bytes 602120 | tf_op jit(solution)/shard_map/ppermute | solution.py:21
  18.9 9.7 %collective-permute-start.4 = (bf16[112,896]{1,0:T(8,128)(2,1)S(1)}, bf16[112,896]{1,0:T(8,128)(2,1)S(1)}, u32[]{:S(2)}, u32[]{:S(2)}) collective-permute-start(bf16[112,896]{1,0:T(8,128)(2,1)S(1)} %get-tuple-element.39), channel_id=1, source_target_pairs={{0,8},{4,12},{8,0},{12,4},{16,24},{20,28},{24,16},{28,20},{1,9},{5... | collective-permute-start | bytes 602120 | tf_op jit(solution)/shard_map/ppermute | solution.py:21
  19.5 14.0 %collective-permute-start.5 = (bf16[112,896]{1,0:T(8,128)(2,1)S(1)}, bf16[112,896]{1,0:T(8,128)(2,1)S(1)}, u32[]{:S(2)}, u32[]{:S(2)}) collective-permute-start(bf16[112,896]{1,0:T(8,128)(2,1)S(1)} %get-tuple-element.40), channel_id=1, source_target_pairs={{0,16},{4,20},{8,24},{12,28},{16,0},{20,4},{24,8},{28,12},{1,17},{... | collective-permute-start | bytes 602120 | tf_op jit(solution)/shard_map/ppermute | solution.py:21
  19.6 14.0 %collective-permute-start.6 = (bf16[112,896]{1,0:T(8,128)(2,1)S(1)}, bf16[112,896]{1,0:T(8,128)(2,1)S(1)}, u32[]{:S(2)}, u32[]{:S(2)}) collective-permute-start(bf16[112,896]{1,0:T(8,128)(2,1)S(1)} %get-tuple-element.41), channel_id=1, source_target_pairs={{0,24},{4,28},{8,16},{12,20},{16,8},{20,12},{24,0},{28,4},{1,25},{... | collective-permute-start | bytes 602120 | tf_op jit(solution)/shard_map/ppermute | solution.py:21
  33.7 5.8 %collective-permute-start.9 = (bf16[112,896]{1,0:T(8,128)(2,1)S(1)}, bf16[112,896]{1,0:T(8,128)(2,1)S(1)}, u32[]{:S(2)}, u32[]{:S(2)}) collective-permute-start(bf16[112,896]{1,0:T(8,128)(2,1)S(1)} %get-tuple-element.43), channel_id=1, source_target_pairs={{0,1},{1,0},{2,3},{3,2},{4,5},{5,4},{6,7},{7,6},{8,9},{9,8},{10,11... | collective-permute-start | bytes 602120 | tf_op jit(solution)/shard_map/ppermute | solution.py:21
  35.4 14.1 %collective-permute-start.13 = (bf16[2,112,1024]{2,1,0:T(8,128)(2,1)S(1)}, bf16[2,112,1024]{2,1,0:T(8,128)(2,1)S(1)}, u32[]{:S(2)}, u32[]{:S(2)}) collective-permute-start(bf16[2,112,1024]{2,1,0:T(8,128)(2,1)S(1)} %slice.7), channel_id=1, source_target_pairs={{0,8},{4,12},{8,0},{12,4},{16,24},{20,28},{24,16},{28,20},{1,9},{5... | collective-permute-start | bytes 1376264 | tf_op jit(solution)/shard_map/ppermute | solution.py:21
  36.7 13.5 %collective-permute-start.11 = (bf16[2,112,1024]{2,1,0:T(8,128)(2,1)S(1)}, bf16[2,112,1024]{2,1,0:T(8,128)(2,1)S(1)}, u32[]{:S(2)}, u32[]{:S(2)}) collective-permute-start(bf16[2,112,1024]{2,1,0:T(8,128)(2,1)S(1)} %slice.6), channel_id=1, source_target_pairs={{0,16},{4,20},{8,24},{12,28},{16,0},{20,4},{24,8},{28,12},{1,17},{... | collective-permute-start | bytes 1376264 | tf_op jit(solution)/shard_map/ppermute | solution.py:21
  39.5 9.8 %collective-permute-start.10 = (bf16[112,896]{1,0:T(8,128)(2,1)S(1)}, bf16[112,896]{1,0:T(8,128)(2,1)S(1)}, u32[]{:S(2)}, u32[]{:S(2)}) collective-permute-start(bf16[112,896]{1,0:T(8,128)(2,1)S(1)} %get-tuple-element.45), channel_id=1, source_target_pairs={{0,2},{1,3},{2,0},{3,1},{4,6},{5,7},{6,4},{7,5},{8,10},{9,11},{10,... | collective-permute-start | bytes 602120 | tf_op jit(solution)/shard_map/ppermute | solution.py:21
  50.1 1.9 %collective-permute-start.14 = (bf16[2,112,1024]{2,1,0:T(8,128)(2,1)S(1)}, bf16[2,112,1024]{2,1,0:T(8,128)(2,1)S(1)}, u32[]{:S(2)}, u32[]{:S(2)}) collective-permute-start(bf16[2,112,1024]{2,1,0:T(8,128)(2,1)S(1)} %get-tuple-element.52), channel_id=1, source_target_pairs={{0,4},{4,0},{8,12},{12,8},{16,20},{20,16},{24,28},{28,24},{1,5},{5... | collective-permute-start | bytes 1376264 | tf_op jit(solution)/shard_map/ppermute | solution.py:21
  50.8 2.0 %collective-permute-start.12 = (bf16[2,112,1024]{2,1,0:T(8,128)(2,1)S(1)}, bf16[2,112,1024]{2,1,0:T(8,128)(2,1)S(1)}, u32[]{:S(2)}, u32[]{:S(2)}) collective-permute-start(bf16[2,112,1024]{2,1,0:T(8,128)(2,1)S(1)} %get-tuple-element.50), channel_id=1, source_target_pairs={{0,4},{4,0},{8,12},{12,8},{16,20},{20,16},{24,28},{28,24},{1,5},{5... | collective-permute-start | bytes 1376264 | tf_op jit(solution)/shard_map/ppermute | solution.py:21

commit v4 on v3

v4 whole, which is shorter than its diff:
```python
import functools

import jax
import jax.numpy as jnp
from jax import lax
from jax.experimental import pallas as pl
from jax.experimental.pallas import tpu as pltpu
from jax.sharding import PartitionSpec as P

AHEAD = 3
PAIR_VMEM = 40 * 2**20
SMALL_VMEM = 12 * 2**20
HBM = pl.BlockSpec(memory_space=pltpu.HBM)
VMEM = pl.BlockSpec(memory_space=pltpu.VMEM)
ANY = pl.BlockSpec(memory_space=pl.ANY)
FREE = pl.CostEstimate(flops=0, bytes_accessed=0, transcendentals=0)


def filler(gigaflops):
    return pl.CostEstimate(flops=int(gigaflops * 10**9), bytes_accessed=0, transcendentals=0)


PLANE_FILL = (filler(5), filler(1))
GROUP_FILL = (filler(2), filler(2))
LAST_FILL = filler(10)


def swap(array, axis, size, offset):
    return lax.ppermute(array, axis, [(i, i ^ offset) for i in range(size)])


def in_vmem(arrays):
    return [pltpu.with_memory_space_constraint(array, pltpu.VMEM) for array in arrays]


def depth_chunks(depth):
    cuts = [0]
    for size in (256, 512, 1024, 1280):
        if cuts[-1] + size < depth:
            cuts.append(cuts[-1] + size)
    while depth - cuts[-1] > 2048:
        cuts.append(cuts[-1] + 1024)
    return [(a, b - a) for a, b in zip(cuts, cuts[1:] + [depth])]


def pair_kernel(chunks, left_hbm, right_hbm, own_hbm, total, own_ref, left, right, sems, own_sem):
    copies = []
    for n, (start, size) in enumerate(chunks):
        span = pl.ds(start, size)
        pair = (
            pltpu.make_async_copy(left_hbm.at[span], left.at[span], sems.at[0, n]),
            pltpu.make_async_copy(right_hbm.at[span], right.at[span], sems.at[1, n]),
        )
        copies.append(pair)
    own_copy = pltpu.make_async_copy(own_hbm, own_ref, own_sem)
    copies.append((own_copy,))
    for copy in [copy for pair in copies[:AHEAD] for copy in pair]:
        copy.start()
    for n, (start, size) in enumerate(chunks):
        for copy in copies[n]:
            copy.wait()
        for copy in [copy for pair in copies[n + AHEAD : n + AHEAD + 1] for copy in pair]:
            copy.start()
        span = pl.ds(start, size)
        term = lax.dot_general(
            left[span], right[span], (((0,), (0,)), ((), ())), preferred_element_type=jnp.float32
        )
        if n == 0:
            total[...] = term
        else:
            total[...] += term
    own_copy.wait()


def pair_product(left, right, own):
    depth, full = left.shape
    chunks = depth_chunks(depth)
    return pl.pallas_call(
        functools.partial(pair_kernel, chunks),
        out_shape=[pltpu.VMEM((full, full), jnp.float32), pltpu.VMEM(own.shape, own.dtype)],
        in_specs=[HBM] * 3,
        out_specs=[VMEM] * 2,
        scratch_shapes=[
            pltpu.VMEM((depth, full), left.dtype),
            pltpu.VMEM((depth, full), right.dtype),
            pltpu.SemaphoreType.DMA((2, len(chunks))),
            pltpu.SemaphoreType.DMA,
        ],
        compiler_params=pltpu.CompilerParams(vmem_limit_bytes=PAIR_VMEM),
        cost_estimate=pl.CostEstimate(
            flops=2 * depth * full * full, bytes_accessed=4 * depth * full, transcendentals=0
        ),
    )(*[pltpu.with_memory_space_constraint(side, pltpu.HBM) for side in (left, right, own)])


def cut_kernel(rows, parity, total, *outs):
    me = lax.axis_index("virt")
    chips = outs[0].shape[0]
    for mine in range(2 * chips):

        @pl.when(me == mine)
        def _():
            core = (mine & 1) ^ parity
            for side, out in enumerate(outs):
                for k in range(chips):
                    chip = (mine >> 1) ^ k
                    first = (2 * chip + (side ^ core)) * rows
                    pieces = []
                    for a in (first, first + rows // 2):
                        for offset in range(chips):
                            b = (2 * (chip ^ offset) + core) * rows
                            pieces.append(total[a : a + rows // 2, b : b + rows])
                    out[k] = jnp.concatenate(pieces, axis=1).astype(out.dtype)


def cut(total, rows, parity, kind):
    full = total.shape[0]
    chips = full // rows // 2
    return pl.pallas_call(
        functools.partial(cut_kernel, rows, parity),
        out_shape=[pltpu.VMEM((chips, rows // 2, full), kind)] * 2,
        in_specs=[VMEM],
        out_specs=[VMEM] * 2,
        compiler_params=pltpu.CompilerParams(vmem_limit_bytes=SMALL_VMEM),
        cost_estimate=FREE,
    )(*in_vmem([total]))


def merge_kernel(sent, rest, count, term, other, *refs):
    narrow, wide = refs[count:]
    for places, out in ((sent, narrow), (rest, wide)):
        for n, k in enumerate(places):
            out[n] = (term[k] + other[k].astype(jnp.float32)).astype(out.dtype)


def merge(term, other, sent, rest, after, cost):
    shape = term.shape[1:]
    return pl.pallas_call(
        functools.partial(merge_kernel, sent, rest, len(after)),
        out_shape=[
            pltpu.VMEM((len(sent), *shape), jnp.bfloat16),
            pltpu.VMEM((len(rest), *shape), jnp.float32),
        ],
        in_specs=[VMEM] * 2 + [ANY] * len(after),
        out_specs=[VMEM] * 2,
        compiler_params=pltpu.CompilerParams(vmem_limit_bytes=SMALL_VMEM),
        cost_estimate=cost,
    )(*in_vmem([term, other]), *after)


def low_kernel(count, vv_ref, part_ref, *refs):
    low_ref = refs[count]
    whole = vv_ref[0] + part_ref[0].astype(jnp.float32)
    half = whole.shape[1] // 2
    low_ref[...] = jnp.concatenate([whole[:, :half], whole[:, half:]], axis=0).astype(low_ref.dtype)


def low_rows(vv, part, after, cost):
    _, rows, full = vv.shape
    return pl.pallas_call(
        functools.partial(low_kernel, len(after)),
        out_shape=pltpu.VMEM((2 * rows, full // 2), jnp.bfloat16),
        in_specs=[VMEM] * 2 + [ANY] * len(after),
        out_specs=VMEM,
        compiler_params=pltpu.CompilerParams(vmem_limit_bytes=SMALL_VMEM),
        cost_estimate=cost,
    )(*in_vmem([vv, part]), *after)


def block_rows(blocks, place):
    return jnp.concatenate([blocks[n][at] for n, at in place], axis=0)


def places_of(blocks):
    arrays = {id(array): array for block in blocks for array, _ in block}
    index = {name: n for n, name in enumerate(arrays)}
    return list(arrays.values()), [[(index[id(array)], at) for array, at in block] for block in blocks]


def other_kernel(places, low_ref, *refs):
    *blocks, out_ref = refs
    for i, place in enumerate(places):
        out_ref[i] = jnp.dot(
            low_ref[...], block_rows(blocks, place), preferred_element_type=jnp.float32
        ).astype(out_ref.dtype)


def other_density(low, blocks):
    arrays, places = places_of(blocks)
    return pl.pallas_call(
        functools.partial(other_kernel, places),
        out_shape=pltpu.VMEM((len(blocks), low.shape[0], arrays[0].shape[2]), jnp.bfloat16),
        in_specs=[VMEM] * (1 + len(arrays)),
        out_specs=VMEM,
        compiler_params=pltpu.CompilerParams(vmem_limit_bytes=SMALL_VMEM),
        cost_estimate=FREE,
    )(*in_vmem([low, *arrays]))


def own_kernel(places, cuts, low_ref, *refs):
    *blocks, out_ref = refs
    blocks, arrived = blocks[: -len(cuts)], blocks[-len(cuts) :]
    for i, place in enumerate(places):
        n = max(n for n, start in enumerate(cuts) if start <= i)

        @pl.when(pl.program_id(0) == i)
        def _():
            both = jnp.dot(
                low_ref[...], block_rows(blocks, place), preferred_element_type=jnp.float32
            )
            both += arrived[n][i - cuts[n]].astype(jnp.float32)
            out_ref[0] = both.astype(out_ref.dtype)


def own_density(low, blocks, arrived):
    arrays, places = places_of(blocks)
    cuts = [sum(part.shape[0] for part in arrived[:n]) for n in range(len(arrived))]
    rows, vectors = low.shape[0], arrays[0].shape[2]
    return pl.pallas_call(
        functools.partial(own_kernel, places, cuts),
        grid=(len(blocks),),
        out_shape=jax.ShapeDtypeStruct((len(blocks), rows, vectors), jnp.bfloat16),
        in_specs=[VMEM] * (1 + len(arrays) + len(arrived)),
        out_specs=pl.BlockSpec((1, rows, vectors), lambda i: (i, 0, 0)),
        compiler_params=pltpu.CompilerParams(vmem_limit_bytes=SMALL_VMEM),
        cost_estimate=FREE,
    )(*in_vmem([low, *arrays, *arrived]))


def load_kernel(cuts, own_hbm, *refs):
    outs, sems = refs[:-1], refs[-1]
    copies = [
        pltpu.make_async_copy(own_hbm.at[pl.ds(start, size)], out, sems.at[n])
        for n, ((start, size), out) in enumerate(zip(cuts, outs))
    ]
    for copy in copies:
        copy.start()
    for copy in copies:
        copy.wait()


def load(own, cuts):
    return pl.pallas_call(
        functools.partial(load_kernel, cuts),
        out_shape=[pltpu.VMEM((size, *own.shape[1:]), own.dtype) for _, size in cuts],
        in_specs=[HBM],
        out_specs=[VMEM] * len(cuts),
        scratch_shapes=[pltpu.SemaphoreType.DMA((len(cuts),))],
        compiler_params=pltpu.CompilerParams(vmem_limit_bytes=SMALL_VMEM),
        cost_estimate=FREE,
    )(pltpu.with_memory_space_constraint(own, pltpu.HBM))


def lay(*arrays):
    return [(array, at) for array in arrays for at in range(array.shape[0])]


def pick(places):
    runs = []
    for array, at in places:
        if runs and runs[-1][0] is array and runs[-1][2] == at:
            runs[-1][2] = at + 1
        else:
            runs.append([array, at, at + 1])
    pieces = [array[start:stop] for array, start, stop in runs]
    return pieces[0] if len(pieces) == 1 else jnp.concatenate(pieces, axis=0)


def permuted(count, groups, lambda_amps, t2_amps, chol_ov):
    rows, full = chol_ov.shape[2], lambda_amps.shape[2]
    own = jnp.transpose(chol_ov, (1, 2, 0))
    occ = own.shape[0]
    half = occ // 2
    bits = [k for k in range(2, count) if k & (k - 1) == 0]
    even = range(0, count, 2)
    early = occ - occ // 4
    first = {k: (0, occ) if k == 2 else (0, early) for k in bits}
    pieces = sorted({cut for cut in first.values() if cut[1] < occ})
    loaded = dict(zip(pieces, load(own, pieces))) if pieces else {}
    came = {k: swap(loaded.get(first[k], own), "virt", count, k) for k in bits}

    product, own = pair_product(lambda_amps.reshape(-1, full), t2_amps.reshape(-1, full), own)
    other = [swap(part, "virt", count, 1) for part in cut(product, rows, 1, jnp.bfloat16)]
    vv = list(cut(product, rows, 0, jnp.float32))
    narrow = [None, None]
    for step in range(len(bits) + 1):
        for side in (1, 0):
            held = range(vv[side].shape[0])
            if step < len(bits):
                bit = (bits[::-1] if side else bits)[step]
                place = len(held) // 2 if side else 1
                sent = [k for k in held if k & place]
                rest = [k for k in held if not k & place]
            else:
                sent = rest = [0]
            after = list(came.values()) if (step, side) == (1, 1) else []
            cost = PLANE_FILL[side] if step == len(bits) else FREE
            narrow[side], vv[side] = merge(vv[side], other[side], sent, rest, after, cost)
            if step < len(bits):
                other[side] = swap(narrow[side], "virt", count, bit)

    held = {0: lay(own)}
    for k in bits:
        start, size = first[k]
        parts = [came[k]]
        if start:
            parts.insert(0, swap(own[:start], "virt", count, k))
        if start + size < occ:
            parts.append(swap(own[start + size :], "virt", count, k))
        held[k] = lay(*parts)
    for k in sorted(set(even) - set(held), key=lambda k: (bin(k).count("1"), k)):
        low_bit, high_bit = k & -k, 1 << (k.bit_length() - 1)
        lower = pick(held[k ^ low_bit][:half])
        upper = pick(held[k ^ high_bit][half:])
        held[k] = lay(swap(lower, "virt", count, low_bit), swap(upper, "virt", count, high_bit))
    blocks = [[held[k][i] for k in even] for i in range(occ)]

    step = 1
    while step < groups:
        part = {side: swap(narrow[side], "pair", groups, step) for side in (1, 0)}
        after = [narrow[0]]
        if 2 * step < groups:
            narrow[1], vv[1] = merge(vv[1], part[1], [0], [0], after, GROUP_FILL[1])
            narrow[0], vv[0] = merge(vv[0], part[0], [0], [0], [], GROUP_FILL[0])
        step *= 2
    low = {1: low_rows(vv[1], part[1], after, FREE), 0: low_rows(vv[0], part[0], [], LAST_FILL)}
    arrived = [
        swap(other_density(low[1], part), "virt", count, 1) for part in (blocks[:half], blocks[half:])
    ]
    return jnp.transpose(own_density(low[0], blocks, arrived), (2, 0, 1))


def gathered(lambda_amps, t2_amps, chol_ov):
    vv = lax.dot_general(
        lambda_amps, t2_amps, (((0, 1), (0, 1)), ((), ())), preferred_element_type=jnp.float32
    )
    vv = lax.psum_scatter(vv, "virt", scatter_dimension=0, tiled=True)
    low = lax.psum(vv, "pair").astype(jnp.bfloat16)
    blocks = lax.all_gather(jnp.transpose(chol_ov, (1, 2, 0)), "virt", axis=1, tiled=True)
    density = jnp.einsum("ab,ibq->iaq", low, blocks, preferred_element_type=jnp.float32)
    return jnp.transpose(density, (2, 0, 1)).astype(jnp.bfloat16)


def solution(mesh):
    count, groups = mesh.shape["virt"], mesh.shape["pair"]
    paired = count & (count - 1) == 0 and groups & (groups - 1) == 0 and count > 3 and groups > 1

    def shards(lambda_amps, t2_amps, chol_ov):
        if paired and chol_ov.shape[2] % 16 == 0 and chol_ov.shape[1] > 1:
            return permuted(count, groups, lambda_amps, t2_amps, chol_ov)
        return gathered(lambda_amps, t2_amps, chol_ov)

    placed = (P("pair", "virt", None), P("pair", "virt", None), P("pair", None, "virt"))
    return jax.shard_map(
        shards, mesh=mesh, in_specs=placed, out_specs=P("pair", None, "virt"), check_vma=False
    )
```

time: 53.8 us -> 51.7 us (0.961)
  waiting for transfers between devices: 21.8 us -> 12.4 us
  starting transfers between devices: 15.9 us -> 21.7 us
  Pallas kernels: 15.7 us -> 17.2 us
    ppermute x15 -> x17, waiting for transfers between devices: 21.8 us -> 12.4 us  [swap(): return lax.ppermute(array, axis, [(i, i ^ offset) for i in range(size)])]
    ppermute x15 -> x17, starting transfers between devices: 15.9 us -> 21.7 us  [swap(): return lax.ppermute(array, axis, [(i, i ^ offset) for i in range(size)])]
    pallas_call x9 -> x14, Pallas kernels: 3.37 us -> 4.88 us  [the longest x1 2.34 us: own_density(): pl.pallas_call(functools.partial(own_kernel, places, cuts), grid=(len(blo...]
  transfers between devices with their start and end apart: 15 -> 17, of which waited for: 8 -> 8; matrix products, arithmetic and copies ran while one was open for 0% -> 0% of each run, Pallas kernels for 28% -> 29%
where the time goes in v4:
time: 51.7 us; the launch traced here: 51.5 us
  starting transfers between devices  21.7 us (42%)
  Pallas kernels  17.2 us (33%)
  waiting for transfers between devices  12.4 us (24%)
    ppermute x17, starting transfers between devices, swap(): return lax.ppermute(array, axis, [(i, i ^ offset) for i in range(size)])  21.7 us
    ppermute x17, waiting for transfers between devices, swap(): return lax.ppermute(array, axis, [(i, i ^ offset) for i in range(size)])  12.4 us
    pallas_call x1, Pallas kernels, pair_product(): pl.pallas_call(functools.partial(pair_kernel, chunks), out_shape=[pltpu.V...  10.8 us
    pallas_call x1, Pallas kernels, own_density(): pl.pallas_call(functools.partial(own_kernel, places, cuts), grid=(len(blo...  2.34 us
    pallas_call x2, Pallas kernels, cut(): pl.pallas_call(functools.partial(cut_kernel, rows, parity), out_shape=[pl...  1.48 us
    pallas_call x1, Pallas kernels, load(): pl.pallas_call(functools.partial(load_kernel, cuts), out_shape=[pltpu.VME...  1.14 us
  transfers between devices with their start and end apart: 17, of which 8 were waited for; matrix products, arithmetic and copies ran while one was open for 0% of the time, Pallas kernels for 29%

profile of v4, /device:TPU:0, one launch (start us, length us, event | category | flops | bytes accessed | tf_op | source)
XLA Modules:
  0.0 51.5 jit_solution(17045838525602463491)
XLA Ops:
  0.0 2.9 %collective-permute-start.5 = (bf16[4,112,1024]{2,1,0:T(8,128)(2,1)}, bf16[4,112,1024]{2,1,0:T(8,128)(2,1)S(1)}, u32[]{:S(2)}, u32[]{:S(2)}) collective-permute-start(bf16[4,112,1024]{2,1,0:T(8,128)(2,1)} %bitcast.4), channel_id=1, source_target_pairs={{0,8},{4,12},{8,0},{12,4},{16,24},{20,28},{24,16},{28,20},{1,9},{5... | collective-permute-start | bytes 2752520 | tf_op jit(solution)/shard_map/ppermute | solution.py:29
  2.9 1.1 %shard_map.45 = bf16[3,112,1024]{2,1,0:T(8,128)(2,1)S(1)} custom-call(bf16[4,112,1024]{2,1,0:T(8,128)(2,1)} %bitcast.5), custom_call_target="tpu_custom_call" | custom-call | tf_op jit(solution)/shard_map/pallas_call | solution.py:243
  4.1 1.6 %collective-permute-start.6 = (bf16[3,112,1024]{2,1,0:T(8,128)(2,1)S(1)}, bf16[3,112,1024]{2,1,0:T(8,128)(2,1)S(1)}, u32[]{:S(2)}, u32[]{:S(2)}) collective-permute-start(bf16[3,112,1024]{2,1,0:T(8,128)(2,1)S(1)} %shard_map.45), channel_id=1, source_target_pairs={{0,16},{4,20},{8,24},{12,28},{16,0},{20,4},{24,8},{28,12},{1,17},{... | collective-permute-start | bytes 2064392 | tf_op jit(solution)/shard_map/ppermute | solution.py:29
  5.7 10.8 %shard_map.37 = (f32[896,896]{1,0:T(8,128)S(1)}, bf16[4,112,1024]{2,1,0:T(8,128)(2,1)S(1)}) custom-call(bf16[4480,896]{1,0:T(8,128)(2,1)} %bitcast.7, bf16[4480,896]{1,0:T(8,128)(2,1)} %bitcast.8, bf16[4,112,1024]{2,1,0:T(8,128)(2,1)} %bitcast.6), custom_call_target="tpu_custom_call" | custom-call | flops 7193231360 | bytes 16056320 | tf_op jit(solution)/shard_map/pallas_call | solution.py:78
  16.5 0.5 shard_map.39
  17.0 0.1 collective-permute-start.10
  17.1 0.5 collective-permute-start
  17.6 1.0 %shard_map.38 = (f32[4,56,896]{2,1,0:T(8,128)S(1)}, f32[4,56,896]{2,1,0:T(8,128)S(1)}) custom-call(f32[896,896]{1,0:T(8,128)S(1)} %get-tuple-element.27.total), custom_call_target="tpu_custom_call" | custom-call | tf_op jit(solution)/shard_map/pallas_call | solution.py:119
  18.6 0.2 collective-permute-done.10.other
  18.8 0.1 shard_map.46
  18.9 0.6 %collective-permute-start.11 = (bf16[2,56,896]{2,1,0:T(8,128)(2,1)S(1)}, bf16[2,56,896]{2,1,0:T(8,128)(2,1)S(1)}, u32[]{:S(2)}, u32[]{:S(2)}) collective-permute-start(bf16[2,56,896]{2,1,0:T(8,128)(2,1)S(1)} %get-tuple-element.42), channel_id=1, source_target_pairs={{0,16},{4,20},{8,24},{12,28},{16,0},{20,4},{24,8},{28,12},{1,17},{... | collective-permute-start | bytes 602120 | tf_op jit(solution)/shard_map/ppermute | solution.py:29
  19.5 0.0 collective-permute-done.other
  19.5 0.1 shard_map.40
  19.5 0.5 collective-permute-start.1
  20.0 5.9 %collective-permute-done.11.other = bf16[2,56,896]{2,1,0:T(8,128)(2,1)S(1)} collective-permute-done((bf16[2,56,896]{2,1,0:T(8,128)(2,1)S(1)}, bf16[2,56,896]{2,1,0:T(8,128)(2,1)S(1)}, u32[]{:S(2)}, u32[]{:S(2)}) %collective-permute-start.11) | collective-permute-done | bytes 200736 | tf_op jit(solution)/shard_map/ppermute | solution.py:29
  26.0 0.0 collective-permute-done.6.refs_1_.refs_2_
  26.0 0.0 collective-permute-done.5.refs_0_.refs_1_
  26.1 0.6 %collective-permute-start.12 = (bf16[1,56,896]{2,1,0:T(8,128)(2,1)S(1)}, bf16[1,56,896]{2,1,0:T(8,128)(2,1)S(1)}, u32[]{:S(2)}, u32[]{:S(2)}) collective-permute-start(bf16[1,56,896]{2,1,0:T(8,128)(2,1)S(1)} %get-tuple-element.44), channel_id=1, source_target_pairs={{0,8},{4,12},{8,0},{12,4},{16,24},{20,28},{24,16},{28,20},{1,9},{5... | collective-permute-start | bytes 301064 | tf_op jit(solution)/shard_map/ppermute | solution.py:29
  26.6 1.3 %collective-permute-done.1.other = bf16[2,56,896]{2,1,0:T(8,128)(2,1)S(1)} collective-permute-done((bf16[2,56,896]{2,1,0:T(8,128)(2,1)S(1)}, bf16[2,56,896]{2,1,0:T(8,128)(2,1)S(1)}, u32[]{:S(2)}, u32[]{:S(2)}) %collective-permute-start.1) | collective-permute-done | bytes 200736 | tf_op jit(solution)/shard_map/ppermute | solution.py:29
  28.0 1.9 %collective-permute-start.2 = (bf16[1,56,896]{2,1,0:T(8,128)(2,1)S(1)}, bf16[1,56,896]{2,1,0:T(8,128)(2,1)S(1)}, u32[]{:S(2)}, u32[]{:S(2)}) collective-permute-start(bf16[1,56,896]{2,1,0:T(8,128)(2,1)S(1)} %get-tuple-element.33), channel_id=1, source_target_pairs={{0,16},{4,20},{8,24},{12,28},{16,0},{20,4},{24,8},{28,12},{1,17},{... | collective-permute-start | bytes 301064 | tf_op jit(solution)/shard_map/ppermute | solution.py:29
  29.9 0.3 collective-permute-start.9
  30.3 2.5 %collective-permute-start.7 = (bf16[2,112,1024]{2,1,0:T(8,128)(2,1)S(1)}, bf16[2,112,1024]{2,1,0:T(8,128)(2,1)S(1)}, u32[]{:S(2)}, u32[]{:S(2)}) collective-permute-start(bf16[2,112,1024]{2,1,0:T(8,128)(2,1)S(1)} %slice.12), channel_id=1, source_target_pairs={{0,8},{4,12},{8,0},{12,4},{16,24},{20,28},{24,16},{28,20},{1,9},{5... | collective-permute-start | bytes 1376264 | tf_op jit(solution)/shard_map/ppermute | solution.py:29
  32.8 0.0 collective-permute-done.12.other
  32.8 1.6 %collective-permute-start.13 = (bf16[1,56,896]{2,1,0:T(8,128)(2,1)S(1)}, bf16[1,56,896]{2,1,0:T(8,128)(2,1)S(1)}, u32[]{:S(2)}, u32[]{:S(2)}) collective-permute-start(bf16[1,56,896]{2,1,0:T(8,128)(2,1)S(1)} %get-tuple-element.46), channel_id=1, source_target_pairs={{0,1},{1,0},{2,3},{3,2},{4,5},{5,4},{6,7},{7,6},{8,9},{9,8},{10,11... | collective-permute-start | bytes 301064 | tf_op jit(solution)/shard_map/ppermute | solution.py:29
  34.5 0.0 collective-permute-done.2.other
  34.5 1.0 %collective-permute-start.3 = (bf16[1,56,896]{2,1,0:T(8,128)(2,1)S(1)}, bf16[1,56,896]{2,1,0:T(8,128)(2,1)S(1)}, u32[]{:S(2)}, u32[]{:S(2)}) collective-permute-start(bf16[1,56,896]{2,1,0:T(8,128)(2,1)S(1)} %get-tuple-element.35.refs_0_), channel_id=1, source_target_pairs={{0,1},{1,0},{2,3},{3,2},{4,5},{5,4},{6,7},{7,6},{8,9},{9,8},{10,11... | collective-permute-start | bytes 301064 | tf_op jit(solution)/shard_map/ppermute | solution.py:29
  35.5 1.9 %collective-permute-start.8 = (bf16[2,112,1024]{2,1,0:T(8,128)(2,1)S(1)}, bf16[2,112,1024]{2,1,0:T(8,128)(2,1)S(1)}, u32[]{:S(2)}, u32[]{:S(2)}) collective-permute-start(bf16[2,112,1024]{2,1,0:T(8,128)(2,1)S(1)} %slice.13), channel_id=1, source_target_pairs={{0,16},{4,20},{8,24},{12,28},{16,0},{20,4},{24,8},{28,12},{1,17},{... | collective-permute-start | bytes 1376264 | tf_op jit(solution)/shard_map/ppermute | solution.py:29
  37.5 0.1 collective-permute-done.13.other
  37.6 3.7 %collective-permute-start.14 = (bf16[1,56,896]{2,1,0:T(8,128)(2,1)S(1)}, bf16[1,56,896]{2,1,0:T(8,128)(2,1)S(1)}, u32[]{:S(2)}, u32[]{:S(2)}) collective-permute-start(bf16[1,56,896]{2,1,0:T(8,128)(2,1)S(1)} %get-tuple-element.48), channel_id=1, source_target_pairs={{0,2},{1,3},{2,0},{3,1},{4,6},{5,7},{6,4},{7,5},{8,10},{9,11},{10,... | collective-permute-start | bytes 301064 | tf_op jit(solution)/shard_map/ppermute | solution.py:29
  41.3 0.0 collective-permute-done.3.other
  41.3 1.8 %collective-permute-start.4 = (bf16[1,56,896]{2,1,0:T(8,128)(2,1)S(1)}, bf16[1,56,896]{2,1,0:T(8,128)(2,1)S(1)}, u32[]{:S(2)}, u32[]{:S(2)}) collective-permute-start(bf16[1,56,896]{2,1,0:T(8,128)(2,1)S(1)} %get-tuple-element.37.refs_0_), channel_id=1, source_target_pairs={{0,2},{1,3},{2,0},{3,1},{4,6},{5,7},{6,4},{7,5},{8,10},{9,11},{10,... | collective-permute-start | bytes 301064 | tf_op jit(solution)/shard_map/ppermute | solution.py:29
  43.1 1.9 %collective-permute-done.14.part_ref = bf16[1,56,896]{2,1,0:T(8,128)(2,1)S(1)} collective-permute-done((bf16[1,56,896]{2,1,0:T(8,128)(2,1)S(1)}, bf16[1,56,896]{2,1,0:T(8,128)(2,1)S(1)}, u32[]{:S(2)}, u32[]{:S(2)}) %collective-permute-start.14) | collective-permute-done | bytes 100384 | tf_op jit(solution)/shard_map/ppermute | solution.py:29
  45.0 0.1 shard_map.50.low_ref
  45.1 0.0 collective-permute-done.7.refs_3_
  45.1 0.4 shard_map.51
  45.5 0.1 collective-permute-start.15
  45.6 0.0 collective-permute-done.9.refs_4_.refs_5_
  45.6 1.3 %collective-permute-done.8.refs_3_.refs_4_ = bf16[2,112,1024]{2,1,0:T(8,128)(2,1)S(1)} collective-permute-done((bf16[2,112,1024]{2,1,0:T(8,128)(2,1)S(1)}, bf16[2,112,1024]{2,1,0:T(8,128)(2,1)S(1)}, u32[]{:S(2)}, u32[]{:S(2)}) %collective-permute-start.8) | collective-permute-done | bytes 458784 | tf_op jit(solution)/shard_map/ppermute | solution.py:29
  46.9 0.4 shard_map.52
  47.3 0.1 collective-permute-start.16
  47.4 0.6 %collective-permute-done.4.part_ref = bf16[1,56,896]{2,1,0:T(8,128)(2,1)S(1)} collective-permute-done((bf16[1,56,896]{2,1,0:T(8,128)(2,1)S(1)}, bf16[1,56,896]{2,1,0:T(8,128)(2,1)S(1)}, u32[]{:S(2)}, u32[]{:S(2)}) %collective-permute-start.4) | collective-permute-done | bytes 100384 | tf_op jit(solution)/shard_map/ppermute | solution.py:29
  48.0 0.1 shard_map.44.low_ref
  48.1 0.0 collective-permute-done.15.refs_6_
  48.1 1.1 %collective-permute-done.16.refs_7_ = bf16[2,112,1024]{2,1,0:T(8,128)(2,1)S(1)} collective-permute-done((bf16[2,112,1024]{2,1,0:T(8,128)(2,1)S(1)}, bf16[2,112,1024]{2,1,0:T(8,128)(2,1)S(1)}, u32[]{:S(2)}, u32[]{:S(2)}) %collective-permute-start.16) | collective-permute-done | bytes 458784 | tf_op jit(solution)/shard_map/ppermute | solution.py:29
  49.2 2.3 %shard_map.53 = bf16[4,112,1024]{2,1,0:T(8,128)(2,1)} custom-call(bf16[112,448]{1,0:T(8,128)(2,1)S(1)} %shard_map.44.low_ref, bf16[4,112,1024]{2,1,0:T(8,128)(2,1)S(1)} %get-tuple-element.38.refs_0_, bf16[4,112,1024]{2,1,0:T(8,128)(2,1)S(1)} %collective-permute-done.5.refs_0_.refs_1_, bf16[3,112,1024]{2,1,0:T(8,128)(2,1)S(1)} %collective-permute-done.6.refs_1_.refs_2_, ...), custom_call_target="tpu_custom_call" | custom-call | tf_op jit(solution)/shard_map/pallas_call | solution.py:219
  (9 shorter events, 0.3 us)
Async XLA Ops:
  0.0 26.0 %collective-permute-start.5 = (bf16[4,112,1024]{2,1,0:T(8,128)(2,1)}, bf16[4,112,1024]{2,1,0:T(8,128)(2,1)S(1)}, u32[]{:S(2)}, u32[]{:S(2)}) collective-permute-start(bf16[4,112,1024]{2,1,0:T(8,128)(2,1)} %bitcast.4), channel_id=1, source_target_pairs={{0,8},{4,12},{8,0},{12,4},{16,24},{20,28},{24,16},{28,20},{1,9},{5... | collective-permute-start | bytes 2752520 | tf_op jit(solution)/shard_map/ppermute | solution.py:29
  4.1 21.9 %collective-permute-start.6 = (bf16[3,112,1024]{2,1,0:T(8,128)(2,1)S(1)}, bf16[3,112,1024]{2,1,0:T(8,128)(2,1)S(1)}, u32[]{:S(2)}, u32[]{:S(2)}) collective-permute-start(bf16[3,112,1024]{2,1,0:T(8,128)(2,1)S(1)} %shard_map.45), channel_id=1, source_target_pairs={{0,16},{4,20},{8,24},{12,28},{16,0},{20,4},{24,8},{28,12},{1,17},{... | collective-permute-start | bytes 2064392 | tf_op jit(solution)/shard_map/ppermute | solution.py:29
  17.0 1.8 %collective-permute-start.10 = (bf16[4,56,896]{2,1,0:T(8,128)(2,1)S(1)}, bf16[4,56,896]{2,1,0:T(8,128)(2,1)S(1)}, u32[]{:S(2)}, u32[]{:S(2)}) collective-permute-start(bf16[4,56,896]{2,1,0:T(8,128)(2,1)S(1)} %get-tuple-element.40), channel_id=1, source_target_pairs={{0,4},{4,0},{8,12},{12,8},{16,20},{20,16},{24,28},{28,24},{1,5},{5... | collective-permute-start | bytes 1204232 | tf_op jit(solution)/shard_map/ppermute | solution.py:29
  17.1 2.4 %collective-permute-start = (bf16[4,56,896]{2,1,0:T(8,128)(2,1)S(1)}, bf16[4,56,896]{2,1,0:T(8,128)(2,1)S(1)}, u32[]{:S(2)}, u32[]{:S(2)}) collective-permute-start(bf16[4,56,896]{2,1,0:T(8,128)(2,1)S(1)} %get-tuple-element.29), channel_id=1, source_target_pairs={{0,4},{4,0},{8,12},{12,8},{16,20},{20,16},{24,28},{28,24},{1,5},{5... | collective-permute-start | bytes 1204232 | tf_op jit(solution)/shard_map/ppermute | solution.py:29
  18.9 7.1 %collective-permute-start.11 = (bf16[2,56,896]{2,1,0:T(8,128)(2,1)S(1)}, bf16[2,56,896]{2,1,0:T(8,128)(2,1)S(1)}, u32[]{:S(2)}, u32[]{:S(2)}) collective-permute-start(bf16[2,56,896]{2,1,0:T(8,128)(2,1)S(1)} %get-tuple-element.42), channel_id=1, source_target_pairs={{0,16},{4,20},{8,24},{12,28},{16,0},{20,4},{24,8},{28,12},{1,17},{... | collective-permute-start | bytes 602120 | tf_op jit(solution)/shard_map/ppermute | solution.py:29
  19.5 8.4 %collective-permute-start.1 = (bf16[2,56,896]{2,1,0:T(8,128)(2,1)S(1)}, bf16[2,56,896]{2,1,0:T(8,128)(2,1)S(1)}, u32[]{:S(2)}, u32[]{:S(2)}) collective-permute-start(bf16[2,56,896]{2,1,0:T(8,128)(2,1)S(1)} %get-tuple-element.31), channel_id=1, source_target_pairs={{0,8},{4,12},{8,0},{12,4},{16,24},{20,28},{24,16},{28,20},{1,9},{5... | collective-permute-start | bytes 602120 | tf_op jit(solution)/shard_map/ppermute | solution.py:29
  26.1 6.7 %collective-permute-start.12 = (bf16[1,56,896]{2,1,0:T(8,128)(2,1)S(1)}, bf16[1,56,896]{2,1,0:T(8,128)(2,1)S(1)}, u32[]{:S(2)}, u32[]{:S(2)}) collective-permute-start(bf16[1,56,896]{2,1,0:T(8,128)(2,1)S(1)} %get-tuple-element.44), channel_id=1, source_target_pairs={{0,8},{4,12},{8,0},{12,4},{16,24},{20,28},{24,16},{28,20},{1,9},{5... | collective-permute-start | bytes 301064 | tf_op jit(solution)/shard_map/ppermute | solution.py:29
  28.0 6.4 %collective-permute-start.2 = (bf16[1,56,896]{2,1,0:T(8,128)(2,1)S(1)}, bf16[1,56,896]{2,1,0:T(8,128)(2,1)S(1)}, u32[]{:S(2)}, u32[]{:S(2)}) collective-permute-start(bf16[1,56,896]{2,1,0:T(8,128)(2,1)S(1)} %get-tuple-element.33), channel_id=1, source_target_pairs={{0,16},{4,20},{8,24},{12,28},{16,0},{20,4},{24,8},{28,12},{1,17},{... | collective-permute-start | bytes 301064 | tf_op jit(solution)/shard_map/ppermute | solution.py:29
  29.9 15.7 %collective-permute-start.9 = (bf16[1,112,1024]{2,1,0:T(8,128)(2,1)S(1)}, bf16[1,112,1024]{2,1,0:T(8,128)(2,1)S(1)}, u32[]{:S(2)}, u32[]{:S(2)}) collective-permute-start(bf16[1,112,1024]{2,1,0:T(8,128)(2,1)S(1)} %slice.11), channel_id=1, source_target_pairs={{0,16},{4,20},{8,24},{12,28},{16,0},{20,4},{24,8},{28,12},{1,17},{... | collective-permute-start | bytes 688136 | tf_op jit(solution)/shard_map/ppermute | solution.py:29
  30.3 14.8 %collective-permute-start.7 = (bf16[2,112,1024]{2,1,0:T(8,128)(2,1)S(1)}, bf16[2,112,1024]{2,1,0:T(8,128)(2,1)S(1)}, u32[]{:S(2)}, u32[]{:S(2)}) collective-permute-start(bf16[2,112,1024]{2,1,0:T(8,128)(2,1)S(1)} %slice.12), channel_id=1, source_target_pairs={{0,8},{4,12},{8,0},{12,4},{16,24},{20,28},{24,16},{28,20},{1,9},{5... | collective-permute-start | bytes 1376264 | tf_op jit(solution)/shard_map/ppermute | solution.py:29
  32.8 4.7 %collective-permute-start.13 = (bf16[1,56,896]{2,1,0:T(8,128)(2,1)S(1)}, bf16[1,56,896]{2,1,0:T(8,128)(2,1)S(1)}, u32[]{:S(2)}, u32[]{:S(2)}) collective-permute-start(bf16[1,56,896]{2,1,0:T(8,128)(2,1)S(1)} %get-tuple-element.46), channel_id=1, source_target_pairs={{0,1},{1,0},{2,3},{3,2},{4,5},{5,4},{6,7},{7,6},{8,9},{9,8},{10,11... | collective-permute-start | bytes 301064 | tf_op jit(solution)/shard_map/ppermute | solution.py:29
  34.5 6.8 %collective-permute-start.3 = (bf16[1,56,896]{2,1,0:T(8,128)(2,1)S(1)}, bf16[1,56,896]{2,1,0:T(8,128)(2,1)S(1)}, u32[]{:S(2)}, u32[]{:S(2)}) collective-permute-start(bf16[1,56,896]{2,1,0:T(8,128)(2,1)S(1)} %get-tuple-element.35.refs_0_), channel_id=1, source_target_pairs={{0,1},{1,0},{2,3},{3,2},{4,5},{5,4},{6,7},{7,6},{8,9},{9,8},{10,11... | collective-permute-start | bytes 301064 | tf_op jit(solution)/shard_map/ppermute | solution.py:29
  35.5 11.3 %collective-permute-start.8 = (bf16[2,112,1024]{2,1,0:T(8,128)(2,1)S(1)}, bf16[2,112,1024]{2,1,0:T(8,128)(2,1)S(1)}, u32[]{:S(2)}, u32[]{:S(2)}) collective-permute-start(bf16[2,112,1024]{2,1,0:T(8,128)(2,1)S(1)} %slice.13), channel_id=1, source_target_pairs={{0,16},{4,20},{8,24},{12,28},{16,0},{20,4},{24,8},{28,12},{1,17},{... | collective-permute-start | bytes 1376264 | tf_op jit(solution)/shard_map/ppermute | solution.py:29
  37.6 7.4 %collective-permute-start.14 = (bf16[1,56,896]{2,1,0:T(8,128)(2,1)S(1)}, bf16[1,56,896]{2,1,0:T(8,128)(2,1)S(1)}, u32[]{:S(2)}, u32[]{:S(2)}) collective-permute-start(bf16[1,56,896]{2,1,0:T(8,128)(2,1)S(1)} %get-tuple-element.48), channel_id=1, source_target_pairs={{0,2},{1,3},{2,0},{3,1},{4,6},{5,7},{6,4},{7,5},{8,10},{9,11},{10,... | collective-permute-start | bytes 301064 | tf_op jit(solution)/shard_map/ppermute | solution.py:29
  41.3 6.7 %collective-permute-start.4 = (bf16[1,56,896]{2,1,0:T(8,128)(2,1)S(1)}, bf16[1,56,896]{2,1,0:T(8,128)(2,1)S(1)}, u32[]{:S(2)}, u32[]{:S(2)}) collective-permute-start(bf16[1,56,896]{2,1,0:T(8,128)(2,1)S(1)} %get-tuple-element.37.refs_0_), channel_id=1, source_target_pairs={{0,2},{1,3},{2,0},{3,1},{4,6},{5,7},{6,4},{7,5},{8,10},{9,11},{10,... | collective-permute-start | bytes 301064 | tf_op jit(solution)/shard_map/ppermute | solution.py:29
  45.5 2.6 %collective-permute-start.15 = (bf16[2,112,1024]{2,1,0:T(8,128)(2,1)S(1)}, bf16[2,112,1024]{2,1,0:T(8,128)(2,1)S(1)}, u32[]{:S(2)}, u32[]{:S(2)}) collective-permute-start(bf16[2,112,1024]{2,1,0:T(8,128)(2,1)S(1)} %shard_map.51), channel_id=1, source_target_pairs={{0,4},{4,0},{8,12},{12,8},{16,20},{20,16},{24,28},{28,24},{1,5},{5... | collective-permute-start | bytes 1376264 | tf_op jit(solution)/shard_map/ppermute | solution.py:29
  47.3 1.9 %collective-permute-start.16 = (bf16[2,112,1024]{2,1,0:T(8,128)(2,1)S(1)}, bf16[2,112,1024]{2,1,0:T(8,128)(2,1)S(1)}, u32[]{:S(2)}, u32[]{:S(2)}) collective-permute-start(bf16[2,112,1024]{2,1,0:T(8,128)(2,1)S(1)} %shard_map.52), channel_id=1, source_target_pairs={{0,4},{4,0},{8,12},{12,8},{16,20},{20,16},{24,28},{28,24},{1,5},{5... | collective-permute-start | bytes 1376264 | tf_op jit(solution)/shard_map/ppermute | solution.py:29

commit v5 on v4

--- a/solution.py
+++ b/solution.py
@@ -197,34 +197,35 @@
     )(*in_vmem([low, *arrays]))
 
 
-def own_kernel(places, cuts, low_ref, *refs):
-    *blocks, out_ref = refs
-    blocks, arrived = blocks[: -len(cuts)], blocks[-len(cuts) :]
+def own_kernel(places, start, low_ref, arrived_ref, *refs):
+    out_hbm, out, sems = refs[-3:]
+    copies = []
     for i, place in enumerate(places):
-        n = max(n for n, start in enumerate(cuts) if start <= i)
-
-        @pl.when(pl.program_id(0) == i)
-        def _():
-            both = jnp.dot(
-                low_ref[...], block_rows(blocks, place), preferred_element_type=jnp.float32
-            )
-            both += arrived[n][i - cuts[n]].astype(jnp.float32)
-            out_ref[0] = both.astype(out_ref.dtype)
-
-
-def own_density(low, blocks, arrived):
+        both = jnp.dot(low_ref[...], block_rows(refs, place), preferred_element_type=jnp.float32)
+        out[i] = (both + arrived_ref[i].astype(jnp.float32)).astype(out.dtype)
+        copies.append(pltpu.make_async_copy(out.at[i], out_hbm.at[start + i], sems.at[i]))
+        copies[i].start()
+    for copy in copies:
+        copy.wait()
+
+
+def own_density(low, blocks, arrived, start, occ, base):
     arrays, places = places_of(blocks)
-    cuts = [sum(part.shape[0] for part in arrived[:n]) for n in range(len(arrived))]
     rows, vectors = low.shape[0], arrays[0].shape[2]
-    return pl.pallas_call(
-        functools.partial(own_kernel, places, cuts),
-        grid=(len(blocks),),
-        out_shape=jax.ShapeDtypeStruct((len(blocks), rows, vectors), jnp.bfloat16),
-        in_specs=[VMEM] * (1 + len(arrays) + len(arrived)),
-        out_specs=pl.BlockSpec((1, rows, vectors), lambda i: (i, 0, 0)),
+    given = [] if base is None else [base]
+    return pl.pallas_call(
+        functools.partial(own_kernel, places, start),
+        out_shape=jax.ShapeDtypeStruct((occ, rows, vectors), jnp.bfloat16),
+        in_specs=[VMEM] * (2 + len(arrays)) + [HBM] * len(given),
+        out_specs=HBM,
+        scratch_shapes=[
+            pltpu.VMEM((len(blocks), rows, vectors), jnp.bfloat16),
+            pltpu.SemaphoreType.DMA((len(blocks),)),
+        ],
+        input_output_aliases={2 + len(arrays): 0} if given else {},
         compiler_params=pltpu.CompilerParams(vmem_limit_bytes=SMALL_VMEM),
         cost_estimate=FREE,
-    )(*in_vmem([low, *arrays, *arrived]))
+    )(*in_vmem([low, arrived, *arrays]), *given)
 
 
 def load_kernel(cuts, own_hbm, *refs):
@@ -324,10 +325,12 @@
             narrow[0], vv[0] = merge(vv[0], part[0], [0], [0], [], GROUP_FILL[0])
         step *= 2
     low = {1: low_rows(vv[1], part[1], after, FREE), 0: low_rows(vv[0], part[0], [], LAST_FILL)}
-    arrived = [
-        swap(other_density(low[1], part), "virt", count, 1) for part in (blocks[:half], blocks[half:])
-    ]
-    return jnp.transpose(own_density(low[0], blocks, arrived), (2, 0, 1))
+    cuts = ((0, half), (half, occ))
+    arrived = [swap(other_density(low[1], blocks[a:b]), "virt", count, 1) for a, b in cuts]
+    density = None
+    for (a, b), part in zip(cuts, arrived):
+        density = own_density(low[0], blocks[a:b], part, a, occ, density)
+    return jnp.transpose(density, (2, 0, 1))
 
 
 def gathered(lambda_amps, t2_amps, chol_ov):

time: 51.7 us -> 50.7 us (0.981)
  waiting for transfers between devices: 12.4 us -> 11.3 us
    ppermute x17, waiting for transfers between devices: 12.4 us -> 11.3 us  [swap(): return lax.ppermute(array, axis, [(i, i ^ offset) for i in range(size)])]
    pallas_call x1 -> x2, Pallas kernels: 2.34 us -> 2.3 us  [own_density(): pl.pallas_call(functools.partial(own_kernel, places, start), out_shape=ja...]
  transfers between devices with their start and end apart: 17 -> 17, of which waited for: 8 -> 7; matrix products, arithmetic and copies ran while one was open for 0% -> 0% of each run, Pallas kernels for 29% -> 32%
where the time goes in v5:
time: 50.7 us; the launch traced here: 50.6 us
  starting transfers between devices  21.7 us (43%)
  Pallas kernels  17.2 us (34%)
  waiting for transfers between devices  11.3 us (22%)
    ppermute x17, starting transfers between devices, swap(): return lax.ppermute(array, axis, [(i, i ^ offset) for i in range(size)])  21.7 us
    ppermute x17, waiting for transfers between devices, swap(): return lax.ppermute(array, axis, [(i, i ^ offset) for i in range(size)])  11.3 us
    pallas_call x1, Pallas kernels, pair_product(): pl.pallas_call(functools.partial(pair_kernel, chunks), out_shape=[pltpu.V...  10.8 us
    pallas_call x2, Pallas kernels, own_density(): pl.pallas_call(functools.partial(own_kernel, places, start), out_shape=ja...  2.3 us
    pallas_call x2, Pallas kernels, cut(): pl.pallas_call(functools.partial(cut_kernel, rows, parity), out_shape=[pl...  1.48 us
    pallas_call x1, Pallas kernels, load(): pl.pallas_call(functools.partial(load_kernel, cuts), out_shape=[pltpu.VME...  1.14 us
  transfers between devices with their start and end apart: 17, of which 7 were waited for; matrix products, arithmetic and copies ran while one was open for 0% of the time, Pallas kernels for 32%

profile of v5, /device:TPU:0, one launch (start us, length us, event | category | flops | bytes accessed | tf_op | source)
XLA Modules:
  0.0 50.6 jit_solution(9533472220179400755)
XLA Ops:
  0.0 2.9 %collective-permute-start.7 = (bf16[4,112,1024]{2,1,0:T(8,128)(2,1)}, bf16[4,112,1024]{2,1,0:T(8,128)(2,1)S(1)}, u32[]{:S(2)}, u32[]{:S(2)}) collective-permute-start(bf16[4,112,1024]{2,1,0:T(8,128)(2,1)} %bitcast.4), channel_id=1, source_target_pairs={{0,8},{4,12},{8,0},{12,4},{16,24},{20,28},{24,16},{28,20},{1,9},{5... | collective-permute-start | bytes 2752520 | tf_op jit(solution)/shard_map/ppermute | solution.py:29
  2.9 1.1 %shard_map.46 = bf16[3,112,1024]{2,1,0:T(8,128)(2,1)S(1)} custom-call(bf16[4,112,1024]{2,1,0:T(8,128)(2,1)} %bitcast.5), custom_call_target="tpu_custom_call" | custom-call | tf_op jit(solution)/shard_map/pallas_call | solution.py:244
  4.1 1.6 %collective-permute-start.8 = (bf16[3,112,1024]{2,1,0:T(8,128)(2,1)S(1)}, bf16[3,112,1024]{2,1,0:T(8,128)(2,1)S(1)}, u32[]{:S(2)}, u32[]{:S(2)}) collective-permute-start(bf16[3,112,1024]{2,1,0:T(8,128)(2,1)S(1)} %shard_map.46), channel_id=1, source_target_pairs={{0,16},{4,20},{8,24},{12,28},{16,0},{20,4},{24,8},{28,12},{1,17},{... | collective-permute-start | bytes 2064392 | tf_op jit(solution)/shard_map/ppermute | solution.py:29
  5.7 10.8 %shard_map.37 = (f32[896,896]{1,0:T(8,128)S(1)}, bf16[4,112,1024]{2,1,0:T(8,128)(2,1)S(1)}) custom-call(bf16[4480,896]{1,0:T(8,128)(2,1)} %bitcast.7, bf16[4480,896]{1,0:T(8,128)(2,1)} %bitcast.8, bf16[4,112,1024]{2,1,0:T(8,128)(2,1)} %bitcast.6), custom_call_target="tpu_custom_call" | custom-call | flops 7193231360 | bytes 16056320 | tf_op jit(solution)/shard_map/pallas_call | solution.py:78
  16.5 0.5 shard_map.39
  17.0 0.1 collective-permute-start.5
  17.1 0.5 collective-permute-start
  17.6 1.0 %shard_map.38 = (f32[4,56,896]{2,1,0:T(8,128)S(1)}, f32[4,56,896]{2,1,0:T(8,128)S(1)}) custom-call(f32[896,896]{1,0:T(8,128)S(1)} %get-tuple-element.27.total), custom_call_target="tpu_custom_call" | custom-call | tf_op jit(solution)/shard_map/pallas_call | solution.py:119
  18.6 0.2 collective-permute-done.5.other
  18.8 0.1 shard_map.45
  18.9 0.6 %collective-permute-start.6 = (bf16[2,56,896]{2,1,0:T(8,128)(2,1)S(1)}, bf16[2,56,896]{2,1,0:T(8,128)(2,1)S(1)}, u32[]{:S(2)}, u32[]{:S(2)}) collective-permute-start(bf16[2,56,896]{2,1,0:T(8,128)(2,1)S(1)} %get-tuple-element.41), channel_id=1, source_target_pairs={{0,16},{4,20},{8,24},{12,28},{16,0},{20,4},{24,8},{28,12},{1,17},{... | collective-permute-start | bytes 602120 | tf_op jit(solution)/shard_map/ppermute | solution.py:29
  19.5 0.0 collective-permute-done.other
  19.5 0.1 shard_map.40
  19.5 0.5 collective-permute-start.1
  20.0 5.9 %collective-permute-done.6.other = bf16[2,56,896]{2,1,0:T(8,128)(2,1)S(1)} collective-permute-done((bf16[2,56,896]{2,1,0:T(8,128)(2,1)S(1)}, bf16[2,56,896]{2,1,0:T(8,128)(2,1)S(1)}, u32[]{:S(2)}, u32[]{:S(2)}) %collective-permute-start.6) | collective-permute-done | bytes 200736 | tf_op jit(solution)/shard_map/ppermute | solution.py:29
  26.0 0.0 collective-permute-done.8.refs_1_.refs_2_
  26.0 0.0 collective-permute-done.7.refs_0_.refs_1_
  26.1 0.6 %collective-permute-start.9 = (bf16[1,56,896]{2,1,0:T(8,128)(2,1)S(1)}, bf16[1,56,896]{2,1,0:T(8,128)(2,1)S(1)}, u32[]{:S(2)}, u32[]{:S(2)}) collective-permute-start(bf16[1,56,896]{2,1,0:T(8,128)(2,1)S(1)} %get-tuple-element.43), channel_id=1, source_target_pairs={{0,8},{4,12},{8,0},{12,4},{16,24},{20,28},{24,16},{28,20},{1,9},{5... | collective-permute-start | bytes 301064 | tf_op jit(solution)/shard_map/ppermute | solution.py:29
  26.6 1.3 %collective-permute-done.1.other = bf16[2,56,896]{2,1,0:T(8,128)(2,1)S(1)} collective-permute-done((bf16[2,56,896]{2,1,0:T(8,128)(2,1)S(1)}, bf16[2,56,896]{2,1,0:T(8,128)(2,1)S(1)}, u32[]{:S(2)}, u32[]{:S(2)}) %collective-permute-start.1) | collective-permute-done | bytes 200736 | tf_op jit(solution)/shard_map/ppermute | solution.py:29
  28.0 1.9 %collective-permute-start.2 = (bf16[1,56,896]{2,1,0:T(8,128)(2,1)S(1)}, bf16[1,56,896]{2,1,0:T(8,128)(2,1)S(1)}, u32[]{:S(2)}, u32[]{:S(2)}) collective-permute-start(bf16[1,56,896]{2,1,0:T(8,128)(2,1)S(1)} %get-tuple-element.33), channel_id=1, source_target_pairs={{0,16},{4,20},{8,24},{12,28},{16,0},{20,4},{24,8},{28,12},{1,17},{... | collective-permute-start | bytes 301064 | tf_op jit(solution)/shard_map/ppermute | solution.py:29
  29.9 0.3 collective-permute-start.13
  30.3 2.5 %collective-permute-start.15 = (bf16[2,112,1024]{2,1,0:T(8,128)(2,1)S(1)}, bf16[2,112,1024]{2,1,0:T(8,128)(2,1)S(1)}, u32[]{:S(2)}, u32[]{:S(2)}) collective-permute-start(bf16[2,112,1024]{2,1,0:T(8,128)(2,1)S(1)} %slice.13), channel_id=1, source_target_pairs={{0,8},{4,12},{8,0},{12,4},{16,24},{20,28},{24,16},{28,20},{1,9},{5... | collective-permute-start | bytes 1376264 | tf_op jit(solution)/shard_map/ppermute | solution.py:29
  32.8 0.0 collective-permute-done.9.other
  32.8 1.6 %collective-permute-start.10 = (bf16[1,56,896]{2,1,0:T(8,128)(2,1)S(1)}, bf16[1,56,896]{2,1,0:T(8,128)(2,1)S(1)}, u32[]{:S(2)}, u32[]{:S(2)}) collective-permute-start(bf16[1,56,896]{2,1,0:T(8,128)(2,1)S(1)} %get-tuple-element.45), channel_id=1, source_target_pairs={{0,1},{1,0},{2,3},{3,2},{4,5},{5,4},{6,7},{7,6},{8,9},{9,8},{10,11... | collective-permute-start | bytes 301064 | tf_op jit(solution)/shard_map/ppermute | solution.py:29
  34.5 0.0 collective-permute-done.2.other
  34.5 1.0 %collective-permute-start.3 = (bf16[1,56,896]{2,1,0:T(8,128)(2,1)S(1)}, bf16[1,56,896]{2,1,0:T(8,128)(2,1)S(1)}, u32[]{:S(2)}, u32[]{:S(2)}) collective-permute-start(bf16[1,56,896]{2,1,0:T(8,128)(2,1)S(1)} %get-tuple-element.35.refs_0_), channel_id=1, source_target_pairs={{0,1},{1,0},{2,3},{3,2},{4,5},{5,4},{6,7},{7,6},{8,9},{9,8},{10,11... | collective-permute-start | bytes 301064 | tf_op jit(solution)/shard_map/ppermute | solution.py:29
  35.5 1.9 %collective-permute-start.12 = (bf16[2,112,1024]{2,1,0:T(8,128)(2,1)S(1)}, bf16[2,112,1024]{2,1,0:T(8,128)(2,1)S(1)}, u32[]{:S(2)}, u32[]{:S(2)}) collective-permute-start(bf16[2,112,1024]{2,1,0:T(8,128)(2,1)S(1)} %slice.12), channel_id=1, source_target_pairs={{0,16},{4,20},{8,24},{12,28},{16,0},{20,4},{24,8},{28,12},{1,17},{... | collective-permute-start | bytes 1376264 | tf_op jit(solution)/shard_map/ppermute | solution.py:29
  37.5 0.1 collective-permute-done.10.other
  37.6 3.7 %collective-permute-start.11 = (bf16[1,56,896]{2,1,0:T(8,128)(2,1)S(1)}, bf16[1,56,896]{2,1,0:T(8,128)(2,1)S(1)}, u32[]{:S(2)}, u32[]{:S(2)}) collective-permute-start(bf16[1,56,896]{2,1,0:T(8,128)(2,1)S(1)} %get-tuple-element.47), channel_id=1, source_target_pairs={{0,2},{1,3},{2,0},{3,1},{4,6},{5,7},{6,4},{7,5},{8,10},{9,11},{10,... | collective-permute-start | bytes 301064 | tf_op jit(solution)/shard_map/ppermute | solution.py:29
  41.3 0.0 collective-permute-done.3.other
  41.3 1.8 %collective-permute-start.4 = (bf16[1,56,896]{2,1,0:T(8,128)(2,1)S(1)}, bf16[1,56,896]{2,1,0:T(8,128)(2,1)S(1)}, u32[]{:S(2)}, u32[]{:S(2)}) collective-permute-start(bf16[1,56,896]{2,1,0:T(8,128)(2,1)S(1)} %get-tuple-element.37.refs_0_), channel_id=1, source_target_pairs={{0,2},{1,3},{2,0},{3,1},{4,6},{5,7},{6,4},{7,5},{8,10},{9,11},{10,... | collective-permute-start | bytes 301064 | tf_op jit(solution)/shard_map/ppermute | solution.py:29
  43.1 1.9 %collective-permute-done.11.part_ref = bf16[1,56,896]{2,1,0:T(8,128)(2,1)S(1)} collective-permute-done((bf16[1,56,896]{2,1,0:T(8,128)(2,1)S(1)}, bf16[1,56,896]{2,1,0:T(8,128)(2,1)S(1)}, u32[]{:S(2)}, u32[]{:S(2)}) %collective-permute-start.11) | collective-permute-done | bytes 100384 | tf_op jit(solution)/shard_map/ppermute | solution.py:29
  45.0 0.1 shard_map.50.low_ref
  45.1 0.0 collective-permute-done.15.refs_3_
  45.1 0.4 shard_map.52
  45.5 0.1 collective-permute-start.16
  45.6 0.0 collective-permute-done.13.refs_4_
  45.6 1.3 %collective-permute-done.12.refs_3_ = bf16[2,112,1024]{2,1,0:T(8,128)(2,1)S(1)} collective-permute-done((bf16[2,112,1024]{2,1,0:T(8,128)(2,1)S(1)}, bf16[2,112,1024]{2,1,0:T(8,128)(2,1)S(1)}, u32[]{:S(2)}, u32[]{:S(2)}) %collective-permute-start.12) | collective-permute-done | bytes 458784 | tf_op jit(solution)/shard_map/ppermute | solution.py:29
  46.9 0.4 shard_map.51
  47.3 0.1 collective-permute-start.14
  47.4 0.6 %collective-permute-done.4.part_ref = bf16[1,56,896]{2,1,0:T(8,128)(2,1)S(1)} collective-permute-done((bf16[1,56,896]{2,1,0:T(8,128)(2,1)S(1)}, bf16[1,56,896]{2,1,0:T(8,128)(2,1)S(1)}, u32[]{:S(2)}, u32[]{:S(2)}) %collective-permute-start.4) | collective-permute-done | bytes 100384 | tf_op jit(solution)/shard_map/ppermute | solution.py:29
  48.0 0.1 shard_map.44.low_ref
  48.1 0.0 collective-permute-done.16.arrived_ref
  48.1 1.2 %shard_map.53.refs_5_ = bf16[4,112,1024]{2,1,0:T(8,128)(2,1)} custom-call(bf16[112,448]{1,0:T(8,128)(2,1)S(1)} %shard_map.44.low_ref, bf16[2,112,1024]{2,1,0:T(8,128)(2,1)S(1)} %collective-permute-done.16.arrived_ref, bf16[4,112,1024]{2,1,0:T(8,128)(2,1)S(1)} %get-tuple-element.48.refs_0_, bf16[4,112,1024]{2,1,0:T(8,128)(2,1)S(1)} %collective-permute-done.7.refs_0_.refs_1_, ...), custom_call_target="tpu_custom_call" | custom-call | tf_op jit(solution)/shard_map/pallas_call | solution.py:216
  49.3 0.0 collective-permute-done.14.arrived_ref
  49.3 1.2 %shard_map.54 = bf16[4,112,1024]{2,1,0:T(8,128)(2,1)} custom-call(bf16[112,448]{1,0:T(8,128)(2,1)S(1)} %shard_map.44.low_ref, bf16[2,112,1024]{2,1,0:T(8,128)(2,1)S(1)} %collective-permute-done.14.arrived_ref, bf16[4,112,1024]{2,1,0:T(8,128)(2,1)S(1)} %get-tuple-element.48.refs_0_, ...), custom_call_target="tpu_custom_call", output_to_operand_aliasing={{}: (7, {})} | custom-call | tf_op jit(solution)/shard_map/pallas_call | solution.py:216
  (9 shorter events, 0.3 us)
Async XLA Ops:
  0.0 26.0 %collective-permute-start.7 = (bf16[4,112,1024]{2,1,0:T(8,128)(2,1)}, bf16[4,112,1024]{2,1,0:T(8,128)(2,1)S(1)}, u32[]{:S(2)}, u32[]{:S(2)}) collective-permute-start(bf16[4,112,1024]{2,1,0:T(8,128)(2,1)} %bitcast.4), channel_id=1, source_target_pairs={{0,8},{4,12},{8,0},{12,4},{16,24},{20,28},{24,16},{28,20},{1,9},{5... | collective-permute-start | bytes 2752520 | tf_op jit(solution)/shard_map/ppermute | solution.py:29
  4.1 21.9 %collective-permute-start.8 = (bf16[3,112,1024]{2,1,0:T(8,128)(2,1)S(1)}, bf16[3,112,1024]{2,1,0:T(8,128)(2,1)S(1)}, u32[]{:S(2)}, u32[]{:S(2)}) collective-permute-start(bf16[3,112,1024]{2,1,0:T(8,128)(2,1)S(1)} %shard_map.46), channel_id=1, source_target_pairs={{0,16},{4,20},{8,24},{12,28},{16,0},{20,4},{24,8},{28,12},{1,17},{... | collective-permute-start | bytes 2064392 | tf_op jit(solution)/shard_map/ppermute | solution.py:29
  17.0 1.8 %collective-permute-start.5 = (bf16[4,56,896]{2,1,0:T(8,128)(2,1)S(1)}, bf16[4,56,896]{2,1,0:T(8,128)(2,1)S(1)}, u32[]{:S(2)}, u32[]{:S(2)}) collective-permute-start(bf16[4,56,896]{2,1,0:T(8,128)(2,1)S(1)} %get-tuple-element.39), channel_id=1, source_target_pairs={{0,4},{4,0},{8,12},{12,8},{16,20},{20,16},{24,28},{28,24},{1,5},{5... | collective-permute-start | bytes 1204232 | tf_op jit(solution)/shard_map/ppermute | solution.py:29
  17.1 2.4 %collective-permute-start = (bf16[4,56,896]{2,1,0:T(8,128)(2,1)S(1)}, bf16[4,56,896]{2,1,0:T(8,128)(2,1)S(1)}, u32[]{:S(2)}, u32[]{:S(2)}) collective-permute-start(bf16[4,56,896]{2,1,0:T(8,128)(2,1)S(1)} %get-tuple-element.29), channel_id=1, source_target_pairs={{0,4},{4,0},{8,12},{12,8},{16,20},{20,16},{24,28},{28,24},{1,5},{5... | collective-permute-start | bytes 1204232 | tf_op jit(solution)/shard_map/ppermute | solution.py:29
  18.9 7.1 %collective-permute-start.6 = (bf16[2,56,896]{2,1,0:T(8,128)(2,1)S(1)}, bf16[2,56,896]{2,1,0:T(8,128)(2,1)S(1)}, u32[]{:S(2)}, u32[]{:S(2)}) collective-permute-start(bf16[2,56,896]{2,1,0:T(8,128)(2,1)S(1)} %get-tuple-element.41), channel_id=1, source_target_pairs={{0,16},{4,20},{8,24},{12,28},{16,0},{20,4},{24,8},{28,12},{1,17},{... | collective-permute-start | bytes 602120 | tf_op jit(solution)/shard_map/ppermute | solution.py:29
  19.5 8.4 %collective-permute-start.1 = (bf16[2,56,896]{2,1,0:T(8,128)(2,1)S(1)}, bf16[2,56,896]{2,1,0:T(8,128)(2,1)S(1)}, u32[]{:S(2)}, u32[]{:S(2)}) collective-permute-start(bf16[2,56,896]{2,1,0:T(8,128)(2,1)S(1)} %get-tuple-element.31), channel_id=1, source_target_pairs={{0,8},{4,12},{8,0},{12,4},{16,24},{20,28},{24,16},{28,20},{1,9},{5... | collective-permute-start | bytes 602120 | tf_op jit(solution)/shard_map/ppermute | solution.py:29
  26.1 6.7 %collective-permute-start.9 = (bf16[1,56,896]{2,1,0:T(8,128)(2,1)S(1)}, bf16[1,56,896]{2,1,0:T(8,128)(2,1)S(1)}, u32[]{:S(2)}, u32[]{:S(2)}) collective-permute-start(bf16[1,56,896]{2,1,0:T(8,128)(2,1)S(1)} %get-tuple-element.43), channel_id=1, source_target_pairs={{0,8},{4,12},{8,0},{12,4},{16,24},{20,28},{24,16},{28,20},{1,9},{5... | collective-permute-start | bytes 301064 | tf_op jit(solution)/shard_map/ppermute | solution.py:29
  28.0 6.4 %collective-permute-start.2 = (bf16[1,56,896]{2,1,0:T(8,128)(2,1)S(1)}, bf16[1,56,896]{2,1,0:T(8,128)(2,1)S(1)}, u32[]{:S(2)}, u32[]{:S(2)}) collective-permute-start(bf16[1,56,896]{2,1,0:T(8,128)(2,1)S(1)} %get-tuple-element.33), channel_id=1, source_target_pairs={{0,16},{4,20},{8,24},{12,28},{16,0},{20,4},{24,8},{28,12},{1,17},{... | collective-permute-start | bytes 301064 | tf_op jit(solution)/shard_map/ppermute | solution.py:29
  29.9 15.7 %collective-permute-start.13 = (bf16[1,112,1024]{2,1,0:T(8,128)(2,1)S(1)}, bf16[1,112,1024]{2,1,0:T(8,128)(2,1)S(1)}, u32[]{:S(2)}, u32[]{:S(2)}) collective-permute-start(bf16[1,112,1024]{2,1,0:T(8,128)(2,1)S(1)} %slice.10), channel_id=1, source_target_pairs={{0,16},{4,20},{8,24},{12,28},{16,0},{20,4},{24,8},{28,12},{1,17},{... | collective-permute-start | bytes 688136 | tf_op jit(solution)/shard_map/ppermute | solution.py:29
  30.3 14.8 %collective-permute-start.15 = (bf16[2,112,1024]{2,1,0:T(8,128)(2,1)S(1)}, bf16[2,112,1024]{2,1,0:T(8,128)(2,1)S(1)}, u32[]{:S(2)}, u32[]{:S(2)}) collective-permute-start(bf16[2,112,1024]{2,1,0:T(8,128)(2,1)S(1)} %slice.13), channel_id=1, source_target_pairs={{0,8},{4,12},{8,0},{12,4},{16,24},{20,28},{24,16},{28,20},{1,9},{5... | collective-permute-start | bytes 1376264 | tf_op jit(solution)/shard_map/ppermute | solution.py:29
  32.8 4.7 %collective-permute-start.10 = (bf16[1,56,896]{2,1,0:T(8,128)(2,1)S(1)}, bf16[1,56,896]{2,1,0:T(8,128)(2,1)S(1)}, u32[]{:S(2)}, u32[]{:S(2)}) collective-permute-start(bf16[1,56,896]{2,1,0:T(8,128)(2,1)S(1)} %get-tuple-element.45), channel_id=1, source_target_pairs={{0,1},{1,0},{2,3},{3,2},{4,5},{5,4},{6,7},{7,6},{8,9},{9,8},{10,11... | collective-permute-start | bytes 301064 | tf_op jit(solution)/shard_map/ppermute | solution.py:29
  34.5 6.8 %collective-permute-start.3 = (bf16[1,56,896]{2,1,0:T(8,128)(2,1)S(1)}, bf16[1,56,896]{2,1,0:T(8,128)(2,1)S(1)}, u32[]{:S(2)}, u32[]{:S(2)}) collective-permute-start(bf16[1,56,896]{2,1,0:T(8,128)(2,1)S(1)} %get-tuple-element.35.refs_0_), channel_id=1, source_target_pairs={{0,1},{1,0},{2,3},{3,2},{4,5},{5,4},{6,7},{7,6},{8,9},{9,8},{10,11... | collective-permute-start | bytes 301064 | tf_op jit(solution)/shard_map/ppermute | solution.py:29
  35.5 11.3 %collective-permute-start.12 = (bf16[2,112,1024]{2,1,0:T(8,128)(2,1)S(1)}, bf16[2,112,1024]{2,1,0:T(8,128)(2,1)S(1)}, u32[]{:S(2)}, u32[]{:S(2)}) collective-permute-start(bf16[2,112,1024]{2,1,0:T(8,128)(2,1)S(1)} %slice.12), channel_id=1, source_target_pairs={{0,16},{4,20},{8,24},{12,28},{16,0},{20,4},{24,8},{28,12},{1,17},{... | collective-permute-start | bytes 1376264 | tf_op jit(solution)/shard_map/ppermute | solution.py:29
  37.6 7.4 %collective-permute-start.11 = (bf16[1,56,896]{2,1,0:T(8,128)(2,1)S(1)}, bf16[1,56,896]{2,1,0:T(8,128)(2,1)S(1)}, u32[]{:S(2)}, u32[]{:S(2)}) collective-permute-start(bf16[1,56,896]{2,1,0:T(8,128)(2,1)S(1)} %get-tuple-element.47), channel_id=1, source_target_pairs={{0,2},{1,3},{2,0},{3,1},{4,6},{5,7},{6,4},{7,5},{8,10},{9,11},{10,... | collective-permute-start | bytes 301064 | tf_op jit(solution)/shard_map/ppermute | solution.py:29
  41.3 6.7 %collective-permute-start.4 = (bf16[1,56,896]{2,1,0:T(8,128)(2,1)S(1)}, bf16[1,56,896]{2,1,0:T(8,128)(2,1)S(1)}, u32[]{:S(2)}, u32[]{:S(2)}) collective-permute-start(bf16[1,56,896]{2,1,0:T(8,128)(2,1)S(1)} %get-tuple-element.37.refs_0_), channel_id=1, source_target_pairs={{0,2},{1,3},{2,0},{3,1},{4,6},{5,7},{6,4},{7,5},{8,10},{9,11},{10,... | collective-permute-start | bytes 301064 | tf_op jit(solution)/shard_map/ppermute | solution.py:29
  45.5 2.6 %collective-permute-start.16 = (bf16[2,112,1024]{2,1,0:T(8,128)(2,1)S(1)}, bf16[2,112,1024]{2,1,0:T(8,128)(2,1)S(1)}, u32[]{:S(2)}, u32[]{:S(2)}) collective-permute-start(bf16[2,112,1024]{2,1,0:T(8,128)(2,1)S(1)} %shard_map.52), channel_id=1, source_target_pairs={{0,4},{4,0},{8,12},{12,8},{16,20},{20,16},{24,28},{28,24},{1,5},{5... | collective-permute-start | bytes 1376264 | tf_op jit(solution)/shard_map/ppermute | solution.py:29
  47.3 2.0 %collective-permute-start.14 = (bf16[2,112,1024]{2,1,0:T(8,128)(2,1)S(1)}, bf16[2,112,1024]{2,1,0:T(8,128)(2,1)S(1)}, u32[]{:S(2)}, u32[]{:S(2)}) collective-permute-start(bf16[2,112,1024]{2,1,0:T(8,128)(2,1)S(1)} %shard_map.51), channel_id=1, source_target_pairs={{0,4},{4,0},{8,12},{12,8},{16,20},{20,16},{24,28},{28,24},{1,5},{5... | collective-permute-start | bytes 1376264 | tf_op jit(solution)/shard_map/ppermute | solution.py:29

commit v6 on v5

--- a/solution.py
+++ b/solution.py
@@ -21,7 +21,7 @@
 
 
 PLANE_FILL = (filler(5), filler(1))
-GROUP_FILL = (filler(2), filler(2))
+GROUP_FILL = (filler(1), filler(1))
 LAST_FILL = filler(10)
 
 
@@ -197,59 +197,53 @@
     )(*in_vmem([low, *arrays]))
 
 
-def own_kernel(places, start, low_ref, arrived_ref, *refs):
-    out_hbm, out, sems = refs[-3:]
-    copies = []
+def own_rows(places, low_ref, arrived_ref, blocks, out):
     for i, place in enumerate(places):
-        both = jnp.dot(low_ref[...], block_rows(refs, place), preferred_element_type=jnp.float32)
+        both = jnp.dot(low_ref[...], block_rows(blocks, place), preferred_element_type=jnp.float32)
         out[i] = (both + arrived_ref[i].astype(jnp.float32)).astype(out.dtype)
-        copies.append(pltpu.make_async_copy(out.at[i], out_hbm.at[start + i], sems.at[i]))
-        copies[i].start()
+        yield i
+
+
+def first_kernel(places, low_ref, arrived_ref, *refs):
+    for _ in own_rows(places, low_ref, arrived_ref, refs[:-1], refs[-1]):
+        pass
+
+
+def last_kernel(places, low_ref, arrived_ref, head_ref, *refs):
+    *blocks, out_hbm, out, sems = refs
+    head = head_ref.shape[0]
+    copies = [pltpu.make_async_copy(head_ref, out_hbm.at[pl.ds(0, head)], sems.at[len(places)])]
+    copies[0].start()
+    for i in own_rows(places, low_ref, arrived_ref, blocks, out):
+        copies.append(pltpu.make_async_copy(out.at[i], out_hbm.at[head + i], sems.at[i]))
+        copies[-1].start()
     for copy in copies:
         copy.wait()
 
 
-def own_density(low, blocks, arrived, start, occ, base):
+def own_density(low, blocks, arrived, head):
     arrays, places = places_of(blocks)
-    rows, vectors = low.shape[0], arrays[0].shape[2]
-    given = [] if base is None else [base]
-    return pl.pallas_call(
-        functools.partial(own_kernel, places, start),
-        out_shape=jax.ShapeDtypeStruct((occ, rows, vectors), jnp.bfloat16),
-        in_specs=[VMEM] * (2 + len(arrays)) + [HBM] * len(given),
-        out_specs=HBM,
-        scratch_shapes=[
-            pltpu.VMEM((len(blocks), rows, vectors), jnp.bfloat16),
-            pltpu.SemaphoreType.DMA((len(blocks),)),
-        ],
-        input_output_aliases={2 + len(arrays): 0} if given else {},
+    count, rows, vectors = len(blocks), low.shape[0], arrays[0].shape[2]
+    given = [] if head is None else [head]
+    if head is None:
+        kernel, out_spec, scratch = first_kernel, VMEM, []
+        out = pltpu.VMEM((count, rows, vectors), jnp.bfloat16)
+    else:
+        kernel, out_spec = last_kernel, HBM
+        out = jax.ShapeDtypeStruct((head.shape[0] + count, rows, vectors), jnp.bfloat16)
+        scratch = [
+            pltpu.VMEM((count, rows, vectors), jnp.bfloat16),
+            pltpu.SemaphoreType.DMA((count + 1,)),
+        ]
+    return pl.pallas_call(
+        functools.partial(kernel, places),
+        out_shape=out,
+        in_specs=[VMEM] * (2 + len(given) + len(arrays)),
+        out_specs=out_spec,
+        scratch_shapes=scratch,
         compiler_params=pltpu.CompilerParams(vmem_limit_bytes=SMALL_VMEM),
         cost_estimate=FREE,
-    )(*in_vmem([low, arrived, *arrays]), *given)
-
-
-def load_kernel(cuts, own_hbm, *refs):
-    outs, sems = refs[:-1], refs[-1]
-    copies = [
-        pltpu.make_async_copy(own_hbm.at[pl.ds(start, size)], out, sems.at[n])
-        for n, ((start, size), out) in enumerate(zip(cuts, outs))
-    ]
-    for copy in copies:
-        copy.start()
-    for copy in copies:
-        copy.wait()
-
-
-def load(own, cuts):
-    return pl.pallas_call(
-        functools.partial(load_kernel, cuts),
-        out_shape=[pltpu.VMEM((size, *own.shape[1:]), own.dtype) for _, size in cuts],
-        in_specs=[HBM],
-        out_specs=[VMEM] * len(cuts),
-        scratch_shapes=[pltpu.SemaphoreType.DMA((len(cuts),))],
-        compiler_params=pltpu.CompilerParams(vmem_limit_bytes=SMALL_VMEM),
-        cost_estimate=FREE,
-    )(pltpu.with_memory_space_constraint(own, pltpu.HBM))
+    )(*in_vmem([low, arrived, *given, *arrays]))
 
 
 def lay(*arrays):
@@ -274,11 +268,7 @@
     half = occ // 2
     bits = [k for k in range(2, count) if k & (k - 1) == 0]
     even = range(0, count, 2)
-    early = occ - occ // 4
-    first = {k: (0, occ) if k == 2 else (0, early) for k in bits}
-    pieces = sorted({cut for cut in first.values() if cut[1] < occ})
-    loaded = dict(zip(pieces, load(own, pieces))) if pieces else {}
-    came = {k: swap(loaded.get(first[k], own), "virt", count, k) for k in bits}
+    came = {k: swap(own, "virt", count, k) for k in bits}
 
     product, own = pair_product(lambda_amps.reshape(-1, full), t2_amps.reshape(-1, full), own)
     other = [swap(part, "virt", count, 1) for part in cut(product, rows, 1, jnp.bfloat16)]
@@ -288,8 +278,8 @@
         for side in (1, 0):
             held = range(vv[side].shape[0])
             if step < len(bits):
-                bit = (bits[::-1] if side else bits)[step]
-                place = len(held) // 2 if side else 1
+                bit = (bits if side else bits[::-1])[step]
+                place = 1 if side else len(held) // 2
                 sent = [k for k in held if k & place]
                 rest = [k for k in held if not k & place]
             else:
@@ -300,15 +290,7 @@
             if step < len(bits):
                 other[side] = swap(narrow[side], "virt", count, bit)
 
-    held = {0: lay(own)}
-    for k in bits:
-        start, size = first[k]
-        parts = [came[k]]
-        if start:
-            parts.insert(0, swap(own[:start], "virt", count, k))
-        if start + size < occ:
-            parts.append(swap(own[start + size :], "virt", count, k))
-        held[k] = lay(*parts)
+    held = {0: lay(own)} | {k: lay(came[k]) for k in bits}
     for k in sorted(set(even) - set(held), key=lambda k: (bin(k).count("1"), k)):
         low_bit, high_bit = k & -k, 1 << (k.bit_length() - 1)
         lower = pick(held[k ^ low_bit][:half])
@@ -329,7 +311,7 @@
     arrived = [swap(other_density(low[1], blocks[a:b]), "virt", count, 1) for a, b in cuts]
     density = None
     for (a, b), part in zip(cuts, arrived):
-        density = own_density(low[0], blocks[a:b], part, a, occ, density)
+        density = own_density(low[0], blocks[a:b], part, density)
     return jnp.transpose(density, (2, 0, 1))
 
 

time: 50.7 us -> 50.6 us (level); the launches traced: 50.6 us -> 49.9 us
  waiting for transfers between devices: 11.3 us -> 13.5 us
  Pallas kernels: 17.2 us -> 15.4 us
  starting transfers between devices: 21.7 us -> 20.6 us
    ppermute x17 -> x16, waiting for transfers between devices: 11.3 us -> 13.5 us  [swap(): return lax.ppermute(array, axis, [(i, i ^ offset) for i in range(size)])]
    pallas_call x3 -> x2, Pallas kernels: 3.44 us -> 1.63 us  [own_density(): pl.pallas_call(functools.partial(kernel, places), out_shape=out, in_specs...]
    ppermute x17 -> x16, starting transfers between devices: 21.7 us -> 20.6 us  [swap(): return lax.ppermute(array, axis, [(i, i ^ offset) for i in range(size)])]
  transfers between devices with their start and end apart: 17 -> 16, of which waited for: 7 -> 7; matrix products, arithmetic and copies ran while one was open for 0% -> 0% of each run, Pallas kernels for 32% -> 28%
where the time goes in v6:
time: 50.6 us; the launch traced here: 49.9 us
  starting transfers between devices  20.6 us (41%)
  Pallas kernels  15.4 us (30%)
  waiting for transfers between devices  13.5 us (27%)
    ppermute x16, starting transfers between devices, swap(): return lax.ppermute(array, axis, [(i, i ^ offset) for i in range(size)])  20.6 us
    ppermute x16, waiting for transfers between devices, swap(): return lax.ppermute(array, axis, [(i, i ^ offset) for i in range(size)])  13.5 us
    pallas_call x1, Pallas kernels, pair_product(): pl.pallas_call(functools.partial(pair_kernel, chunks), out_shape=[pltpu.V...  10.8 us
    pallas_call x2, Pallas kernels, own_density(): pl.pallas_call(functools.partial(kernel, places), out_shape=out, in_specs...  1.63 us
    pallas_call x2, Pallas kernels, cut(): pl.pallas_call(functools.partial(cut_kernel, rows, parity), out_shape=[pl...  1.48 us
  transfers between devices with their start and end apart: 16, of which 7 were waited for; matrix products, arithmetic and copies ran while one was open for 0% of the time, Pallas kernels for 28%

profile of v6, /device:TPU:0, one launch (start us, length us, event | category | flops | bytes accessed | tf_op | source)
XLA Modules:
  0.0 49.9 jit_solution(6059099115928949566)
XLA Ops:
  0.0 2.9 %collective-permute-start.7 = (bf16[4,112,1024]{2,1,0:T(8,128)(2,1)}, bf16[4,112,1024]{2,1,0:T(8,128)(2,1)S(1)}, u32[]{:S(2)}, u32[]{:S(2)}) collective-permute-start(bf16[4,112,1024]{2,1,0:T(8,128)(2,1)} %bitcast.6), channel_id=1, source_target_pairs={{0,8},{4,12},{8,0},{12,4},{16,24},{20,28},{24,16},{28,20},{1,9},{5... | collective-permute-start | bytes 2752520 | tf_op jit(solution)/shard_map/ppermute | solution.py:29
  2.9 1.5 %collective-permute-start.8 = (bf16[4,112,1024]{2,1,0:T(8,128)(2,1)}, bf16[4,112,1024]{2,1,0:T(8,128)(2,1)S(1)}, u32[]{:S(2)}, u32[]{:S(2)}) collective-permute-start(bf16[4,112,1024]{2,1,0:T(8,128)(2,1)} %bitcast.7), channel_id=1, source_target_pairs={{0,16},{4,20},{8,24},{12,28},{16,0},{20,4},{24,8},{28,12},{1,17},{... | collective-permute-start | bytes 2752520 | tf_op jit(solution)/shard_map/ppermute | solution.py:29
  4.5 10.8 %shard_map.37 = (f32[896,896]{1,0:T(8,128)S(1)}, bf16[4,112,1024]{2,1,0:T(8,128)(2,1)S(1)}) custom-call(bf16[4480,896]{1,0:T(8,128)(2,1)} %bitcast.4, bf16[4480,896]{1,0:T(8,128)(2,1)} %bitcast.5, bf16[4,112,1024]{2,1,0:T(8,128)(2,1)} %bitcast.8), custom_call_target="tpu_custom_call" | custom-call | flops 7193231360 | bytes 16056320 | tf_op jit(solution)/shard_map/pallas_call | solution.py:78
  15.3 0.5 shard_map.39
  15.8 0.1 collective-permute-start.5
  15.9 0.5 collective-permute-start
  16.4 1.0 %shard_map.38 = (f32[4,56,896]{2,1,0:T(8,128)S(1)}, f32[4,56,896]{2,1,0:T(8,128)S(1)}) custom-call(f32[896,896]{1,0:T(8,128)S(1)} %get-tuple-element.27.total), custom_call_target="tpu_custom_call" | custom-call | tf_op jit(solution)/shard_map/pallas_call | solution.py:119
  17.4 0.2 collective-permute-done.5.other
  17.6 0.1 shard_map.45
  17.7 0.6 %collective-permute-start.6 = (bf16[2,56,896]{2,1,0:T(8,128)(2,1)S(1)}, bf16[2,56,896]{2,1,0:T(8,128)(2,1)S(1)}, u32[]{:S(2)}, u32[]{:S(2)}) collective-permute-start(bf16[2,56,896]{2,1,0:T(8,128)(2,1)S(1)} %get-tuple-element.41), channel_id=1, source_target_pairs={{0,8},{4,12},{8,0},{12,4},{16,24},{20,28},{24,16},{28,20},{1,9},{5... | collective-permute-start | bytes 602120 | tf_op jit(solution)/shard_map/ppermute | solution.py:29
  18.3 0.0 collective-permute-done.other
  18.3 0.1 shard_map.40
  18.4 0.5 collective-permute-start.1
  18.8 9.0 %collective-permute-done.6.other = bf16[2,56,896]{2,1,0:T(8,128)(2,1)S(1)} collective-permute-done((bf16[2,56,896]{2,1,0:T(8,128)(2,1)S(1)}, bf16[2,56,896]{2,1,0:T(8,128)(2,1)S(1)}, u32[]{:S(2)}, u32[]{:S(2)}) %collective-permute-start.6) | collective-permute-done | bytes 200736 | tf_op jit(solution)/shard_map/ppermute | solution.py:29
  27.8 0.0 collective-permute-done.7.refs_0_.refs_1_
  27.8 0.0 collective-permute-done.8.refs_1_.refs_2_
  27.9 1.8 %collective-permute-start.9 = (bf16[1,56,896]{2,1,0:T(8,128)(2,1)S(1)}, bf16[1,56,896]{2,1,0:T(8,128)(2,1)S(1)}, u32[]{:S(2)}, u32[]{:S(2)}) collective-permute-start(bf16[1,56,896]{2,1,0:T(8,128)(2,1)S(1)} %get-tuple-element.43), channel_id=1, source_target_pairs={{0,16},{4,20},{8,24},{12,28},{16,0},{20,4},{24,8},{28,12},{1,17},{... | collective-permute-start | bytes 301064 | tf_op jit(solution)/shard_map/ppermute | solution.py:29
  29.7 0.0 collective-permute-done.1.other
  29.7 1.6 %collective-permute-start.2 = (bf16[1,56,896]{2,1,0:T(8,128)(2,1)S(1)}, bf16[1,56,896]{2,1,0:T(8,128)(2,1)S(1)}, u32[]{:S(2)}, u32[]{:S(2)}) collective-permute-start(bf16[1,56,896]{2,1,0:T(8,128)(2,1)S(1)} %get-tuple-element.33), channel_id=1, source_target_pairs={{0,8},{4,12},{8,0},{12,4},{16,24},{20,28},{24,16},{28,20},{1,9},{5... | collective-permute-start | bytes 301064 | tf_op jit(solution)/shard_map/ppermute | solution.py:29
  31.3 0.6 %collective-permute-start.14 = (bf16[2,112,1024]{2,1,0:T(8,128)(2,1)S(1)}, bf16[2,112,1024]{2,1,0:T(8,128)(2,1)S(1)}, u32[]{:S(2)}, u32[]{:S(2)}) collective-permute-start(bf16[2,112,1024]{2,1,0:T(8,128)(2,1)S(1)} %slice.9), channel_id=1, source_target_pairs={{0,8},{4,12},{8,0},{12,4},{16,24},{20,28},{24,16},{28,20},{1,9},{5... | collective-permute-start | bytes 1376264 | tf_op jit(solution)/shard_map/ppermute | solution.py:29
  32.0 1.2 %collective-permute-start.12 = (bf16[2,112,1024]{2,1,0:T(8,128)(2,1)S(1)}, bf16[2,112,1024]{2,1,0:T(8,128)(2,1)S(1)}, u32[]{:S(2)}, u32[]{:S(2)}) collective-permute-start(bf16[2,112,1024]{2,1,0:T(8,128)(2,1)S(1)} %slice.8), channel_id=1, source_target_pairs={{0,16},{4,20},{8,24},{12,28},{16,0},{20,4},{24,8},{28,12},{1,17},{... | collective-permute-start | bytes 1376264 | tf_op jit(solution)/shard_map/ppermute | solution.py:29
  33.1 0.0 collective-permute-done.9.other
  33.1 1.6 %collective-permute-start.10 = (bf16[1,56,896]{2,1,0:T(8,128)(2,1)S(1)}, bf16[1,56,896]{2,1,0:T(8,128)(2,1)S(1)}, u32[]{:S(2)}, u32[]{:S(2)}) collective-permute-start(bf16[1,56,896]{2,1,0:T(8,128)(2,1)S(1)} %get-tuple-element.45), channel_id=1, source_target_pairs={{0,1},{1,0},{2,3},{3,2},{4,5},{5,4},{6,7},{7,6},{8,9},{9,8},{10,11... | collective-permute-start | bytes 301064 | tf_op jit(solution)/shard_map/ppermute | solution.py:29
  34.8 0.7 %collective-permute-done.2.other = bf16[1,56,896]{2,1,0:T(8,128)(2,1)S(1)} collective-permute-done((bf16[1,56,896]{2,1,0:T(8,128)(2,1)S(1)}, bf16[1,56,896]{2,1,0:T(8,128)(2,1)S(1)}, u32[]{:S(2)}, u32[]{:S(2)}) %collective-permute-start.2) | collective-permute-done | bytes 100384 | tf_op jit(solution)/shard_map/ppermute | solution.py:29
  35.5 1.6 %collective-permute-start.3 = (bf16[1,56,896]{2,1,0:T(8,128)(2,1)S(1)}, bf16[1,56,896]{2,1,0:T(8,128)(2,1)S(1)}, u32[]{:S(2)}, u32[]{:S(2)}) collective-permute-start(bf16[1,56,896]{2,1,0:T(8,128)(2,1)S(1)} %get-tuple-element.35.refs_0_), channel_id=1, source_target_pairs={{0,1},{1,0},{2,3},{3,2},{4,5},{5,4},{6,7},{7,6},{8,9},{9,8},{10,11... | collective-permute-start | bytes 301064 | tf_op jit(solution)/shard_map/ppermute | solution.py:29
  37.2 0.7 %collective-permute-done.10.other = bf16[1,56,896]{2,1,0:T(8,128)(2,1)S(1)} collective-permute-done((bf16[1,56,896]{2,1,0:T(8,128)(2,1)S(1)}, bf16[1,56,896]{2,1,0:T(8,128)(2,1)S(1)}, u32[]{:S(2)}, u32[]{:S(2)}) %collective-permute-start.10) | collective-permute-done | bytes 100384 | tf_op jit(solution)/shard_map/ppermute | solution.py:29
  37.9 3.2 %collective-permute-start.11 = (bf16[1,56,896]{2,1,0:T(8,128)(2,1)S(1)}, bf16[1,56,896]{2,1,0:T(8,128)(2,1)S(1)}, u32[]{:S(2)}, u32[]{:S(2)}) collective-permute-start(bf16[1,56,896]{2,1,0:T(8,128)(2,1)S(1)} %get-tuple-element.47), channel_id=1, source_target_pairs={{0,2},{1,3},{2,0},{3,1},{4,6},{5,7},{6,4},{7,5},{8,10},{9,11},{10,... | collective-permute-start | bytes 301064 | tf_op jit(solution)/shard_map/ppermute | solution.py:29
  41.1 0.0 collective-permute-done.3.other
  41.1 2.3 %collective-permute-start.4 = (bf16[1,56,896]{2,1,0:T(8,128)(2,1)S(1)}, bf16[1,56,896]{2,1,0:T(8,128)(2,1)S(1)}, u32[]{:S(2)}, u32[]{:S(2)}) collective-permute-start(bf16[1,56,896]{2,1,0:T(8,128)(2,1)S(1)} %get-tuple-element.37.refs_0_), channel_id=1, source_target_pairs={{0,2},{1,3},{2,0},{3,1},{4,6},{5,7},{6,4},{7,5},{8,10},{9,11},{10,... | collective-permute-start | bytes 301064 | tf_op jit(solution)/shard_map/ppermute | solution.py:29
  43.4 2.0 %collective-permute-done.11.part_ref = bf16[1,56,896]{2,1,0:T(8,128)(2,1)S(1)} collective-permute-done((bf16[1,56,896]{2,1,0:T(8,128)(2,1)S(1)}, bf16[1,56,896]{2,1,0:T(8,128)(2,1)S(1)}, u32[]{:S(2)}, u32[]{:S(2)}) %collective-permute-start.11) | collective-permute-done | bytes 100384 | tf_op jit(solution)/shard_map/ppermute | solution.py:29
  45.4 0.1 shard_map.49.low_ref
  45.5 0.0 collective-permute-done.14.refs_3_
  45.5 0.4 shard_map.51
  46.0 0.1 collective-permute-start.15
  46.0 0.0 collective-permute-done.12.refs_3_
  46.1 0.4 shard_map.50
  46.5 0.6 %collective-permute-start.13 = (bf16[2,112,1024]{2,1,0:T(8,128)(2,1)S(1)}, bf16[2,112,1024]{2,1,0:T(8,128)(2,1)S(1)}, u32[]{:S(2)}, u32[]{:S(2)}) collective-permute-start(bf16[2,112,1024]{2,1,0:T(8,128)(2,1)S(1)} %shard_map.50), channel_id=1, source_target_pairs={{0,4},{4,0},{8,12},{12,8},{16,20},{20,16},{24,28},{28,24},{1,5},{5... | collective-permute-start | bytes 1376264 | tf_op jit(solution)/shard_map/ppermute | solution.py:29
  47.1 0.0 collective-permute-done.4.part_ref
  47.1 0.1 shard_map.44.low_ref
  47.2 0.7 %collective-permute-done.15.arrived_ref = bf16[2,112,1024]{2,1,0:T(8,128)(2,1)S(1)} collective-permute-done((bf16[2,112,1024]{2,1,0:T(8,128)(2,1)S(1)}, bf16[2,112,1024]{2,1,0:T(8,128)(2,1)S(1)}, u32[]{:S(2)}, u32[]{:S(2)}) %collective-permute-start.15) | collective-permute-done | bytes 458784 | tf_op jit(solution)/shard_map/ppermute | solution.py:29
  47.9 0.4 shard_map.52.head_ref
  48.3 0.2 collective-permute-done.13.arrived_ref
  48.5 1.2 %shard_map.53 = bf16[4,112,1024]{2,1,0:T(8,128)(2,1)} custom-call(bf16[112,448]{1,0:T(8,128)(2,1)S(1)} %shard_map.44.low_ref, bf16[2,112,1024]{2,1,0:T(8,128)(2,1)S(1)} %collective-permute-done.13.arrived_ref, bf16[2,112,1024]{2,1,0:T(8,128)(2,1)S(1)} %shard_map.52.head_ref, bf16[4,112,1024]{2,1,0:T(8,128)(2,1)S(1)} %get-tuple-element.48.refs_0_, ...), custom_call_target="tpu_custom_call" | custom-call | tf_op jit(solution)/shard_map/pallas_call | solution.py:238
  (8 shorter events, 0.3 us)
Async XLA Ops:
  0.0 27.8 %collective-permute-start.7 = (bf16[4,112,1024]{2,1,0:T(8,128)(2,1)}, bf16[4,112,1024]{2,1,0:T(8,128)(2,1)S(1)}, u32[]{:S(2)}, u32[]{:S(2)}) collective-permute-start(bf16[4,112,1024]{2,1,0:T(8,128)(2,1)} %bitcast.6), channel_id=1, source_target_pairs={{0,8},{4,12},{8,0},{12,4},{16,24},{20,28},{24,16},{28,20},{1,9},{5... | collective-permute-start | bytes 2752520 | tf_op jit(solution)/shard_map/ppermute | solution.py:29
  2.9 24.9 %collective-permute-start.8 = (bf16[4,112,1024]{2,1,0:T(8,128)(2,1)}, bf16[4,112,1024]{2,1,0:T(8,128)(2,1)S(1)}, u32[]{:S(2)}, u32[]{:S(2)}) collective-permute-start(bf16[4,112,1024]{2,1,0:T(8,128)(2,1)} %bitcast.7), channel_id=1, source_target_pairs={{0,16},{4,20},{8,24},{12,28},{16,0},{20,4},{24,8},{28,12},{1,17},{... | collective-permute-start | bytes 2752520 | tf_op jit(solution)/shard_map/ppermute | solution.py:29
  15.8 1.8 %collective-permute-start.5 = (bf16[4,56,896]{2,1,0:T(8,128)(2,1)S(1)}, bf16[4,56,896]{2,1,0:T(8,128)(2,1)S(1)}, u32[]{:S(2)}, u32[]{:S(2)}) collective-permute-start(bf16[4,56,896]{2,1,0:T(8,128)(2,1)S(1)} %get-tuple-element.39), channel_id=1, source_target_pairs={{0,4},{4,0},{8,12},{12,8},{16,20},{20,16},{24,28},{28,24},{1,5},{5... | collective-permute-start | bytes 1204232 | tf_op jit(solution)/shard_map/ppermute | solution.py:29
  15.9 2.4 %collective-permute-start = (bf16[4,56,896]{2,1,0:T(8,128)(2,1)S(1)}, bf16[4,56,896]{2,1,0:T(8,128)(2,1)S(1)}, u32[]{:S(2)}, u32[]{:S(2)}) collective-permute-start(bf16[4,56,896]{2,1,0:T(8,128)(2,1)S(1)} %get-tuple-element.29), channel_id=1, source_target_pairs={{0,4},{4,0},{8,12},{12,8},{16,20},{20,16},{24,28},{28,24},{1,5},{5... | collective-permute-start | bytes 1204232 | tf_op jit(solution)/shard_map/ppermute | solution.py:29
  17.7 10.1 %collective-permute-start.6 = (bf16[2,56,896]{2,1,0:T(8,128)(2,1)S(1)}, bf16[2,56,896]{2,1,0:T(8,128)(2,1)S(1)}, u32[]{:S(2)}, u32[]{:S(2)}) collective-permute-start(bf16[2,56,896]{2,1,0:T(8,128)(2,1)S(1)} %get-tuple-element.41), channel_id=1, source_target_pairs={{0,8},{4,12},{8,0},{12,4},{16,24},{20,28},{24,16},{28,20},{1,9},{5... | collective-permute-start | bytes 602120 | tf_op jit(solution)/shard_map/ppermute | solution.py:29
  18.4 11.3 %collective-permute-start.1 = (bf16[2,56,896]{2,1,0:T(8,128)(2,1)S(1)}, bf16[2,56,896]{2,1,0:T(8,128)(2,1)S(1)}, u32[]{:S(2)}, u32[]{:S(2)}) collective-permute-start(bf16[2,56,896]{2,1,0:T(8,128)(2,1)S(1)} %get-tuple-element.31), channel_id=1, source_target_pairs={{0,16},{4,20},{8,24},{12,28},{16,0},{20,4},{24,8},{28,12},{1,17},{... | collective-permute-start | bytes 602120 | tf_op jit(solution)/shard_map/ppermute | solution.py:29
  27.9 5.3 %collective-permute-start.9 = (bf16[1,56,896]{2,1,0:T(8,128)(2,1)S(1)}, bf16[1,56,896]{2,1,0:T(8,128)(2,1)S(1)}, u32[]{:S(2)}, u32[]{:S(2)}) collective-permute-start(bf16[1,56,896]{2,1,0:T(8,128)(2,1)S(1)} %get-tuple-element.43), channel_id=1, source_target_pairs={{0,16},{4,20},{8,24},{12,28},{16,0},{20,4},{24,8},{28,12},{1,17},{... | collective-permute-start | bytes 301064 | tf_op jit(solution)/shard_map/ppermute | solution.py:29
  29.7 5.8 %collective-permute-start.2 = (bf16[1,56,896]{2,1,0:T(8,128)(2,1)S(1)}, bf16[1,56,896]{2,1,0:T(8,128)(2,1)S(1)}, u32[]{:S(2)}, u32[]{:S(2)}) collective-permute-start(bf16[1,56,896]{2,1,0:T(8,128)(2,1)S(1)} %get-tuple-element.33), channel_id=1, source_target_pairs={{0,8},{4,12},{8,0},{12,4},{16,24},{20,28},{24,16},{28,20},{1,9},{5... | collective-permute-start | bytes 301064 | tf_op jit(solution)/shard_map/ppermute | solution.py:29
  31.3 14.2 %collective-permute-start.14 = (bf16[2,112,1024]{2,1,0:T(8,128)(2,1)S(1)}, bf16[2,112,1024]{2,1,0:T(8,128)(2,1)S(1)}, u32[]{:S(2)}, u32[]{:S(2)}) collective-permute-start(bf16[2,112,1024]{2,1,0:T(8,128)(2,1)S(1)} %slice.9), channel_id=1, source_target_pairs={{0,8},{4,12},{8,0},{12,4},{16,24},{20,28},{24,16},{28,20},{1,9},{5... | collective-permute-start | bytes 1376264 | tf_op jit(solution)/shard_map/ppermute | solution.py:29
  32.0 14.1 %collective-permute-start.12 = (bf16[2,112,1024]{2,1,0:T(8,128)(2,1)S(1)}, bf16[2,112,1024]{2,1,0:T(8,128)(2,1)S(1)}, u32[]{:S(2)}, u32[]{:S(2)}) collective-permute-start(bf16[2,112,1024]{2,1,0:T(8,128)(2,1)S(1)} %slice.8), channel_id=1, source_target_pairs={{0,16},{4,20},{8,24},{12,28},{16,0},{20,4},{24,8},{28,12},{1,17},{... | collective-permute-start | bytes 1376264 | tf_op jit(solution)/shard_map/ppermute | solution.py:29
  33.1 4.7 %collective-permute-start.10 = (bf16[1,56,896]{2,1,0:T(8,128)(2,1)S(1)}, bf16[1,56,896]{2,1,0:T(8,128)(2,1)S(1)}, u32[]{:S(2)}, u32[]{:S(2)}) collective-permute-start(bf16[1,56,896]{2,1,0:T(8,128)(2,1)S(1)} %get-tuple-element.45), channel_id=1, source_target_pairs={{0,1},{1,0},{2,3},{3,2},{4,5},{5,4},{6,7},{7,6},{8,9},{9,8},{10,11... | collective-permute-start | bytes 301064 | tf_op jit(solution)/shard_map/ppermute | solution.py:29
  35.5 5.5 %collective-permute-start.3 = (bf16[1,56,896]{2,1,0:T(8,128)(2,1)S(1)}, bf16[1,56,896]{2,1,0:T(8,128)(2,1)S(1)}, u32[]{:S(2)}, u32[]{:S(2)}) collective-permute-start(bf16[1,56,896]{2,1,0:T(8,128)(2,1)S(1)} %get-tuple-element.35.refs_0_), channel_id=1, source_target_pairs={{0,1},{1,0},{2,3},{3,2},{4,5},{5,4},{6,7},{7,6},{8,9},{9,8},{10,11... | collective-permute-start | bytes 301064 | tf_op jit(solution)/shard_map/ppermute | solution.py:29
  37.9 7.5 %collective-permute-start.11 = (bf16[1,56,896]{2,1,0:T(8,128)(2,1)S(1)}, bf16[1,56,896]{2,1,0:T(8,128)(2,1)S(1)}, u32[]{:S(2)}, u32[]{:S(2)}) collective-permute-start(bf16[1,56,896]{2,1,0:T(8,128)(2,1)S(1)} %get-tuple-element.47), channel_id=1, source_target_pairs={{0,2},{1,3},{2,0},{3,1},{4,6},{5,7},{6,4},{7,5},{8,10},{9,11},{10,... | collective-permute-start | bytes 301064 | tf_op jit(solution)/shard_map/ppermute | solution.py:29
  41.1 6.0 %collective-permute-start.4 = (bf16[1,56,896]{2,1,0:T(8,128)(2,1)S(1)}, bf16[1,56,896]{2,1,0:T(8,128)(2,1)S(1)}, u32[]{:S(2)}, u32[]{:S(2)}) collective-permute-start(bf16[1,56,896]{2,1,0:T(8,128)(2,1)S(1)} %get-tuple-element.37.refs_0_), channel_id=1, source_target_pairs={{0,2},{1,3},{2,0},{3,1},{4,6},{5,7},{6,4},{7,5},{8,10},{9,11},{10,... | collective-permute-start | bytes 301064 | tf_op jit(solution)/shard_map/ppermute | solution.py:29
  46.0 1.9 %collective-permute-start.15 = (bf16[2,112,1024]{2,1,0:T(8,128)(2,1)S(1)}, bf16[2,112,1024]{2,1,0:T(8,128)(2,1)S(1)}, u32[]{:S(2)}, u32[]{:S(2)}) collective-permute-start(bf16[2,112,1024]{2,1,0:T(8,128)(2,1)S(1)} %shard_map.51), channel_id=1, source_target_pairs={{0,4},{4,0},{8,12},{12,8},{16,20},{20,16},{24,28},{28,24},{1,5},{5... | collective-permute-start | bytes 1376264 | tf_op jit(solution)/shard_map/ppermute | solution.py:29
  46.5 2.0 %collective-permute-start.13 = (bf16[2,112,1024]{2,1,0:T(8,128)(2,1)S(1)}, bf16[2,112,1024]{2,1,0:T(8,128)(2,1)S(1)}, u32[]{:S(2)}, u32[]{:S(2)}) collective-permute-start(bf16[2,112,1024]{2,1,0:T(8,128)(2,1)S(1)} %shard_map.50), channel_id=1, source_target_pairs={{0,4},{4,0},{8,12},{12,8},{16,20},{20,16},{24,28},{28,24},{1,5},{5... | collective-permute-start | bytes 1376264 | tf_op jit(solution)/shard_map/ppermute | solution.py:29

commit v7 on v6

--- a/solution.py
+++ b/solution.py
@@ -209,34 +209,39 @@
         pass
 
 
-def last_kernel(places, low_ref, arrived_ref, head_ref, *refs):
-    *blocks, out_hbm, out, sems = refs
-    head = head_ref.shape[0]
-    copies = [pltpu.make_async_copy(head_ref, out_hbm.at[pl.ds(0, head)], sems.at[len(places)])]
-    copies[0].start()
+def last_kernel(places, count, low_ref, arrived_ref, *refs):
+    heads, blocks = refs[:count], refs[count:-3]
+    out_hbm, out, sems = refs[-3:]
+    copies, at = [], 0
+    for n, head in enumerate(heads):
+        span = pl.ds(at, head.shape[0])
+        copies.append(pltpu.make_async_copy(head, out_hbm.at[span], sems.at[len(places) + n]))
+        copies[-1].start()
+        at += head.shape[0]
     for i in own_rows(places, low_ref, arrived_ref, blocks, out):
-        copies.append(pltpu.make_async_copy(out.at[i], out_hbm.at[head + i], sems.at[i]))
+        copies.append(pltpu.make_async_copy(out.at[i], out_hbm.at[at + i], sems.at[i]))
         copies[-1].start()
     for copy in copies:
         copy.wait()
 
 
-def own_density(low, blocks, arrived, head):
+def own_density(low, blocks, arrived, heads):
     arrays, places = places_of(blocks)
     count, rows, vectors = len(blocks), low.shape[0], arrays[0].shape[2]
-    given = [] if head is None else [head]
-    if head is None:
-        kernel, out_spec, scratch = first_kernel, VMEM, []
+    given = heads or []
+    if heads is None:
+        kernel, out_spec, scratch = functools.partial(first_kernel, places), VMEM, []
         out = pltpu.VMEM((count, rows, vectors), jnp.bfloat16)
     else:
-        kernel, out_spec = last_kernel, HBM
-        out = jax.ShapeDtypeStruct((head.shape[0] + count, rows, vectors), jnp.bfloat16)
+        kernel, out_spec = functools.partial(last_kernel, places, len(given)), HBM
+        occ = sum(head.shape[0] for head in given) + count
+        out = jax.ShapeDtypeStruct((occ, rows, vectors), jnp.bfloat16)
         scratch = [
             pltpu.VMEM((count, rows, vectors), jnp.bfloat16),
-            pltpu.SemaphoreType.DMA((count + 1,)),
+            pltpu.SemaphoreType.DMA((count + len(given),)),
         ]
     return pl.pallas_call(
-        functools.partial(kernel, places),
+        kernel,
         out_shape=out,
         in_specs=[VMEM] * (2 + len(given) + len(arrays)),
         out_specs=out_spec,
@@ -307,11 +312,13 @@
             narrow[0], vv[0] = merge(vv[0], part[0], [0], [0], [], GROUP_FILL[0])
         step *= 2
     low = {1: low_rows(vv[1], part[1], after, FREE), 0: low_rows(vv[0], part[0], [], LAST_FILL)}
-    cuts = ((0, half), (half, occ))
+    edges = sorted({0, occ - 1, occ})
+    cuts = list(zip(edges, edges[1:]))
     arrived = [swap(other_density(low[1], blocks[a:b]), "virt", count, 1) for a, b in cuts]
-    density = None
-    for (a, b), part in zip(cuts, arrived):
-        density = own_density(low[0], blocks[a:b], part, density)
+    heads = [
+        own_density(low[0], blocks[a:b], part, None) for (a, b), part in zip(cuts[:-1], arrived)
+    ]
+    density = own_density(low[0], blocks[cuts[-1][0] :], arrived[-1], heads)
     return jnp.transpose(density, (2, 0, 1))
 
 

time: 50.6 us -> 50.6 us (level)
  transfers between devices with their start and end apart: 16 -> 16, of which waited for: 7 -> 7; matrix products, arithmetic and copies ran while one was open for 0% -> 0% of each run, Pallas kernels for 28% -> 29%
where the time goes in v7:
time: 50.6 us; the launch traced here: 50.2 us
  starting transfers between devices  20.7 us (41%)
  Pallas kernels  15.4 us (30%)
  waiting for transfers between devices  13.7 us (27%)
    ppermute x16, starting transfers between devices, swap(): return lax.ppermute(array, axis, [(i, i ^ offset) for i in range(size)])  20.7 us
    ppermute x16, waiting for transfers between devices, swap(): return lax.ppermute(array, axis, [(i, i ^ offset) for i in range(size)])  13.7 us
    pallas_call x1, Pallas kernels, pair_product(): pl.pallas_call(functools.partial(pair_kernel, chunks), out_shape=[pltpu.V...  10.8 us
    pallas_call x2, Pallas kernels, own_density(): pl.pallas_call(kernel, out_shape=out, in_specs=[VMEM] * (2 + len(given) +...  1.64 us
    pallas_call x2, Pallas kernels, cut(): pl.pallas_call(functools.partial(cut_kernel, rows, parity), out_shape=[pl...  1.48 us
  transfers between devices with their start and end apart: 16, of which 7 were waited for; matrix products, arithmetic and copies ran while one was open for 0% of the time, Pallas kernels for 29%

profile of v7, /device:TPU:0, one launch (start us, length us, event | category | flops | bytes accessed | tf_op | source)
XLA Modules:
  0.0 50.2 jit_solution(6660835416169062617)
XLA Ops:
  0.0 2.9 %collective-permute-start.7 = (bf16[4,112,1024]{2,1,0:T(8,128)(2,1)}, bf16[4,112,1024]{2,1,0:T(8,128)(2,1)S(1)}, u32[]{:S(2)}, u32[]{:S(2)}) collective-permute-start(bf16[4,112,1024]{2,1,0:T(8,128)(2,1)} %bitcast.6), channel_id=1, source_target_pairs={{0,8},{4,12},{8,0},{12,4},{16,24},{20,28},{24,16},{28,20},{1,9},{5... | collective-permute-start | bytes 2752520 | tf_op jit(solution)/shard_map/ppermute | solution.py:29
  2.9 1.5 %collective-permute-start.8 = (bf16[4,112,1024]{2,1,0:T(8,128)(2,1)}, bf16[4,112,1024]{2,1,0:T(8,128)(2,1)S(1)}, u32[]{:S(2)}, u32[]{:S(2)}) collective-permute-start(bf16[4,112,1024]{2,1,0:T(8,128)(2,1)} %bitcast.7), channel_id=1, source_target_pairs={{0,16},{4,20},{8,24},{12,28},{16,0},{20,4},{24,8},{28,12},{1,17},{... | collective-permute-start | bytes 2752520 | tf_op jit(solution)/shard_map/ppermute | solution.py:29
  4.5 10.8 %shard_map.37 = (f32[896,896]{1,0:T(8,128)S(1)}, bf16[4,112,1024]{2,1,0:T(8,128)(2,1)S(1)}) custom-call(bf16[4480,896]{1,0:T(8,128)(2,1)} %bitcast.4, bf16[4480,896]{1,0:T(8,128)(2,1)} %bitcast.5, bf16[4,112,1024]{2,1,0:T(8,128)(2,1)} %bitcast.8), custom_call_target="tpu_custom_call" | custom-call | flops 7193231360 | bytes 16056320 | tf_op jit(solution)/shard_map/pallas_call | solution.py:78
  15.3 0.5 shard_map.39
  15.8 0.1 collective-permute-start.5
  15.9 0.5 collective-permute-start
  16.4 1.0 %shard_map.38 = (f32[4,56,896]{2,1,0:T(8,128)S(1)}, f32[4,56,896]{2,1,0:T(8,128)S(1)}) custom-call(f32[896,896]{1,0:T(8,128)S(1)} %get-tuple-element.27.total), custom_call_target="tpu_custom_call" | custom-call | tf_op jit(solution)/shard_map/pallas_call | solution.py:119
  17.4 0.2 collective-permute-done.5.other
  17.6 0.1 shard_map.45
  17.7 0.6 %collective-permute-start.6 = (bf16[2,56,896]{2,1,0:T(8,128)(2,1)S(1)}, bf16[2,56,896]{2,1,0:T(8,128)(2,1)S(1)}, u32[]{:S(2)}, u32[]{:S(2)}) collective-permute-start(bf16[2,56,896]{2,1,0:T(8,128)(2,1)S(1)} %get-tuple-element.41), channel_id=1, source_target_pairs={{0,8},{4,12},{8,0},{12,4},{16,24},{20,28},{24,16},{28,20},{1,9},{5... | collective-permute-start | bytes 602120 | tf_op jit(solution)/shard_map/ppermute | solution.py:29
  18.3 0.0 collective-permute-done.other
  18.3 0.1 shard_map.40
  18.4 0.5 collective-permute-start.1
  18.8 9.0 %collective-permute-done.6.other = bf16[2,56,896]{2,1,0:T(8,128)(2,1)S(1)} collective-permute-done((bf16[2,56,896]{2,1,0:T(8,128)(2,1)S(1)}, bf16[2,56,896]{2,1,0:T(8,128)(2,1)S(1)}, u32[]{:S(2)}, u32[]{:S(2)}) %collective-permute-start.6) | collective-permute-done | bytes 200736 | tf_op jit(solution)/shard_map/ppermute | solution.py:29
  27.8 0.0 collective-permute-done.7.refs_0_.refs_1_.refs_2_
  27.8 0.0 collective-permute-done.8.refs_1_.refs_2_.refs_3_
  27.9 1.8 %collective-permute-start.9 = (bf16[1,56,896]{2,1,0:T(8,128)(2,1)S(1)}, bf16[1,56,896]{2,1,0:T(8,128)(2,1)S(1)}, u32[]{:S(2)}, u32[]{:S(2)}) collective-permute-start(bf16[1,56,896]{2,1,0:T(8,128)(2,1)S(1)} %get-tuple-element.43), channel_id=1, source_target_pairs={{0,16},{4,20},{8,24},{12,28},{16,0},{20,4},{24,8},{28,12},{1,17},{... | collective-permute-start | bytes 301064 | tf_op jit(solution)/shard_map/ppermute | solution.py:29
  29.7 0.0 collective-permute-done.1.other
  29.7 1.6 %collective-permute-start.2 = (bf16[1,56,896]{2,1,0:T(8,128)(2,1)S(1)}, bf16[1,56,896]{2,1,0:T(8,128)(2,1)S(1)}, u32[]{:S(2)}, u32[]{:S(2)}) collective-permute-start(bf16[1,56,896]{2,1,0:T(8,128)(2,1)S(1)} %get-tuple-element.33), channel_id=1, source_target_pairs={{0,8},{4,12},{8,0},{12,4},{16,24},{20,28},{24,16},{28,20},{1,9},{5... | collective-permute-start | bytes 301064 | tf_op jit(solution)/shard_map/ppermute | solution.py:29
  31.3 0.6 %collective-permute-start.12 = (bf16[2,112,1024]{2,1,0:T(8,128)(2,1)S(1)}, bf16[2,112,1024]{2,1,0:T(8,128)(2,1)S(1)}, u32[]{:S(2)}, u32[]{:S(2)}) collective-permute-start(bf16[2,112,1024]{2,1,0:T(8,128)(2,1)S(1)} %slice.8), channel_id=1, source_target_pairs={{0,16},{4,20},{8,24},{12,28},{16,0},{20,4},{24,8},{28,12},{1,17},{... | collective-permute-start | bytes 1376264 | tf_op jit(solution)/shard_map/ppermute | solution.py:29
  32.0 1.2 %collective-permute-start.14 = (bf16[2,112,1024]{2,1,0:T(8,128)(2,1)S(1)}, bf16[2,112,1024]{2,1,0:T(8,128)(2,1)S(1)}, u32[]{:S(2)}, u32[]{:S(2)}) collective-permute-start(bf16[2,112,1024]{2,1,0:T(8,128)(2,1)S(1)} %slice.9), channel_id=1, source_target_pairs={{0,8},{4,12},{8,0},{12,4},{16,24},{20,28},{24,16},{28,20},{1,9},{5... | collective-permute-start | bytes 1376264 | tf_op jit(solution)/shard_map/ppermute | solution.py:29
  33.1 0.0 collective-permute-done.9.other
  33.2 1.8 %collective-permute-start.10 = (bf16[1,56,896]{2,1,0:T(8,128)(2,1)S(1)}, bf16[1,56,896]{2,1,0:T(8,128)(2,1)S(1)}, u32[]{:S(2)}, u32[]{:S(2)}) collective-permute-start(bf16[1,56,896]{2,1,0:T(8,128)(2,1)S(1)} %get-tuple-element.45), channel_id=1, source_target_pairs={{0,1},{1,0},{2,3},{3,2},{4,5},{5,4},{6,7},{7,6},{8,9},{9,8},{10,11... | collective-permute-start | bytes 301064 | tf_op jit(solution)/shard_map/ppermute | solution.py:29
  34.9 0.5 %collective-permute-done.2.other = bf16[1,56,896]{2,1,0:T(8,128)(2,1)S(1)} collective-permute-done((bf16[1,56,896]{2,1,0:T(8,128)(2,1)S(1)}, bf16[1,56,896]{2,1,0:T(8,128)(2,1)S(1)}, u32[]{:S(2)}, u32[]{:S(2)}) %collective-permute-start.2) | collective-permute-done | bytes 100384 | tf_op jit(solution)/shard_map/ppermute | solution.py:29
  35.5 1.6 %collective-permute-start.3 = (bf16[1,56,896]{2,1,0:T(8,128)(2,1)S(1)}, bf16[1,56,896]{2,1,0:T(8,128)(2,1)S(1)}, u32[]{:S(2)}, u32[]{:S(2)}) collective-permute-start(bf16[1,56,896]{2,1,0:T(8,128)(2,1)S(1)} %get-tuple-element.35.refs_0_), channel_id=1, source_target_pairs={{0,1},{1,0},{2,3},{3,2},{4,5},{5,4},{6,7},{7,6},{8,9},{9,8},{10,11... | collective-permute-start | bytes 301064 | tf_op jit(solution)/shard_map/ppermute | solution.py:29
  37.1 0.7 %collective-permute-done.10.other = bf16[1,56,896]{2,1,0:T(8,128)(2,1)S(1)} collective-permute-done((bf16[1,56,896]{2,1,0:T(8,128)(2,1)S(1)}, bf16[1,56,896]{2,1,0:T(8,128)(2,1)S(1)}, u32[]{:S(2)}, u32[]{:S(2)}) %collective-permute-start.10) | collective-permute-done | bytes 100384 | tf_op jit(solution)/shard_map/ppermute | solution.py:29
  37.9 3.5 %collective-permute-start.11 = (bf16[1,56,896]{2,1,0:T(8,128)(2,1)S(1)}, bf16[1,56,896]{2,1,0:T(8,128)(2,1)S(1)}, u32[]{:S(2)}, u32[]{:S(2)}) collective-permute-start(bf16[1,56,896]{2,1,0:T(8,128)(2,1)S(1)} %get-tuple-element.47), channel_id=1, source_target_pairs={{0,2},{1,3},{2,0},{3,1},{4,6},{5,7},{6,4},{7,5},{8,10},{9,11},{10,... | collective-permute-start | bytes 301064 | tf_op jit(solution)/shard_map/ppermute | solution.py:29
  41.4 0.0 collective-permute-done.3.other
  41.4 1.9 %collective-permute-start.4 = (bf16[1,56,896]{2,1,0:T(8,128)(2,1)S(1)}, bf16[1,56,896]{2,1,0:T(8,128)(2,1)S(1)}, u32[]{:S(2)}, u32[]{:S(2)}) collective-permute-start(bf16[1,56,896]{2,1,0:T(8,128)(2,1)S(1)} %get-tuple-element.37.refs_0_), channel_id=1, source_target_pairs={{0,2},{1,3},{2,0},{3,1},{4,6},{5,7},{6,4},{7,5},{8,10},{9,11},{10,... | collective-permute-start | bytes 301064 | tf_op jit(solution)/shard_map/ppermute | solution.py:29
  43.3 2.1 %collective-permute-done.11.part_ref = bf16[1,56,896]{2,1,0:T(8,128)(2,1)S(1)} collective-permute-done((bf16[1,56,896]{2,1,0:T(8,128)(2,1)S(1)}, bf16[1,56,896]{2,1,0:T(8,128)(2,1)S(1)}, u32[]{:S(2)}, u32[]{:S(2)}) %collective-permute-start.11) | collective-permute-done | bytes 100384 | tf_op jit(solution)/shard_map/ppermute | solution.py:29
  45.5 0.1 shard_map.49.low_ref
  45.6 0.0 collective-permute-done.12.refs_3_.refs_4_
  45.6 0.0 collective-permute-done.14.refs_3_
  45.6 0.6 %shard_map.51 = bf16[3,112,1024]{2,1,0:T(8,128)(2,1)S(1)} custom-call(bf16[112,448]{1,0:T(8,128)(2,1)S(1)} %shard_map.49.low_ref, bf16[4,112,1024]{2,1,0:T(8,128)(2,1)S(1)} %get-tuple-element.48.refs_0_.refs_1_, bf16[4,112,1024]{2,1,0:T(8,128)(2,1)S(1)} %collective-permute-done.7.refs_0_.refs_1_.refs_2_, ...), custom_call_target="tpu_custom_call" | custom-call | tf_op jit(solution)/shard_map/pallas_call | solution.py:190
  46.2 0.1 collective-permute-start.15
  46.2 0.3 shard_map.50
  46.5 0.6 %collective-permute-start.13 = (bf16[1,112,1024]{2,1,0:T(8,128)(2,1)S(1)}, bf16[1,112,1024]{2,1,0:T(8,128)(2,1)S(1)}, u32[]{:S(2)}, u32[]{:S(2)}) collective-permute-start(bf16[1,112,1024]{2,1,0:T(8,128)(2,1)S(1)} %shard_map.50), channel_id=1, source_target_pairs={{0,4},{4,0},{8,12},{12,8},{16,20},{20,16},{24,28},{28,24},{1,5},{5... | collective-permute-start | bytes 688136 | tf_op jit(solution)/shard_map/ppermute | solution.py:29
  47.1 1.0 %collective-permute-done.4.part_ref = bf16[1,56,896]{2,1,0:T(8,128)(2,1)S(1)} collective-permute-done((bf16[1,56,896]{2,1,0:T(8,128)(2,1)S(1)}, bf16[1,56,896]{2,1,0:T(8,128)(2,1)S(1)}, u32[]{:S(2)}, u32[]{:S(2)}) %collective-permute-start.4) | collective-permute-done | bytes 100384 | tf_op jit(solution)/shard_map/ppermute | solution.py:29
  48.1 0.1 shard_map.44.low_ref
  48.2 0.2 collective-permute-done.15.arrived_ref
  48.4 0.6 %shard_map.52.refs_0_ = bf16[3,112,1024]{2,1,0:T(8,128)(2,1)S(1)} custom-call(bf16[112,448]{1,0:T(8,128)(2,1)S(1)} %shard_map.44.low_ref, bf16[3,112,1024]{2,1,0:T(8,128)(2,1)S(1)} %collective-permute-done.15.arrived_ref, bf16[4,112,1024]{2,1,0:T(8,128)(2,1)S(1)} %get-tuple-element.48.refs_0_.refs_1_, ...), custom_call_target="tpu_custom_call" | custom-call | tf_op jit(solution)/shard_map/pallas_call | solution.py:243
  48.9 0.0 collective-permute-done.13.arrived_ref
  49.0 1.1 %shard_map.53 = bf16[4,112,1024]{2,1,0:T(8,128)(2,1)} custom-call(bf16[112,448]{1,0:T(8,128)(2,1)S(1)} %shard_map.44.low_ref, bf16[1,112,1024]{2,1,0:T(8,128)(2,1)S(1)} %collective-permute-done.13.arrived_ref, bf16[3,112,1024]{2,1,0:T(8,128)(2,1)S(1)} %shard_map.52.refs_0_, bf16[4,112,1024]{2,1,0:T(8,128)(2,1)S(1)} %get-tuple-element.48.refs_0_.refs_1_, ...), custom_call_target="tpu_custom_call" | custom-call | tf_op jit(solution)/shard_map/pallas_call | solution.py:243
  (8 shorter events, 0.3 us)
Async XLA Ops:
  0.0 27.8 %collective-permute-start.7 = (bf16[4,112,1024]{2,1,0:T(8,128)(2,1)}, bf16[4,112,1024]{2,1,0:T(8,128)(2,1)S(1)}, u32[]{:S(2)}, u32[]{:S(2)}) collective-permute-start(bf16[4,112,1024]{2,1,0:T(8,128)(2,1)} %bitcast.6), channel_id=1, source_target_pairs={{0,8},{4,12},{8,0},{12,4},{16,24},{20,28},{24,16},{28,20},{1,9},{5... | collective-permute-start | bytes 2752520 | tf_op jit(solution)/shard_map/ppermute | solution.py:29
  2.9 24.9 %collective-permute-start.8 = (bf16[4,112,1024]{2,1,0:T(8,128)(2,1)}, bf16[4,112,1024]{2,1,0:T(8,128)(2,1)S(1)}, u32[]{:S(2)}, u32[]{:S(2)}) collective-permute-start(bf16[4,112,1024]{2,1,0:T(8,128)(2,1)} %bitcast.7), channel_id=1, source_target_pairs={{0,16},{4,20},{8,24},{12,28},{16,0},{20,4},{24,8},{28,12},{1,17},{... | collective-permute-start | bytes 2752520 | tf_op jit(solution)/shard_map/ppermute | solution.py:29
  15.8 1.8 %collective-permute-start.5 = (bf16[4,56,896]{2,1,0:T(8,128)(2,1)S(1)}, bf16[4,56,896]{2,1,0:T(8,128)(2,1)S(1)}, u32[]{:S(2)}, u32[]{:S(2)}) collective-permute-start(bf16[4,56,896]{2,1,0:T(8,128)(2,1)S(1)} %get-tuple-element.39), channel_id=1, source_target_pairs={{0,4},{4,0},{8,12},{12,8},{16,20},{20,16},{24,28},{28,24},{1,5},{5... | collective-permute-start | bytes 1204232 | tf_op jit(solution)/shard_map/ppermute | solution.py:29
  15.9 2.4 %collective-permute-start = (bf16[4,56,896]{2,1,0:T(8,128)(2,1)S(1)}, bf16[4,56,896]{2,1,0:T(8,128)(2,1)S(1)}, u32[]{:S(2)}, u32[]{:S(2)}) collective-permute-start(bf16[4,56,896]{2,1,0:T(8,128)(2,1)S(1)} %get-tuple-element.29), channel_id=1, source_target_pairs={{0,4},{4,0},{8,12},{12,8},{16,20},{20,16},{24,28},{28,24},{1,5},{5... | collective-permute-start | bytes 1204232 | tf_op jit(solution)/shard_map/ppermute | solution.py:29
  17.7 10.1 %collective-permute-start.6 = (bf16[2,56,896]{2,1,0:T(8,128)(2,1)S(1)}, bf16[2,56,896]{2,1,0:T(8,128)(2,1)S(1)}, u32[]{:S(2)}, u32[]{:S(2)}) collective-permute-start(bf16[2,56,896]{2,1,0:T(8,128)(2,1)S(1)} %get-tuple-element.41), channel_id=1, source_target_pairs={{0,8},{4,12},{8,0},{12,4},{16,24},{20,28},{24,16},{28,20},{1,9},{5... | collective-permute-start | bytes 602120 | tf_op jit(solution)/shard_map/ppermute | solution.py:29
  18.4 11.3 %collective-permute-start.1 = (bf16[2,56,896]{2,1,0:T(8,128)(2,1)S(1)}, bf16[2,56,896]{2,1,0:T(8,128)(2,1)S(1)}, u32[]{:S(2)}, u32[]{:S(2)}) collective-permute-start(bf16[2,56,896]{2,1,0:T(8,128)(2,1)S(1)} %get-tuple-element.31), channel_id=1, source_target_pairs={{0,16},{4,20},{8,24},{12,28},{16,0},{20,4},{24,8},{28,12},{1,17},{... | collective-permute-start | bytes 602120 | tf_op jit(solution)/shard_map/ppermute | solution.py:29
  27.9 5.3 %collective-permute-start.9 = (bf16[1,56,896]{2,1,0:T(8,128)(2,1)S(1)}, bf16[1,56,896]{2,1,0:T(8,128)(2,1)S(1)}, u32[]{:S(2)}, u32[]{:S(2)}) collective-permute-start(bf16[1,56,896]{2,1,0:T(8,128)(2,1)S(1)} %get-tuple-element.43), channel_id=1, source_target_pairs={{0,16},{4,20},{8,24},{12,28},{16,0},{20,4},{24,8},{28,12},{1,17},{... | collective-permute-start | bytes 301064 | tf_op jit(solution)/shard_map/ppermute | solution.py:29
  29.7 5.7 %collective-permute-start.2 = (bf16[1,56,896]{2,1,0:T(8,128)(2,1)S(1)}, bf16[1,56,896]{2,1,0:T(8,128)(2,1)S(1)}, u32[]{:S(2)}, u32[]{:S(2)}) collective-permute-start(bf16[1,56,896]{2,1,0:T(8,128)(2,1)S(1)} %get-tuple-element.33), channel_id=1, source_target_pairs={{0,8},{4,12},{8,0},{12,4},{16,24},{20,28},{24,16},{28,20},{1,9},{5... | collective-permute-start | bytes 301064 | tf_op jit(solution)/shard_map/ppermute | solution.py:29
  31.3 14.2 %collective-permute-start.12 = (bf16[2,112,1024]{2,1,0:T(8,128)(2,1)S(1)}, bf16[2,112,1024]{2,1,0:T(8,128)(2,1)S(1)}, u32[]{:S(2)}, u32[]{:S(2)}) collective-permute-start(bf16[2,112,1024]{2,1,0:T(8,128)(2,1)S(1)} %slice.8), channel_id=1, source_target_pairs={{0,16},{4,20},{8,24},{12,28},{16,0},{20,4},{24,8},{28,12},{1,17},{... | collective-permute-start | bytes 1376264 | tf_op jit(solution)/shard_map/ppermute | solution.py:29
  32.0 13.6 %collective-permute-start.14 = (bf16[2,112,1024]{2,1,0:T(8,128)(2,1)S(1)}, bf16[2,112,1024]{2,1,0:T(8,128)(2,1)S(1)}, u32[]{:S(2)}, u32[]{:S(2)}) collective-permute-start(bf16[2,112,1024]{2,1,0:T(8,128)(2,1)S(1)} %slice.9), channel_id=1, source_target_pairs={{0,8},{4,12},{8,0},{12,4},{16,24},{20,28},{24,16},{28,20},{1,9},{5... | collective-permute-start | bytes 1376264 | tf_op jit(solution)/shard_map/ppermute | solution.py:29
  33.2 4.7 %collective-permute-start.10 = (bf16[1,56,896]{2,1,0:T(8,128)(2,1)S(1)}, bf16[1,56,896]{2,1,0:T(8,128)(2,1)S(1)}, u32[]{:S(2)}, u32[]{:S(2)}) collective-permute-start(bf16[1,56,896]{2,1,0:T(8,128)(2,1)S(1)} %get-tuple-element.45), channel_id=1, source_target_pairs={{0,1},{1,0},{2,3},{3,2},{4,5},{5,4},{6,7},{7,6},{8,9},{9,8},{10,11... | collective-permute-start | bytes 301064 | tf_op jit(solution)/shard_map/ppermute | solution.py:29
  35.5 5.9 %collective-permute-start.3 = (bf16[1,56,896]{2,1,0:T(8,128)(2,1)S(1)}, bf16[1,56,896]{2,1,0:T(8,128)(2,1)S(1)}, u32[]{:S(2)}, u32[]{:S(2)}) collective-permute-start(bf16[1,56,896]{2,1,0:T(8,128)(2,1)S(1)} %get-tuple-element.35.refs_0_), channel_id=1, source_target_pairs={{0,1},{1,0},{2,3},{3,2},{4,5},{5,4},{6,7},{7,6},{8,9},{9,8},{10,11... | collective-permute-start | bytes 301064 | tf_op jit(solution)/shard_map/ppermute | solution.py:29
  37.9 7.6 %collective-permute-start.11 = (bf16[1,56,896]{2,1,0:T(8,128)(2,1)S(1)}, bf16[1,56,896]{2,1,0:T(8,128)(2,1)S(1)}, u32[]{:S(2)}, u32[]{:S(2)}) collective-permute-start(bf16[1,56,896]{2,1,0:T(8,128)(2,1)S(1)} %get-tuple-element.47), channel_id=1, source_target_pairs={{0,2},{1,3},{2,0},{3,1},{4,6},{5,7},{6,4},{7,5},{8,10},{9,11},{10,... | collective-permute-start | bytes 301064 | tf_op jit(solution)/shard_map/ppermute | solution.py:29
  41.4 6.7 %collective-permute-start.4 = (bf16[1,56,896]{2,1,0:T(8,128)(2,1)S(1)}, bf16[1,56,896]{2,1,0:T(8,128)(2,1)S(1)}, u32[]{:S(2)}, u32[]{:S(2)}) collective-permute-start(bf16[1,56,896]{2,1,0:T(8,128)(2,1)S(1)} %get-tuple-element.37.refs_0_), channel_id=1, source_target_pairs={{0,2},{1,3},{2,0},{3,1},{4,6},{5,7},{6,4},{7,5},{8,10},{9,11},{10,... | collective-permute-start | bytes 301064 | tf_op jit(solution)/shard_map/ppermute | solution.py:29
  46.2 2.2 %collective-permute-start.15 = (bf16[3,112,1024]{2,1,0:T(8,128)(2,1)S(1)}, bf16[3,112,1024]{2,1,0:T(8,128)(2,1)S(1)}, u32[]{:S(2)}, u32[]{:S(2)}) collective-permute-start(bf16[3,112,1024]{2,1,0:T(8,128)(2,1)S(1)} %shard_map.51), channel_id=1, source_target_pairs={{0,4},{4,0},{8,12},{12,8},{16,20},{20,16},{24,28},{28,24},{1,5},{5... | collective-permute-start | bytes 2064392 | tf_op jit(solution)/shard_map/ppermute | solution.py:29
  46.5 2.4 %collective-permute-start.13 = (bf16[1,112,1024]{2,1,0:T(8,128)(2,1)S(1)}, bf16[1,112,1024]{2,1,0:T(8,128)(2,1)S(1)}, u32[]{:S(2)}, u32[]{:S(2)}) collective-permute-start(bf16[1,112,1024]{2,1,0:T(8,128)(2,1)S(1)} %shard_map.50), channel_id=1, source_target_pairs={{0,4},{4,0},{8,12},{12,8},{16,20},{20,16},{24,28},{28,24},{1,5},{5... | collective-permute-start | bytes 688136 | tf_op jit(solution)/shard_map/ppermute | solution.py:29

commit v8 on v6

--- a/solution.py
+++ b/solution.py
@@ -21,7 +21,7 @@
 
 
 PLANE_FILL = (filler(5), filler(1))
-GROUP_FILL = (filler(1), filler(1))
+GROUP_FILL = (filler(0.5), filler(1))
 LAST_FILL = filler(10)
 
 

time: 50.6 us -> 50.6 us (level)
  no operation moved by 1% of the time
where the time goes in v8:
time: 50.6 us; the launch traced here: 49.9 us
  starting transfers between devices  20.6 us (41%)
  Pallas kernels  15.4 us (30%)
  waiting for transfers between devices  13.5 us (27%)
    ppermute x16, starting transfers between devices, swap(): return lax.ppermute(array, axis, [(i, i ^ offset) for i in range(size)])  20.6 us
    ppermute x16, waiting for transfers between devices, swap(): return lax.ppermute(array, axis, [(i, i ^ offset) for i in range(size)])  13.5 us
    pallas_call x1, Pallas kernels, pair_product(): pl.pallas_call(functools.partial(pair_kernel, chunks), out_shape=[pltpu.V...  10.8 us
    pallas_call x2, Pallas kernels, own_density(): pl.pallas_call(functools.partial(kernel, places), out_shape=out, in_specs...  1.63 us
    pallas_call x2, Pallas kernels, cut(): pl.pallas_call(functools.partial(cut_kernel, rows, parity), out_shape=[pl...  1.48 us
  transfers between devices with their start and end apart: 16, of which 7 were waited for; matrix products, arithmetic and copies ran while one was open for 0% of the time, Pallas kernels for 28%

profile of v8, /device:TPU:0, one launch (start us, length us, event | category | flops | bytes accessed | tf_op | source)
XLA Modules:
  0.0 49.9 jit_solution(6059099115928949566)
XLA Ops:
  0.0 2.9 %collective-permute-start.7 = (bf16[4,112,1024]{2,1,0:T(8,128)(2,1)}, bf16[4,112,1024]{2,1,0:T(8,128)(2,1)S(1)}, u32[]{:S(2)}, u32[]{:S(2)}) collective-permute-start(bf16[4,112,1024]{2,1,0:T(8,128)(2,1)} %bitcast.6), channel_id=1, source_target_pairs={{0,8},{4,12},{8,0},{12,4},{16,24},{20,28},{24,16},{28,20},{1,9},{5... | collective-permute-start | bytes 2752520 | tf_op jit(solution)/shard_map/ppermute | solution.py:29
  2.9 1.5 %collective-permute-start.8 = (bf16[4,112,1024]{2,1,0:T(8,128)(2,1)}, bf16[4,112,1024]{2,1,0:T(8,128)(2,1)S(1)}, u32[]{:S(2)}, u32[]{:S(2)}) collective-permute-start(bf16[4,112,1024]{2,1,0:T(8,128)(2,1)} %bitcast.7), channel_id=1, source_target_pairs={{0,16},{4,20},{8,24},{12,28},{16,0},{20,4},{24,8},{28,12},{1,17},{... | collective-permute-start | bytes 2752520 | tf_op jit(solution)/shard_map/ppermute | solution.py:29
  4.5 10.8 %shard_map.37 = (f32[896,896]{1,0:T(8,128)S(1)}, bf16[4,112,1024]{2,1,0:T(8,128)(2,1)S(1)}) custom-call(bf16[4480,896]{1,0:T(8,128)(2,1)} %bitcast.4, bf16[4480,896]{1,0:T(8,128)(2,1)} %bitcast.5, bf16[4,112,1024]{2,1,0:T(8,128)(2,1)} %bitcast.8), custom_call_target="tpu_custom_call" | custom-call | flops 7193231360 | bytes 16056320 | tf_op jit(solution)/shard_map/pallas_call | solution.py:78
  15.3 0.5 shard_map.39
  15.8 0.1 collective-permute-start.5
  15.9 0.5 collective-permute-start
  16.4 1.0 %shard_map.38 = (f32[4,56,896]{2,1,0:T(8,128)S(1)}, f32[4,56,896]{2,1,0:T(8,128)S(1)}) custom-call(f32[896,896]{1,0:T(8,128)S(1)} %get-tuple-element.27.total), custom_call_target="tpu_custom_call" | custom-call | tf_op jit(solution)/shard_map/pallas_call | solution.py:119
  17.4 0.2 collective-permute-done.5.other
  17.6 0.1 shard_map.45
  17.7 0.6 %collective-permute-start.6 = (bf16[2,56,896]{2,1,0:T(8,128)(2,1)S(1)}, bf16[2,56,896]{2,1,0:T(8,128)(2,1)S(1)}, u32[]{:S(2)}, u32[]{:S(2)}) collective-permute-start(bf16[2,56,896]{2,1,0:T(8,128)(2,1)S(1)} %get-tuple-element.41), channel_id=1, source_target_pairs={{0,8},{4,12},{8,0},{12,4},{16,24},{20,28},{24,16},{28,20},{1,9},{5... | collective-permute-start | bytes 602120 | tf_op jit(solution)/shard_map/ppermute | solution.py:29
  18.3 0.0 collective-permute-done.other
  18.3 0.1 shard_map.40
  18.4 0.5 collective-permute-start.1
  18.8 9.0 %collective-permute-done.6.other = bf16[2,56,896]{2,1,0:T(8,128)(2,1)S(1)} collective-permute-done((bf16[2,56,896]{2,1,0:T(8,128)(2,1)S(1)}, bf16[2,56,896]{2,1,0:T(8,128)(2,1)S(1)}, u32[]{:S(2)}, u32[]{:S(2)}) %collective-permute-start.6) | collective-permute-done | bytes 200736 | tf_op jit(solution)/shard_map/ppermute | solution.py:29
  27.8 0.0 collective-permute-done.7.refs_0_.refs_1_
  27.8 0.0 collective-permute-done.8.refs_1_.refs_2_
  27.9 1.8 %collective-permute-start.9 = (bf16[1,56,896]{2,1,0:T(8,128)(2,1)S(1)}, bf16[1,56,896]{2,1,0:T(8,128)(2,1)S(1)}, u32[]{:S(2)}, u32[]{:S(2)}) collective-permute-start(bf16[1,56,896]{2,1,0:T(8,128)(2,1)S(1)} %get-tuple-element.43), channel_id=1, source_target_pairs={{0,16},{4,20},{8,24},{12,28},{16,0},{20,4},{24,8},{28,12},{1,17},{... | collective-permute-start | bytes 301064 | tf_op jit(solution)/shard_map/ppermute | solution.py:29
  29.7 0.0 collective-permute-done.1.other
  29.7 1.6 %collective-permute-start.2 = (bf16[1,56,896]{2,1,0:T(8,128)(2,1)S(1)}, bf16[1,56,896]{2,1,0:T(8,128)(2,1)S(1)}, u32[]{:S(2)}, u32[]{:S(2)}) collective-permute-start(bf16[1,56,896]{2,1,0:T(8,128)(2,1)S(1)} %get-tuple-element.33), channel_id=1, source_target_pairs={{0,8},{4,12},{8,0},{12,4},{16,24},{20,28},{24,16},{28,20},{1,9},{5... | collective-permute-start | bytes 301064 | tf_op jit(solution)/shard_map/ppermute | solution.py:29
  31.3 0.6 %collective-permute-start.14 = (bf16[2,112,1024]{2,1,0:T(8,128)(2,1)S(1)}, bf16[2,112,1024]{2,1,0:T(8,128)(2,1)S(1)}, u32[]{:S(2)}, u32[]{:S(2)}) collective-permute-start(bf16[2,112,1024]{2,1,0:T(8,128)(2,1)S(1)} %slice.9), channel_id=1, source_target_pairs={{0,8},{4,12},{8,0},{12,4},{16,24},{20,28},{24,16},{28,20},{1,9},{5... | collective-permute-start | bytes 1376264 | tf_op jit(solution)/shard_map/ppermute | solution.py:29
  32.0 1.2 %collective-permute-start.12 = (bf16[2,112,1024]{2,1,0:T(8,128)(2,1)S(1)}, bf16[2,112,1024]{2,1,0:T(8,128)(2,1)S(1)}, u32[]{:S(2)}, u32[]{:S(2)}) collective-permute-start(bf16[2,112,1024]{2,1,0:T(8,128)(2,1)S(1)} %slice.8), channel_id=1, source_target_pairs={{0,16},{4,20},{8,24},{12,28},{16,0},{20,4},{24,8},{28,12},{1,17},{... | collective-permute-start | bytes 1376264 | tf_op jit(solution)/shard_map/ppermute | solution.py:29
  33.1 0.0 collective-permute-done.9.other
  33.1 1.6 %collective-permute-start.10 = (bf16[1,56,896]{2,1,0:T(8,128)(2,1)S(1)}, bf16[1,56,896]{2,1,0:T(8,128)(2,1)S(1)}, u32[]{:S(2)}, u32[]{:S(2)}) collective-permute-start(bf16[1,56,896]{2,1,0:T(8,128)(2,1)S(1)} %get-tuple-element.45), channel_id=1, source_target_pairs={{0,1},{1,0},{2,3},{3,2},{4,5},{5,4},{6,7},{7,6},{8,9},{9,8},{10,11... | collective-permute-start | bytes 301064 | tf_op jit(solution)/shard_map/ppermute | solution.py:29
  34.8 0.7 %collective-permute-done.2.other = bf16[1,56,896]{2,1,0:T(8,128)(2,1)S(1)} collective-permute-done((bf16[1,56,896]{2,1,0:T(8,128)(2,1)S(1)}, bf16[1,56,896]{2,1,0:T(8,128)(2,1)S(1)}, u32[]{:S(2)}, u32[]{:S(2)}) %collective-permute-start.2) | collective-permute-done | bytes 100384 | tf_op jit(solution)/shard_map/ppermute | solution.py:29
  35.5 1.6 %collective-permute-start.3 = (bf16[1,56,896]{2,1,0:T(8,128)(2,1)S(1)}, bf16[1,56,896]{2,1,0:T(8,128)(2,1)S(1)}, u32[]{:S(2)}, u32[]{:S(2)}) collective-permute-start(bf16[1,56,896]{2,1,0:T(8,128)(2,1)S(1)} %get-tuple-element.35.refs_0_), channel_id=1, source_target_pairs={{0,1},{1,0},{2,3},{3,2},{4,5},{5,4},{6,7},{7,6},{8,9},{9,8},{10,11... | collective-permute-start | bytes 301064 | tf_op jit(solution)/shard_map/ppermute | solution.py:29
  37.2 0.7 %collective-permute-done.10.other = bf16[1,56,896]{2,1,0:T(8,128)(2,1)S(1)} collective-permute-done((bf16[1,56,896]{2,1,0:T(8,128)(2,1)S(1)}, bf16[1,56,896]{2,1,0:T(8,128)(2,1)S(1)}, u32[]{:S(2)}, u32[]{:S(2)}) %collective-permute-start.10) | collective-permute-done | bytes 100384 | tf_op jit(solution)/shard_map/ppermute | solution.py:29
  37.9 3.2 %collective-permute-start.11 = (bf16[1,56,896]{2,1,0:T(8,128)(2,1)S(1)}, bf16[1,56,896]{2,1,0:T(8,128)(2,1)S(1)}, u32[]{:S(2)}, u32[]{:S(2)}) collective-permute-start(bf16[1,56,896]{2,1,0:T(8,128)(2,1)S(1)} %get-tuple-element.47), channel_id=1, source_target_pairs={{0,2},{1,3},{2,0},{3,1},{4,6},{5,7},{6,4},{7,5},{8,10},{9,11},{10,... | collective-permute-start | bytes 301064 | tf_op jit(solution)/shard_map/ppermute | solution.py:29
  41.1 0.0 collective-permute-done.3.other
  41.1 2.3 %collective-permute-start.4 = (bf16[1,56,896]{2,1,0:T(8,128)(2,1)S(1)}, bf16[1,56,896]{2,1,0:T(8,128)(2,1)S(1)}, u32[]{:S(2)}, u32[]{:S(2)}) collective-permute-start(bf16[1,56,896]{2,1,0:T(8,128)(2,1)S(1)} %get-tuple-element.37.refs_0_), channel_id=1, source_target_pairs={{0,2},{1,3},{2,0},{3,1},{4,6},{5,7},{6,4},{7,5},{8,10},{9,11},{10,... | collective-permute-start | bytes 301064 | tf_op jit(solution)/shard_map/ppermute | solution.py:29
  43.4 2.0 %collective-permute-done.11.part_ref = bf16[1,56,896]{2,1,0:T(8,128)(2,1)S(1)} collective-permute-done((bf16[1,56,896]{2,1,0:T(8,128)(2,1)S(1)}, bf16[1,56,896]{2,1,0:T(8,128)(2,1)S(1)}, u32[]{:S(2)}, u32[]{:S(2)}) %collective-permute-start.11) | collective-permute-done | bytes 100384 | tf_op jit(solution)/shard_map/ppermute | solution.py:29
  45.4 0.1 shard_map.49.low_ref
  45.5 0.0 collective-permute-done.14.refs_3_
  45.5 0.4 shard_map.51
  46.0 0.1 collective-permute-start.15
  46.0 0.0 collective-permute-done.12.refs_3_
  46.1 0.4 shard_map.50
  46.5 0.6 %collective-permute-start.13 = (bf16[2,112,1024]{2,1,0:T(8,128)(2,1)S(1)}, bf16[2,112,1024]{2,1,0:T(8,128)(2,1)S(1)}, u32[]{:S(2)}, u32[]{:S(2)}) collective-permute-start(bf16[2,112,1024]{2,1,0:T(8,128)(2,1)S(1)} %shard_map.50), channel_id=1, source_target_pairs={{0,4},{4,0},{8,12},{12,8},{16,20},{20,16},{24,28},{28,24},{1,5},{5... | collective-permute-start | bytes 1376264 | tf_op jit(solution)/shard_map/ppermute | solution.py:29
  47.1 0.0 collective-permute-done.4.part_ref
  47.1 0.1 shard_map.44.low_ref
  47.2 0.7 %collective-permute-done.15.arrived_ref = bf16[2,112,1024]{2,1,0:T(8,128)(2,1)S(1)} collective-permute-done((bf16[2,112,1024]{2,1,0:T(8,128)(2,1)S(1)}, bf16[2,112,1024]{2,1,0:T(8,128)(2,1)S(1)}, u32[]{:S(2)}, u32[]{:S(2)}) %collective-permute-start.15) | collective-permute-done | bytes 458784 | tf_op jit(solution)/shard_map/ppermute | solution.py:29
  47.9 0.4 shard_map.52.head_ref
  48.3 0.2 collective-permute-done.13.arrived_ref
  48.5 1.2 %shard_map.53 = bf16[4,112,1024]{2,1,0:T(8,128)(2,1)} custom-call(bf16[112,448]{1,0:T(8,128)(2,1)S(1)} %shard_map.44.low_ref, bf16[2,112,1024]{2,1,0:T(8,128)(2,1)S(1)} %collective-permute-done.13.arrived_ref, bf16[2,112,1024]{2,1,0:T(8,128)(2,1)S(1)} %shard_map.52.head_ref, bf16[4,112,1024]{2,1,0:T(8,128)(2,1)S(1)} %get-tuple-element.48.refs_0_, ...), custom_call_target="tpu_custom_call" | custom-call | tf_op jit(solution)/shard_map/pallas_call | solution.py:238
  (8 shorter events, 0.3 us)
Async XLA Ops:
  0.0 27.8 %collective-permute-start.7 = (bf16[4,112,1024]{2,1,0:T(8,128)(2,1)}, bf16[4,112,1024]{2,1,0:T(8,128)(2,1)S(1)}, u32[]{:S(2)}, u32[]{:S(2)}) collective-permute-start(bf16[4,112,1024]{2,1,0:T(8,128)(2,1)} %bitcast.6), channel_id=1, source_target_pairs={{0,8},{4,12},{8,0},{12,4},{16,24},{20,28},{24,16},{28,20},{1,9},{5... | collective-permute-start | bytes 2752520 | tf_op jit(solution)/shard_map/ppermute | solution.py:29
  2.9 24.9 %collective-permute-start.8 = (bf16[4,112,1024]{2,1,0:T(8,128)(2,1)}, bf16[4,112,1024]{2,1,0:T(8,128)(2,1)S(1)}, u32[]{:S(2)}, u32[]{:S(2)}) collective-permute-start(bf16[4,112,1024]{2,1,0:T(8,128)(2,1)} %bitcast.7), channel_id=1, source_target_pairs={{0,16},{4,20},{8,24},{12,28},{16,0},{20,4},{24,8},{28,12},{1,17},{... | collective-permute-start | bytes 2752520 | tf_op jit(solution)/shard_map/ppermute | solution.py:29
  15.8 1.8 %collective-permute-start.5 = (bf16[4,56,896]{2,1,0:T(8,128)(2,1)S(1)}, bf16[4,56,896]{2,1,0:T(8,128)(2,1)S(1)}, u32[]{:S(2)}, u32[]{:S(2)}) collective-permute-start(bf16[4,56,896]{2,1,0:T(8,128)(2,1)S(1)} %get-tuple-element.39), channel_id=1, source_target_pairs={{0,4},{4,0},{8,12},{12,8},{16,20},{20,16},{24,28},{28,24},{1,5},{5... | collective-permute-start | bytes 1204232 | tf_op jit(solution)/shard_map/ppermute | solution.py:29
  15.9 2.4 %collective-permute-start = (bf16[4,56,896]{2,1,0:T(8,128)(2,1)S(1)}, bf16[4,56,896]{2,1,0:T(8,128)(2,1)S(1)}, u32[]{:S(2)}, u32[]{:S(2)}) collective-permute-start(bf16[4,56,896]{2,1,0:T(8,128)(2,1)S(1)} %get-tuple-element.29), channel_id=1, source_target_pairs={{0,4},{4,0},{8,12},{12,8},{16,20},{20,16},{24,28},{28,24},{1,5},{5... | collective-permute-start | bytes 1204232 | tf_op jit(solution)/shard_map/ppermute | solution.py:29
  17.7 10.1 %collective-permute-start.6 = (bf16[2,56,896]{2,1,0:T(8,128)(2,1)S(1)}, bf16[2,56,896]{2,1,0:T(8,128)(2,1)S(1)}, u32[]{:S(2)}, u32[]{:S(2)}) collective-permute-start(bf16[2,56,896]{2,1,0:T(8,128)(2,1)S(1)} %get-tuple-element.41), channel_id=1, source_target_pairs={{0,8},{4,12},{8,0},{12,4},{16,24},{20,28},{24,16},{28,20},{1,9},{5... | collective-permute-start | bytes 602120 | tf_op jit(solution)/shard_map/ppermute | solution.py:29
  18.4 11.3 %collective-permute-start.1 = (bf16[2,56,896]{2,1,0:T(8,128)(2,1)S(1)}, bf16[2,56,896]{2,1,0:T(8,128)(2,1)S(1)}, u32[]{:S(2)}, u32[]{:S(2)}) collective-permute-start(bf16[2,56,896]{2,1,0:T(8,128)(2,1)S(1)} %get-tuple-element.31), channel_id=1, source_target_pairs={{0,16},{4,20},{8,24},{12,28},{16,0},{20,4},{24,8},{28,12},{1,17},{... | collective-permute-start | bytes 602120 | tf_op jit(solution)/shard_map/ppermute | solution.py:29
  27.9 5.3 %collective-permute-start.9 = (bf16[1,56,896]{2,1,0:T(8,128)(2,1)S(1)}, bf16[1,56,896]{2,1,0:T(8,128)(2,1)S(1)}, u32[]{:S(2)}, u32[]{:S(2)}) collective-permute-start(bf16[1,56,896]{2,1,0:T(8,128)(2,1)S(1)} %get-tuple-element.43), channel_id=1, source_target_pairs={{0,16},{4,20},{8,24},{12,28},{16,0},{20,4},{24,8},{28,12},{1,17},{... | collective-permute-start | bytes 301064 | tf_op jit(solution)/shard_map/ppermute | solution.py:29
  29.7 5.8 %collective-permute-start.2 = (bf16[1,56,896]{2,1,0:T(8,128)(2,1)S(1)}, bf16[1,56,896]{2,1,0:T(8,128)(2,1)S(1)}, u32[]{:S(2)}, u32[]{:S(2)}) collective-permute-start(bf16[1,56,896]{2,1,0:T(8,128)(2,1)S(1)} %get-tuple-element.33), channel_id=1, source_target_pairs={{0,8},{4,12},{8,0},{12,4},{16,24},{20,28},{24,16},{28,20},{1,9},{5... | collective-permute-start | bytes 301064 | tf_op jit(solution)/shard_map/ppermute | solution.py:29
  31.3 14.2 %collective-permute-start.14 = (bf16[2,112,1024]{2,1,0:T(8,128)(2,1)S(1)}, bf16[2,112,1024]{2,1,0:T(8,128)(2,1)S(1)}, u32[]{:S(2)}, u32[]{:S(2)}) collective-permute-start(bf16[2,112,1024]{2,1,0:T(8,128)(2,1)S(1)} %slice.9), channel_id=1, source_target_pairs={{0,8},{4,12},{8,0},{12,4},{16,24},{20,28},{24,16},{28,20},{1,9},{5... | collective-permute-start | bytes 1376264 | tf_op jit(solution)/shard_map/ppermute | solution.py:29
  32.0 14.1 %collective-permute-start.12 = (bf16[2,112,1024]{2,1,0:T(8,128)(2,1)S(1)}, bf16[2,112,1024]{2,1,0:T(8,128)(2,1)S(1)}, u32[]{:S(2)}, u32[]{:S(2)}) collective-permute-start(bf16[2,112,1024]{2,1,0:T(8,128)(2,1)S(1)} %slice.8), channel_id=1, source_target_pairs={{0,16},{4,20},{8,24},{12,28},{16,0},{20,4},{24,8},{28,12},{1,17},{... | collective-permute-start | bytes 1376264 | tf_op jit(solution)/shard_map/ppermute | solution.py:29
  33.1 4.7 %collective-permute-start.10 = (bf16[1,56,896]{2,1,0:T(8,128)(2,1)S(1)}, bf16[1,56,896]{2,1,0:T(8,128)(2,1)S(1)}, u32[]{:S(2)}, u32[]{:S(2)}) collective-permute-start(bf16[1,56,896]{2,1,0:T(8,128)(2,1)S(1)} %get-tuple-element.45), channel_id=1, source_target_pairs={{0,1},{1,0},{2,3},{3,2},{4,5},{5,4},{6,7},{7,6},{8,9},{9,8},{10,11... | collective-permute-start | bytes 301064 | tf_op jit(solution)/shard_map/ppermute | solution.py:29
  35.5 5.5 %collective-permute-start.3 = (bf16[1,56,896]{2,1,0:T(8,128)(2,1)S(1)}, bf16[1,56,896]{2,1,0:T(8,128)(2,1)S(1)}, u32[]{:S(2)}, u32[]{:S(2)}) collective-permute-start(bf16[1,56,896]{2,1,0:T(8,128)(2,1)S(1)} %get-tuple-element.35.refs_0_), channel_id=1, source_target_pairs={{0,1},{1,0},{2,3},{3,2},{4,5},{5,4},{6,7},{7,6},{8,9},{9,8},{10,11... | collective-permute-start | bytes 301064 | tf_op jit(solution)/shard_map/ppermute | solution.py:29
  37.9 7.5 %collective-permute-start.11 = (bf16[1,56,896]{2,1,0:T(8,128)(2,1)S(1)}, bf16[1,56,896]{2,1,0:T(8,128)(2,1)S(1)}, u32[]{:S(2)}, u32[]{:S(2)}) collective-permute-start(bf16[1,56,896]{2,1,0:T(8,128)(2,1)S(1)} %get-tuple-element.47), channel_id=1, source_target_pairs={{0,2},{1,3},{2,0},{3,1},{4,6},{5,7},{6,4},{7,5},{8,10},{9,11},{10,... | collective-permute-start | bytes 301064 | tf_op jit(solution)/shard_map/ppermute | solution.py:29
  41.1 6.0 %collective-permute-start.4 = (bf16[1,56,896]{2,1,0:T(8,128)(2,1)S(1)}, bf16[1,56,896]{2,1,0:T(8,128)(2,1)S(1)}, u32[]{:S(2)}, u32[]{:S(2)}) collective-permute-start(bf16[1,56,896]{2,1,0:T(8,128)(2,1)S(1)} %get-tuple-element.37.refs_0_), channel_id=1, source_target_pairs={{0,2},{1,3},{2,0},{3,1},{4,6},{5,7},{6,4},{7,5},{8,10},{9,11},{10,... | collective-permute-start | bytes 301064 | tf_op jit(solution)/shard_map/ppermute | solution.py:29
  46.0 1.9 %collective-permute-start.15 = (bf16[2,112,1024]{2,1,0:T(8,128)(2,1)S(1)}, bf16[2,112,1024]{2,1,0:T(8,128)(2,1)S(1)}, u32[]{:S(2)}, u32[]{:S(2)}) collective-permute-start(bf16[2,112,1024]{2,1,0:T(8,128)(2,1)S(1)} %shard_map.51), channel_id=1, source_target_pairs={{0,4},{4,0},{8,12},{12,8},{16,20},{20,16},{24,28},{28,24},{1,5},{5... | collective-permute-start | bytes 1376264 | tf_op jit(solution)/shard_map/ppermute | solution.py:29
  46.5 2.0 %collective-permute-start.13 = (bf16[2,112,1024]{2,1,0:T(8,128)(2,1)S(1)}, bf16[2,112,1024]{2,1,0:T(8,128)(2,1)S(1)}, u32[]{:S(2)}, u32[]{:S(2)}) collective-permute-start(bf16[2,112,1024]{2,1,0:T(8,128)(2,1)S(1)} %shard_map.50), channel_id=1, source_target_pairs={{0,4},{4,0},{8,12},{12,8},{16,20},{20,16},{24,28},{28,24},{1,5},{5... | collective-permute-start | bytes 1376264 | tf_op jit(solution)/shard_map/ppermute | solution.py:29
